TPU v7x, 128 devices: a whole 4x4x4 slice. The times are simulated.
128 devices in a mesh: ctx: 32 (over z, y, x_hi), head: 4 (over x_lo, core).
Axes of the slice: x: 4 (x_hi: 2, x_lo: 2; x = x_hi * 2 + x_lo), y: 4, z: 4, core: 2. Of those that a mesh axis runs over, the one named last changes fastest.
Arguments:
- q_proj: bfloat16 [8192, 3072], P('ctx', 'head'), may hold values from -6 to 6
- k_proj: bfloat16 [8192, 3072], P('ctx', 'head'), may hold values from -6 to 6
- v_proj: bfloat16 [8192, 3072], P('ctx', 'head'), may hold values from -6 to 6
- out_weight: bfloat16 [3072, 6144], P('head'), may hold values from -1.5 to 1.5
- out_grad: bfloat16 [8192, 6144], P('ctx', 'head'), may hold values from -1.1953125 to 1.1953125
Outputs:
- mixed_out: bfloat16 [8192, 6144], P('ctx', 'head')
- q_grad: bfloat16 [8192, 3072], P('ctx', 'head')
- k_grad: bfloat16 [8192, 3072], P('ctx', 'head')
- v_grad: bfloat16 [8192, 3072], P('ctx', 'head')
All inputs are finite; a program needn't handle non-finite values.
Results may differ from a plain program's by a relative error of at most 0.014.
The roundings to bfloat16 on the way count: a program that leaves them out, or rounds other values in their place, can miss the bound.
Values may be sent and summed in bfloat16 or wider, within the bound.
No kernel may reach another device: no remote copies, remote signals or barrier semaphores. Data moves between devices by JAX's collectives and lax.ppermute only.
A program may use at most 192 MiB of HBM per device.

v0:
```python
import math

import jax
import jax.numpy as jnp
from jax import lax
from jax.sharding import PartitionSpec as P

HEAD_DIM = 128
SHORT = 4
WINDOW = 1024


def from_behind(shard, axis, by):
    length = lax.axis_size(axis)
    pairs = [(i, i + by) for i in range(length) if 0 <= i + by < length]
    return lax.ppermute(shard, axis, pairs)


def log_totals(scores):
    row_max = jnp.max(scores, -1, keepdims=True)
    return row_max + jnp.log(jnp.sum(jnp.exp(scores - row_max), -1, keepdims=True))


def window_allowed(row_count, offset, present):
    query_pos = jnp.arange(row_count, dtype=jnp.int32)[:, None]
    key_pos = jnp.arange(row_count, dtype=jnp.int32)[None, :] - offset * row_count
    return (key_pos > query_pos - WINDOW) & (key_pos <= query_pos) & present


def shards(q_proj, k_proj, v_proj, out_weight, out_grad):
    row_count, col_count = q_proj.shape
    head_count = col_count // HEAD_DIM
    reach = WINDOW // row_count
    short_rows = row_count // SHORT
    ctx_index = lax.axis_index("ctx")
    score_scale = 1.0 / math.sqrt(HEAD_DIM)
    coarse_scale = 2.0 * score_scale

    def heads_of(matrix):
        return matrix.reshape(matrix.shape[0], head_count, HEAD_DIM)

    query_heads = heads_of(q_proj)
    key_heads = heads_of(k_proj)
    value_heads = heads_of(v_proj)
    key_tiles = [key_heads]
    value_tiles = [value_heads]
    allowed_tiles = [window_allowed(row_count, 0, ctx_index >= 0)]
    for offset in range(1, reach + 1):
        moved = from_behind(jnp.stack((k_proj, v_proj)), "ctx", offset)
        key_tiles.append(heads_of(moved[0]))
        value_tiles.append(heads_of(moved[1]))
        allowed_tiles.append(window_allowed(row_count, offset, ctx_index >= offset))
    key_window = jnp.concatenate(key_tiles, 0)
    value_window = jnp.concatenate(value_tiles, 0)
    allowed = jnp.concatenate(allowed_tiles, 1)
    fine_scores = (
        jnp.einsum("thd,shd->hts", query_heads, key_window, preferred_element_type=jnp.float32)
        * score_scale
    )
    fine_scores = jnp.where(allowed[None], fine_scores, -jnp.inf)
    fine_log = log_totals(fine_scores)
    fine_probs = jnp.exp(fine_scores - fine_log)
    fine_weights = fine_probs.astype(jnp.bfloat16)
    fine_out = jnp.einsum(
        "hts,shd->thd", fine_weights, value_window, preferred_element_type=jnp.float32
    )
    packed = jnp.concatenate((q_proj, k_proj, v_proj), 1)
    carried = from_behind(packed[row_count - (SHORT - 1) :], "ctx", 1)
    extended = jnp.concatenate((carried, packed), 0)[:row_count].astype(jnp.float32)
    pooled = (extended.reshape(short_rows, SHORT, 3 * col_count).sum(1) / SHORT).astype(
        jnp.bfloat16
    )
    pooled_query = pooled[:, :col_count]
    pooled_qh = heads_of(pooled_query)
    gathered = lax.all_gather(
        jnp.stack((pooled[:, col_count : 2 * col_count], pooled[:, 2 * col_count :])),
        "ctx",
        axis=1,
        tiled=True,
    )
    all_keys = heads_of(gathered[0])
    all_values = heads_of(gathered[1])
    total_rows = all_keys.shape[0]
    coarse_query_pos = ctx_index * short_rows + jnp.arange(short_rows, dtype=jnp.int32)[:, None]
    coarse_key_pos = jnp.arange(total_rows, dtype=jnp.int32)[None, :]
    coarse_allowed = coarse_key_pos <= coarse_query_pos
    coarse_scores = (
        jnp.einsum("jhd,ihd->hji", pooled_qh, all_keys, preferred_element_type=jnp.float32)
        * coarse_scale
    )
    coarse_scores = jnp.where(coarse_allowed[None], coarse_scores, -jnp.inf)
    coarse_log = log_totals(coarse_scores)
    coarse_probs = jnp.exp(coarse_scores - coarse_log)
    coarse_weights = coarse_probs.astype(jnp.bfloat16)
    coarse_out = jnp.einsum(
        "hji,ihd->jhd", coarse_weights, all_values, preferred_element_type=jnp.float32
    )
    attn = (
        fine_out.reshape(row_count, col_count)
        + jnp.repeat(coarse_out.reshape(short_rows, col_count), SHORT, axis=0)
    ).astype(jnp.bfloat16)
    partial_value = jnp.dot(attn, out_weight, preferred_element_type=jnp.float32)
    mixed_out = lax.psum_scatter(
        partial_value.astype(jnp.bfloat16), "head", scatter_dimension=1, tiled=True
    )
    grad_attn = lax.dot_general(
        lax.all_gather(out_grad, "head", axis=1, tiled=True),
        out_weight,
        (((1,), (1,)), ((), ())),
        preferred_element_type=jnp.float32,
    ).astype(jnp.bfloat16)
    grad_heads = heads_of(grad_attn)
    fine_delta = jnp.sum(grad_heads.astype(jnp.float32) * fine_out, -1).T[:, :, None]
    fine_gprob = jnp.einsum(
        "thd,shd->hts", grad_heads, value_window, preferred_element_type=jnp.float32
    )
    fine_dscore = (fine_probs * (fine_gprob - fine_delta)).astype(jnp.bfloat16)
    grad_q_fine = (
        jnp.einsum("hts,shd->thd", fine_dscore, key_window, preferred_element_type=jnp.float32)
        * score_scale
    )
    key_terms = (
        jnp.einsum("hts,thd->shd", fine_dscore, query_heads, preferred_element_type=jnp.float32)
        * score_scale
    )
    value_terms = jnp.einsum(
        "hts,thd->shd", fine_weights, grad_heads, preferred_element_type=jnp.float32
    )
    grad_k_fine = key_terms[:row_count]
    grad_v_fine = value_terms[:row_count]
    for offset in range(1, reach + 1):
        lower = offset * row_count
        returned = from_behind(
            jnp.stack(
                (key_terms[lower : lower + row_count], value_terms[lower : lower + row_count])
            ).astype(jnp.bfloat16),
            "ctx",
            -offset,
        ).astype(jnp.float32)
        grad_k_fine = grad_k_fine + returned[0]
        grad_v_fine = grad_v_fine + returned[1]
    grad_pooled = (
        grad_attn.astype(jnp.float32)
        .reshape(short_rows, SHORT, col_count)
        .sum(1)
        .astype(jnp.bfloat16)
    )
    pooled_grad_heads = heads_of(grad_pooled)
    coarse_delta = jnp.sum(pooled_grad_heads.astype(jnp.float32) * coarse_out, -1).T[:, :, None]
    coarse_gprob = jnp.einsum(
        "jhd,ihd->hji", pooled_grad_heads, all_values, preferred_element_type=jnp.float32
    )
    coarse_dscore = (coarse_probs * (coarse_gprob - coarse_delta)).astype(jnp.bfloat16)
    grad_q_coarse = (
        jnp.einsum("hji,ihd->jhd", coarse_dscore, all_keys, preferred_element_type=jnp.float32)
        * coarse_scale
    )
    key_terms_all = (
        jnp.einsum("hji,jhd->ihd", coarse_dscore, pooled_qh, preferred_element_type=jnp.float32)
        * coarse_scale
    )
    value_terms_all = jnp.einsum(
        "hji,jhd->ihd", coarse_weights, pooled_grad_heads, preferred_element_type=jnp.float32
    )
    term_table = jnp.concatenate(
        (
            key_terms_all.reshape(total_rows, col_count),
            value_terms_all.reshape(total_rows, col_count),
        ),
        1,
    )
    summed = lax.psum_scatter(
        term_table.astype(jnp.bfloat16), "ctx", scatter_dimension=0, tiled=True
    ).astype(jnp.float32)
    grad_k_coarse = summed[:, :col_count]
    grad_v_coarse = summed[:, col_count:]
    coarse_grads = jnp.concatenate(
        (grad_q_coarse.reshape(short_rows, col_count), grad_k_coarse, grad_v_coarse), 1
    )
    next_first = from_behind(coarse_grads[:1], "ctx", -1)
    spread = (
        jnp.repeat(jnp.concatenate((coarse_grads, next_first), 0), SHORT, axis=0)[
            SHORT - 1 : SHORT - 1 + row_count
        ]
        / SHORT
    )
    q_grad = (grad_q_fine.reshape(row_count, col_count) + spread[:, :col_count]).astype(
        jnp.bfloat16
    )
    k_grad = (
        grad_k_fine.reshape(row_count, col_count) + spread[:, col_count : 2 * col_count]
    ).astype(jnp.bfloat16)
    v_grad = (grad_v_fine.reshape(row_count, col_count) + spread[:, 2 * col_count :]).astype(
        jnp.bfloat16
    )
    return (mixed_out, q_grad, k_grad, v_grad)


def solution(mesh):
    in_specs = (
        P("ctx", "head"),
        P("ctx", "head"),
        P("ctx", "head"),
        P("head", None),
        P("ctx", "head"),
    )
    out_specs = (P("ctx", "head"), P("ctx", "head"), P("ctx", "head"), P("ctx", "head"))
    return jax.shard_map(shards, mesh=mesh, in_specs=in_specs, out_specs=out_specs, check_vma=False)
```

profile of v0, /device:TPU:36, one launch (start us, length us, event | category | flops | bytes accessed | tf_op | source)
XLA Modules:
  0.0 604.7 jit_solution(870741556586209721)
XLA Ops:
  11.0 3.4 collective-permute-start.4
  14.5 3.7 collective-permute-done.4
  18.4 1.8 reshape.160
  20.3 3.3 reduce_sum.55
  24.9 23.9 %all-gather.5.cloned.1.call-done = bf16[256,6144]{1,0:T(8,128)(2,1)} async-done(((bf16[256,1536]{1,0:T(8,128)(2,1)}), bf16[256,6144]{1,0:T(8,128)(2,1)}) %all-gather.5.cloned.1.call-update) | async-done | bytes 3145744 | tf_op jit(solution)/shard_map/all_gather | solution.py:107
  48.8 7.3 %convolution_convert_fusion.2 = bf16[256,768]{1,0:T(8,128)(2,1)S(1)} fusion(bf16[256,6144]{1,0:T(8,128)(2,1)} %all-gather.5.cloned.1.call-done, bf16[768,6144]{1,0:T(8,128)(2,1)} %param.8), kind=kOutput, calls=%fused_computation.19 | convolution fusion | flops 2416115712 | bytes 12976128 | tf_op jit(solution)/shard_map/dot_general | solution.py:106
  56.7 86.6 %all-gather.3.cloned.1.call-done = bf16[2,2048,768]{2,0,1:T(2,128)(2,1)} async-done(((bf16[2,64,768]{2,0,1:T(2,128)(2,1)}), bf16[2,2048,768]{2,0,1:T(2,128)(2,1)}) %all-gather.3.cloned.1.call-update) | async-done | bytes 6291472 | tf_op jit(solution)/shard_map/all_gather | solution.py:75
  143.4 13.8 %fusion.47 = (bf16[1,2048,768]{2,0,1:T(2,128)(2,1)}, bf16[1,2048,768]{2,0,1:T(2,128)(2,1)}) fusion(bf16[2,2048,768]{2,0,1:T(2,128)(2,1)} %all-gather.3.cloned.1.call-done), kind=kLoop, calls=%fused_computation.124 | loop fusion | bytes 12582912 | tf_op jit(solution)/shard_map/slice | solution.py:81
  157.1 15.3 %copy.127 = bf16[1,2048,768]{1,2,0:T(8,128)(2,1)} copy(bf16[1,2048,768]{2,0,1:T(2,128)(2,1)} %get-tuple-element.6) | data formatting | bytes 6291456
  172.4 2.9 fusion.53
  175.9 15.3 %copy.126 = bf16[1,2048,768]{1,2,0:T(8,128)(2,1)} copy(bf16[1,2048,768]{2,0,1:T(2,128)(2,1)} %get-tuple-element.7) | data formatting | bytes 6291456
  193.1 2.0 fusion.38
  198.3 3.8 pad_maximum_fusion
  202.1 8.6 %copy.123 = bf16[2048,1536]{1,0:T(8,128)(2,1)} copy(bf16[2048,1536]{0,1:T(8,128)(2,1)} %pad_maximum_fusion) | data formatting | bytes 12582912
  213.0 4.6 collective-permute-start
  217.6 3.1 collective-permute-start.1
  220.7 3.3 collective-permute-start.2
  224.0 5.0 collective-permute-start.3
  231.7 6.9 %collective-permute-done = bf16[2,256,768]{1,2,0:T(8,128)(2,1)} collective-permute-done((bf16[2,256,768]{1,2,0:T(8,128)(2,1)}, bf16[2,256,768]{1,2,0:T(8,128)(2,1)}, u32[]{:S(2)}, u32[]{:S(2)}) %collective-permute-start) | collective-permute-done | bytes 786464 | tf_op jit(solution)/shard_map/ppermute | solution.py:16
  238.6 1.9 fusion.51
  240.7 20.2 %collective-permute-done.1 = bf16[2,256,768]{1,2,0:T(8,128)(2,1)} collective-permute-done((bf16[2,256,768]{1,2,0:T(8,128)(2,1)}, bf16[2,256,768]{1,2,0:T(8,128)(2,1)}, u32[]{:S(2)}, u32[]{:S(2)}) %collective-permute-start.1) | collective-permute-done | bytes 786464 | tf_op jit(solution)/shard_map/ppermute | solution.py:16
  260.9 1.9 fusion.50
  263.0 2.1 fusion.49
  266.3 13.1 %collective-permute-done.3 = bf16[2,256,768]{1,2,0:T(8,128)(2,1)} collective-permute-done((bf16[2,256,768]{1,2,0:T(8,128)(2,1)}, bf16[2,256,768]{1,2,0:T(8,128)(2,1)}, u32[]{:S(2)}, u32[]{:S(2)}) %collective-permute-start.3) | collective-permute-done | bytes 786464 | tf_op jit(solution)/shard_map/ppermute | solution.py:16
  279.4 2.0 fusion.48
  281.5 1.9 copy.75
  291.6 2.0 copy-done
  293.8 4.7 fusion.19
  301.9 8.5 %convolution_convert_fusion = bf16[256,6144]{1,0:T(8,128)(2,1)} fusion(bf16[768,6144]{1,0:T(8,128)(2,1)} %param.8, f32[256,768]{1,0:T(8,128)} %copy.86, f32[256,768]{1,0:T(8,128)} %reshape.148), kind=kOutput, calls=%fused_computation.4 | convolution fusion | flops 2417885184 | bytes 14155776 | tf_op jit(solution)/shard_map/dot_general | solution.py:102
  310.4 5.2 multiply_convert_fusion
  315.6 3.4 fusion.55
  319.2 6.9 %fusion.54 = (bf16[1280,6,128]{0,2,1:T(8,128)(2,1)S(1)}, f32[1280,6,128]{0,2,1:T(8,128)}) fusion(bf16[256,6,128]{0,2,1:T(8,128)(2,1)S(1)} %bitcast.169, f32[6,256,1280]{1,2,0:T(8,128)} %copy-done, f32[6,256]{1,0:T(8,128)S(1)} %log_add_fusion), kind=kOutput, calls=%fused_computation.131 | convolution fusion | flops 508231680 | bytes 14161920 | tf_op jit(solution)/shard_map/hts,thd->shd/dot_general | solution.py:126
  326.3 24.6 %collective-permute-start.6 = (bf16[2,256,6,128]{1,3,2,0:T(8,128)(2,1)S(1)}, bf16[2,256,6,128]{1,3,2,0:T(8,128)(2,1)}, u32[]{:S(2)}, u32[]{:S(2)}) collective-permute-start(bf16[2,256,6,128]{1,3,2,0:T(8,128)(2,1)S(1)} %pad_maximum_fusion.5), channel_id=1, source_target_pairs={{4,0},{8,4},{12,8},{16,12},{20,16},{24,20},{28,24},{32,28},{36,32}... | collective-permute-start | bytes 2359304 | tf_op jit(solution)/shard_map/ppermute | solution.py:16
  351.1 1.9 collective-permute-start.7
  354.0 1.9 collective-permute-start.8
  356.9 1.9 collective-permute-start.9
  360.8 9.2 %collective-permute-done.6 = bf16[2,256,6,128]{1,3,2,0:T(8,128)(2,1)} collective-permute-done((bf16[2,256,6,128]{1,3,2,0:T(8,128)(2,1)S(1)}, bf16[2,256,6,128]{1,3,2,0:T(8,128)(2,1)}, u32[]{:S(2)}, u32[]{:S(2)}) %collective-permute-start.6) | collective-permute-done | bytes 786464 | tf_op jit(solution)/shard_map/ppermute | solution.py:16
  371.3 49.9 %collective-permute-done.7 = bf16[2,256,6,128]{1,3,2,0:T(8,128)(2,1)} collective-permute-done((bf16[2,256,6,128]{1,3,2,0:T(8,128)(2,1)S(1)}, bf16[2,256,6,128]{1,3,2,0:T(8,128)(2,1)}, u32[]{:S(2)}, u32[]{:S(2)}) %collective-permute-start.7) | collective-permute-done | bytes 786464 | tf_op jit(solution)/shard_map/ppermute | solution.py:16
  421.2 2.5 convert_element_type.83
  423.8 2.5 convert_element_type.84
  426.3 2.4 convert_element_type.85
  430.8 128.4 %reduce-scatter.7.cloned.1.call-done = bf16[64,1536]{1,0:T(8,128)(2,1)} async-done(((bf16[2048,1536]{1,0:T(8,128)(2,1)}), bf16[64,1536]{1,0:T(8,128)(2,1)}) %reduce-scatter.7.cloned.1.call-update) | async-done | bytes 196624
  561.9 3.7 collective-permute-start.5
  565.6 4.2 fusion.9
  569.8 2.5 copy.107
  575.8 2.3 reshape.156
  578.1 2.1 slice_multiply_fusion
  581.6 16.6 %reduce-scatter.5.cloned.1.call-done = bf16[256,1536]{1,0:T(8,128)(2,1)} async-done(((bf16[256,6144]{1,0:T(8,128)(2,1)}), bf16[256,1536]{1,0:T(8,128)(2,1)}) %reduce-scatter.5.cloned.1.call-update) | async-done | bytes 786448 | tf_op jit(solution)/shard_map/reduce_scatter | solution.py:103
  (128 shorter events, 45.3 us)
Async XLA Ops:
  7.2 41.7 %all-gather.5.cloned.1.call-start = ((), (), s32[]{:S(2)}) async-start(), calls=%async_computation.4 | async-start | bytes 3932160 | tf_op jit(solution)/shard_map/all_gather | solution.py:107
  7.9 135.5 %all-gather.3.cloned.1.call-start = ((), (), s32[]{:S(2)}) async-start(), calls=%async_computation.2 | async-start | bytes 6488064 | tf_op jit(solution)/shard_map/all_gather | solution.py:75
  11.0 7.2 %collective-permute-start.4 = (bf16[3,2304]{1,0:T(4,128)(2,1)S(1)}, bf16[3,2304]{1,0:T(4,128)(2,1)S(1)}, u32[]{:S(2)}, u32[]{:S(2)}) collective-permute-start(bf16[3,2304]{1,0:T(4,128)(2,1)S(1)} %slice.171), channel_id=1, source_target_pairs={{0,4},{4,8},{8,12},{12,16},{16,20},{20,24},{24,28},{28,32},{32,36}... | collective-permute-start | bytes 41480 | tf_op jit(solution)/shard_map/ppermute | solution.py:16
  24.6 534.6 %reduce-scatter.7.cloned.1.call-start = ((), (), s32[]{:S(2)}) async-start(), calls=%async_computation.5 | async-start | bytes 6488064
  56.1 101.0 %copy-start.14 = (bf16[256,768]{1,0:T(8,128)(2,1)}, bf16[256,768]{1,0:T(8,128)(2,1)S(1)}, u32[]{:S(2)}) copy-start(bf16[256,768]{1,0:T(8,128)(2,1)S(1)} %convolution_convert_fusion.2) | copy-start | bytes 1179652
  191.2 1.9 copy-start.1
  196.2 1.1 copy-start.3
  210.7 1.0 copy-start.11
  210.7 1.2 copy-start.12
  210.7 20.8 %copy-start.13 = (bf16[256,768]{1,0:T(8,128)(2,1)S(1)}, bf16[256,768]{1,0:T(8,128)(2,1)}, u32[]{:S(2)}) copy-start(bf16[256,768]{1,0:T(8,128)(2,1)} %param.5) | copy-start | bytes 1179652
  210.7 387.4 %reduce-scatter.5.cloned.1.call-start = ((), (), s32[]{:S(2)}) async-start(), calls=%async_computation.3 | async-start | bytes 3932160 | tf_op jit(solution)/shard_map/reduce_scatter | solution.py:103
  213.0 25.6 %collective-permute-start = (bf16[2,256,768]{1,2,0:T(8,128)(2,1)}, bf16[2,256,768]{1,2,0:T(8,128)(2,1)}, u32[]{:S(2)}, u32[]{:S(2)}) collective-permute-start(bf16[2,256,768]{1,2,0:T(8,128)(2,1)} %pad_maximum_fusion.4), channel_id=1, source_target_pairs={{0,4},{4,8},{8,12},{12,16},{16,20},{20,24},{24,28},{28,32},{32,36}... | collective-permute-start | bytes 2359304 | tf_op jit(solution)/shard_map/ppermute | solution.py:16
  217.6 43.3 %collective-permute-start.1 = (bf16[2,256,768]{1,2,0:T(8,128)(2,1)}, bf16[2,256,768]{1,2,0:T(8,128)(2,1)}, u32[]{:S(2)}, u32[]{:S(2)}) collective-permute-start(bf16[2,256,768]{1,2,0:T(8,128)(2,1)} %pad_maximum_fusion.4), channel_id=1, source_target_pairs={{0,8},{4,12},{8,16},{12,20},{16,24},{20,28},{24,32},{28,36},{32,40... | collective-permute-start | bytes 2359304 | tf_op jit(solution)/shard_map/ppermute | solution.py:16
  220.7 42.3 %collective-permute-start.2 = (bf16[2,256,768]{1,2,0:T(8,128)(2,1)}, bf16[2,256,768]{1,2,0:T(8,128)(2,1)}, u32[]{:S(2)}, u32[]{:S(2)}) collective-permute-start(bf16[2,256,768]{1,2,0:T(8,128)(2,1)} %pad_maximum_fusion.4), channel_id=1, source_target_pairs={{0,12},{4,16},{8,20},{12,24},{16,28},{20,32},{24,36},{28,40},{32,4... | collective-permute-start | bytes 2359304 | tf_op jit(solution)/shard_map/ppermute | solution.py:16
  224.0 55.4 %collective-permute-start.3 = (bf16[2,256,768]{1,2,0:T(8,128)(2,1)}, bf16[2,256,768]{1,2,0:T(8,128)(2,1)}, u32[]{:S(2)}, u32[]{:S(2)}) collective-permute-start(bf16[2,256,768]{1,2,0:T(8,128)(2,1)} %pad_maximum_fusion.4), channel_id=1, source_target_pairs={{0,16},{4,20},{8,24},{12,28},{16,32},{20,36},{24,40},{28,44},{32,4... | collective-permute-start | bytes 2359304 | tf_op jit(solution)/shard_map/ppermute | solution.py:16
  229.7 0.7 copy-start.20
  283.4 4.3 copy-start.16
  283.4 4.4 copy-start.17
  283.4 4.4 copy-start.18
  283.4 4.4 copy-start.19
  283.4 4.5 copy-start.21
  287.7 1.5 copy-start.5
  290.6 3.1 copy-start
  290.6 3.1 copy-start.15
  326.2 32.5 %copy-start.6 = (bf16[1280,6,128]{2,0,1:T(8,128)(2,1)S(1)}, bf16[1280,6,128]{2,0,1:T(8,128)(2,1)}, u32[]{:S(2)}) copy-start(bf16[1280,6,128]{2,0,1:T(8,128)(2,1)} %constant_dynamic-update-slice_fusion.5) | copy-start | bytes 5898244
  326.3 43.7 %collective-permute-start.6 = (bf16[2,256,6,128]{1,3,2,0:T(8,128)(2,1)S(1)}, bf16[2,256,6,128]{1,3,2,0:T(8,128)(2,1)}, u32[]{:S(2)}, u32[]{:S(2)}) collective-permute-start(bf16[2,256,6,128]{1,3,2,0:T(8,128)(2,1)S(1)} %pad_maximum_fusion.5), channel_id=1, source_target_pairs={{4,0},{8,4},{12,8},{16,12},{20,16},{24,20},{28,24},{32,28},{36,32}... | collective-permute-start | bytes 2359304 | tf_op jit(solution)/shard_map/ppermute | solution.py:16
  351.1 70.2 %collective-permute-start.7 = (bf16[2,256,6,128]{1,3,2,0:T(8,128)(2,1)S(1)}, bf16[2,256,6,128]{1,3,2,0:T(8,128)(2,1)}, u32[]{:S(2)}, u32[]{:S(2)}) collective-permute-start(bf16[2,256,6,128]{1,3,2,0:T(8,128)(2,1)S(1)} %pad_maximum_fusion.6), channel_id=1, source_target_pairs={{8,0},{12,4},{16,8},{20,12},{24,16},{28,20},{32,24},{36,28},{40,32... | collective-permute-start | bytes 2359304 | tf_op jit(solution)/shard_map/ppermute | solution.py:16
  354.0 69.8 %collective-permute-start.8 = (bf16[2,256,6,128]{1,3,2,0:T(8,128)(2,1)}, bf16[2,256,6,128]{1,3,2,0:T(8,128)(2,1)}, u32[]{:S(2)}, u32[]{:S(2)}) collective-permute-start(bf16[2,256,6,128]{1,3,2,0:T(8,128)(2,1)} %pad_maximum_fusion.7), channel_id=1, source_target_pairs={{12,0},{16,4},{20,8},{24,12},{28,16},{32,20},{36,24},{40,28},{44,3... | collective-permute-start | bytes 2359304 | tf_op jit(solution)/shard_map/ppermute | solution.py:16
  356.9 69.4 %collective-permute-start.9 = (bf16[2,256,6,128]{1,3,2,0:T(8,128)(2,1)}, bf16[2,256,6,128]{1,3,2,0:T(8,128)(2,1)}, u32[]{:S(2)}, u32[]{:S(2)}) collective-permute-start(bf16[2,256,6,128]{1,3,2,0:T(8,128)(2,1)} %pad_maximum_fusion.8), channel_id=1, source_target_pairs={{16,0},{20,4},{24,8},{28,12},{32,16},{36,20},{40,24},{44,28},{48,3... | collective-permute-start | bytes 2359304 | tf_op jit(solution)/shard_map/ppermute | solution.py:16
  371.3 57.4 %copy-start.2 = (bf16[1,2048,768]{1,2,0:T(8,128)(2,1)S(1)}, bf16[1,2048,768]{1,2,0:T(8,128)(2,1)}, u32[]{:S(2)}) copy-start(bf16[1,2048,768]{1,2,0:T(8,128)(2,1)} %copy.127) | copy-start | bytes 9437188
  371.3 57.4 %copy-start.4 = (bf16[6,64,2048]{2,1,0:T(8,128)(2,1)S(1)}, bf16[6,64,2048]{2,1,0:T(8,128)(2,1)}, u32[]{:S(2)}) copy-start(bf16[6,64,2048]{2,1,0:T(8,128)(2,1)} %copy-done.3) | copy-start | bytes 4718596
  561.9 11.6 %collective-permute-start.5 = (f32[1,2304]{1,0:T(1,128)S(1)}, f32[1,2304]{1,0:T(1,128)}, u32[]{:S(2)}, u32[]{:S(2)}) collective-permute-start(f32[1,2304]{1,0:T(1,128)S(1)} %copy.101), channel_id=1, source_target_pairs={{4,0},{8,4},{12,8},{16,12},{20,16},{24,20},{28,24},{32,28},{36,32}... | collective-permute-start | bytes 27656 | tf_op jit(solution)/shard_map/ppermute | solution.py:16
  569.8 4.7 copy-start.7
  578.1 2.1 copy-start.8
  578.1 2.2 copy-start.9
  578.1 2.4 copy-start.10
Sparse Core Ops, SparseCore 0:
  9.7 39.1 all-gather.4
  52.4 90.9 all-gather.2
  210.8 348.2 reduce-scatter.6
  562.0 36.0 reduce-scatter.4
where the time goes:
time: 609 us; the launch traced here: 605 us
  waiting for transfers between devices  359 us (59%)
  local copies, waits for them, and re-layouts  98.9 us (16%)
  starting transfers between devices  53.8 us (9%)
  matrix products  47.3 us (8%)
  other arithmetic  31 us (5%)
  between operations  14.4 us (2%)
    unnamed x5, waiting for transfers between devices  129 us
    ppermute x10, waiting for transfers between devices, from_behind(): return lax.ppermute(shard, axis, pairs)  103 us
    all_gather x1, waiting for transfers between devices, shards(): lax.all_gather(jnp.stack((pooled[:, col_count:2 * col_count], pooled[:, 2...  86.6 us
    unnamed x62, local copies, waits for them, and re-layouts  53.6 us
    ppermute x10, starting transfers between devices, from_behind(): return lax.ppermute(shard, axis, pairs)  53.5 us
    all_gather x1, waiting for transfers between devices, shards(): lax.all_gather(out_grad, 'head', axis=1, tiled=True)  23.9 us
    reduce_scatter x1, waiting for transfers between devices, shards(): lax.psum_scatter(partial_value.astype(jnp.bfloat16), 'head', scatter_dime...  16.6 us
    slice x1, local copies, waits for them, and re-layouts, shards(): all_keys = heads_of(gathered[0])  13.8 us
  transfers between devices with their start and end apart: 14, of which 10 were waited for; matrix products, arithmetic and copies ran while one was open for 17% of the time, Pallas kernels for 0%

commit v1 on v0

v1 whole, which is shorter than its diff:
```python
import functools
import math

import jax
import jax.numpy as jnp
import numpy as np
from jax import lax
from jax.experimental import pallas as pl
from jax.experimental.pallas import tpu as pltpu
from jax.sharding import Mesh, PartitionSpec as P

HEAD_DIM = 128
SHORT = 4
WINDOW = 1024
PLANES = 4
PLANE_DEVS = 8
BLOCK = 256
TAIL = 16
LOG2E = math.log2(math.e)
SCALE = 1.0 / math.sqrt(HEAD_DIM)
COARSE_SCALE = 2.0 * SCALE
FAR = -1e30
PLANE = ("y", "xh")
bf16 = jnp.bfloat16
f32 = jnp.float32


def call(kernel, out_shape, vmem_mib, **rest):
    return pl.pallas_call(
        kernel,
        out_shape=out_shape,
        compiler_params=pltpu.CompilerParams(vmem_limit_bytes=vmem_mib * 1024 * 1024),
        **rest,
    )


def dot(a, b):
    return jnp.dot(a, b, preferred_element_type=f32)


def dot_nt(a, b):
    return lax.dot_general(a, b, (((1,), (1,)), ((), ())), preferred_element_type=f32)


def iota(shape, dim):
    return lax.broadcasted_iota(jnp.int32, shape, dim)


def split(x):
    high = x.astype(bf16)
    return high, (x - high.astype(f32)).astype(bf16)


def ones_where(mask):
    return jnp.where(mask, 1.0, 0.0).astype(bf16)


def pack_kernel(q_ref, k_ref, v_ref, out_ref, sems):
    tokens = q_ref.shape[0]
    last = q_ref.shape[1] // HEAD_DIM - 1
    copies = []
    for slot in range(PLANE_DEVS):
        cols = pl.ds(min(slot, last) * HEAD_DIM, HEAD_DIM)
        tail = q_ref.at[tokens - TAIL :, cols]
        pieces = (
            (k_ref.at[:, cols], out_ref.at[slot, 0:tokens, 0:128]),
            (v_ref.at[:, cols], out_ref.at[slot, 0:tokens, 128:256]),
            (tail, out_ref.at[slot, tokens:, 0:128]),
            (tail, out_ref.at[slot, tokens:, 128:256]),
        )
        for at, (source, target) in enumerate(pieces):
            copies.append(pltpu.make_async_copy(source, target, sems.at[slot, at]))
    for copy in copies:
        copy.start()
    for copy in copies:
        copy.wait()


def pooling(lead):
    shape = (BLOCK // SHORT, BLOCK + lead)
    back = iota(shape, 1) - lead - SHORT * iota(shape, 0)
    return ones_where((back <= 0) & (back > -SHORT))


def spreading():
    shape = (BLOCK, BLOCK // SHORT + TAIL)
    return ones_where((iota(shape, 0) + (SHORT - 1)) // SHORT == iota(shape, 1))


def pooled_rows(block, lead=None):
    rows = block if lead is None else jnp.concatenate([lead, block], 0)
    taken = pooling(0 if lead is None else TAIL)
    return (dot(taken, rows) * (1.0 / SHORT)).astype(bf16)


def pool_kernel(x_ref, after_ref, near_ref, far_ref):
    del after_ref
    devs, tokens = x_ref.shape[0], x_ref.shape[1] - TAIL
    step = tokens // SHORT
    half = WINDOW // SHORT
    coarse = devs * step
    for slot in range(devs):
        block = x_ref[slot, 0:tokens, :]
        lead = x_ref[slot - 1, tokens - TAIL : tokens, :] if slot else None
        far_ref[slot * step : (slot + 1) * step, :] = pooled_rows(block, lead)
        late = slot * tokens - (devs * tokens - WINDOW)
        if late >= 0:
            near_ref[late : late + tokens, :] = block
    far_ref[coarse : coarse + TAIL, :] = x_ref[devs - 1, tokens - TAIL : tokens, :]
    near_ref[WINDOW : WINDOW + TAIL, :] = x_ref[devs - 1, tokens:, :]
    near_ref[WINDOW + TAIL :, :] = far_ref[0 : half + TAIL, :]


def first_row_fixed(pooled, tail):
    kept = jnp.where(iota(tail.shape, 0) > TAIL - SHORT, tail.astype(f32), 0.0)
    lacking = jnp.sum(kept, 0, keepdims=True) * (1.0 / SHORT)
    head = pooled[0:TAIL, :].astype(f32)
    return jnp.where(iota(head.shape, 0) == 0, head + lacking, head).astype(bf16)


def attention_kernel(
    z_ref,
    x_ref,
    own_ref,
    near_ref,
    far2_ref,
    far3_ref,
    pair_ref,
    attn_ref,
    fine_ref,
    coarse_ref,
    back1_ref,
    back2_ref,
    back3_ref,
    kx,
    vx,
    kxt,
    vxt,
    kc,
    vc,
    kct,
    vct,
    pq,
    gp,
    dkx,
    dvx,
    dkc,
    dvc,
    high_t,
    low_t,
    high,
    low,
    query_high,
    query_low,
):
    z = z_ref[0]
    rows = pair_ref.shape[0]
    tokens = rows // PLANE_DEVS
    coarse = rows // SHORT
    half = WINDOW // SHORT
    step = BLOCK // SHORT
    span = WINDOW + BLOCK
    reach = WINDOW // BLOCK

    kx[0:WINDOW, :] = near_ref[0:WINDOW, 0:128]
    vx[0:WINDOW, :] = near_ref[0:WINDOW, 128:256]
    for slot in range(PLANE_DEVS):
        at = WINDOW + slot * tokens
        kx[at : at + tokens, :] = x_ref[slot, 0:tokens, 0:128]
        vx[at : at + tokens, :] = x_ref[slot, 0:tokens, 128:256]

    def transposed(ref, out, count):
        def body(i, carry):
            at = pl.multiple_of(i * BLOCK, BLOCK)
            out[:, pl.ds(at, BLOCK)] = ref[pl.ds(at, BLOCK), :].T
            return carry

        lax.fori_loop(0, count, body, 0)

    transposed(kx, kxt, (WINDOW + rows) // BLOCK)
    transposed(vx, vxt, (WINDOW + rows) // BLOCK)

    tails = [
        near_ref[WINDOW - TAIL : WINDOW, :],
        far2_ref[coarse : coarse + TAIL, :],
        far3_ref[coarse : coarse + TAIL, :],
    ]
    base = WINDOW + TAIL
    for piece in range(reach):
        at = coarse + half + piece * step
        block = near_ref[piece * BLOCK : (piece + 1) * BLOCK, :]
        lead = near_ref[piece * BLOCK - TAIL : piece * BLOCK, :] if piece else None
        rest = pooled_rows(block, lead)
        kc[at : at + step, :] = rest[:, 0:128]
        vc[at : at + step, :] = rest[:, 128:256]
    sources = ((own_ref, coarse), (near_ref.at[base:], half + TAIL), (far2_ref, coarse), (far3_ref, coarse))
    for slot, (source, count) in enumerate(sources):
        at = slot * coarse
        kc[at : at + count, :] = source[0:count, 0:128]
        vc[at : at + count, :] = source[0:count, 128:256]
        if slot + 1 < PLANES:
            fixed = first_row_fixed(source[0:TAIL, :], tails[slot])
            kc[at : at + TAIL, :] = fixed[:, 0:128]
            vc[at : at + TAIL, :] = fixed[:, 128:256]
    transposed(kc, kct, PLANES * coarse // BLOCK)
    transposed(vc, vct, PLANES * coarse // BLOCK)

    shape = (step, BLOCK)
    offset = iota(shape, 1) - SHORT * iota(shape, 0)
    taken = ones_where((offset >= 0) & (offset < SHORT))
    for block in range(rows // BLOCK):
        at = block * BLOCK
        lead = pair_ref[at - TAIL : at, 0:128] if block else near_ref[WINDOW : WINDOW + TAIL, 0:128]
        pq[block * step : (block + 1) * step, :] = pooled_rows(pair_ref[at : at + BLOCK, 0:128], lead)
        gp[block * step : (block + 1) * step, :] = dot(
            taken, pair_ref[at : at + BLOCK, 128:256]
        ).astype(bf16)

    def weights(scores, biases, factor):
        tops = [jnp.max(s, 0, keepdims=True) + b for s, b in zip(scores, biases)]
        top = functools.reduce(jnp.maximum, tops)
        exps = [jnp.exp2((s - (top - b)) * factor) for s, b in zip(scores, biases)]
        total = functools.reduce(jnp.add, [jnp.sum(e, 0, keepdims=True) for e in exps])
        inverse = 1.0 / total
        return jnp.concatenate([e * inverse for e in exps], 0)

    row_at, col_at = iota((BLOCK, BLOCK), 0), iota((BLOCK, BLOCK), 1)
    diagonal = row_at <= col_at
    for block in range(coarse // BLOCK):
        at = block * BLOCK
        query = pq[at : at + BLOCK, :]
        grad = gp[at : at + BLOCK, :]
        scores, biases, keys, values = [], [], [], []
        for piece in range(block + 1):
            s = dot_nt(kc[piece * BLOCK : (piece + 1) * BLOCK, :], query)
            scores.append(jnp.where(diagonal, s, FAR) if piece == block else s)
            biases.append(0.0)
        for slot in range(1, PLANES):
            s = dot_nt(kc[slot * coarse : (slot + 1) * coarse, :], query)
            scores.append(s)
            biases.append(jnp.where(z >= slot, 0.0, FAR))
        probs = weights(scores, biases, COARSE_SCALE * LOG2E)
        rounded = probs.astype(bf16)
        own = at + BLOCK
        parts = ((0, own, 0), (coarse, PLANES * coarse, own))
        out_t = functools.reduce(
            jnp.add, [dot(vct[:, a:b], rounded[c : c + b - a]) for a, b, c in parts]
        )
        grad_t = grad.astype(f32).T
        delta = jnp.sum(grad_t * out_t, 0, keepdims=True)
        high_t[:, at : at + BLOCK], low_t[:, at : at + BLOCK] = split(out_t)
        query_grad_t = jnp.zeros((HEAD_DIM, BLOCK), f32)
        for a, b, c in parts:
            grad_probs = dot_nt(vc[a:b, :], grad)
            grad_scores = (probs[c : c + b - a] * (grad_probs - delta)).astype(bf16)
            query_grad_t += dot(kct[:, a:b], grad_scores)
            dk = dot(grad_scores, query) * COARSE_SCALE
            dv = dot(rounded[c : c + b - a], grad)
            if block == 0:
                dkc[a:b, :] = dk
                dvc[a:b, :] = dv
                if a == 0:
                    dkc[b:coarse, :] = jnp.zeros((coarse - b, HEAD_DIM), f32)
                    dvc[b:coarse, :] = jnp.zeros((coarse - b, HEAD_DIM), f32)
            else:
                dkc[a:b, :] += dk
                dvc[a:b, :] += dv
        query_grad = query_grad_t.T * COARSE_SCALE
        query_high[at : at + BLOCK, :], query_low[at : at + BLOCK, :] = split(query_grad)
    query_high[coarse:, :] = jnp.zeros((TAIL, HEAD_DIM), bf16)
    query_low[coarse:, :] = jnp.zeros((TAIL, HEAD_DIM), bf16)
    coarse_ref[:, 0:128] = dkc[0:coarse, :]
    coarse_ref[:, 128:256] = dvc[0:coarse, :]

    dkx[...] = jnp.zeros_like(dkx)
    dvx[...] = jnp.zeros_like(dvx)

    def window(block, carry):
        at = pl.multiple_of(block * BLOCK, BLOCK)
        query = pair_ref[pl.ds(at, BLOCK), 0:128]
        grad = pair_ref[pl.ds(at, BLOCK), 128:256]
        scores, biases = [], []
        for piece in range(reach + 1):
            key = kx[pl.ds(pl.multiple_of(at + piece * BLOCK, BLOCK), BLOCK), :]
            s = dot_nt(key, query)
            if piece == 0:
                s = jnp.where(row_at > col_at, s, FAR)
            if piece == reach:
                s = jnp.where(diagonal, s, FAR)
            scores.append(s)
            biases.append(jnp.where((z == 0) & (block + piece < reach), FAR, 0.0))
        probs = weights(scores, biases, SCALE * LOG2E)
        rounded = probs.astype(bf16)
        out_t = dot(vxt[:, pl.ds(at, span)], rounded)
        grad_t = grad.astype(f32).T
        delta = jnp.sum(grad_t * out_t, 0, keepdims=True)
        pair = pl.multiple_of(block // 2 * (2 * step), 2 * step)
        shape = (2 * step, BLOCK)
        spread = ones_where(iota(shape, 0) == block % 2 * step + iota(shape, 1) // SHORT)
        short_t = dot(high_t[:, pl.ds(pair, 2 * step)], spread)
        short_t += dot(low_t[:, pl.ds(pair, 2 * step)], spread)
        attn_ref[pl.ds(at, BLOCK), 0:128] = (out_t + short_t).T.astype(bf16)
        grad_probs = dot_nt(vx[pl.ds(at, span), :], grad)
        grad_scores = (probs * (grad_probs - delta)).astype(bf16)
        query_grad = dot(kxt[:, pl.ds(at, span)], grad_scores).T * SCALE
        below = pl.ds(pl.multiple_of(block * step, step), step + TAIL)
        spread = dot(spreading(), query_high[below, :]) + dot(spreading(), query_low[below, :])
        query_grad += spread * (1.0 / SHORT)
        attn_ref[pl.ds(at, BLOCK), 128:256] = query_grad.astype(bf16)
        dkx[pl.ds(at, span), :] += dot(grad_scores, query)
        dvx[pl.ds(at, span), :] += dot(rounded, grad)
        return carry

    lax.fori_loop(0, rows // BLOCK, window, 0, unroll=8)
    fine_ref[:, 0:128] = dkx[WINDOW:, :] * SCALE
    fine_ref[:, 128:256] = dvx[WINDOW:, :]

    first = iota((TAIL, HEAD_DIM), 0) == 0
    for cols, short in ((slice(0, 128), dkc), (slice(128, 256), dvc)):
        high[0:half, cols], low[0:half, cols] = split(short[2 * coarse - half : 2 * coarse, :])
        above = jnp.where(first, short[0:TAIL, :], 0.0)
        high[half:, cols], low[half:, cols] = split(above)
    taken = spreading()
    for piece in range(reach):
        at = piece * BLOCK
        below = piece * step
        spread = dot(taken, high[below : below + step + TAIL, :])
        spread += dot(taken, low[below : below + step + TAIL, :])
        spread = spread * (1.0 / SHORT)
        back1_ref[at : at + BLOCK, 0:128] = (
            dkx[at : at + BLOCK, :] * SCALE + spread[:, 0:128]
        ).astype(bf16)
        back1_ref[at : at + BLOCK, 128:256] = (
            dvx[at : at + BLOCK, :] + spread[:, 128:256]
        ).astype(bf16)
    query_row = jnp.where(first, query_high[0:TAIL, :].astype(f32), 0.0).astype(bf16)
    back1_ref[WINDOW:base, 0:128] = query_row
    back1_ref[WINDOW:base, 128:256] = query_row
    back1_ref[base:, 0:128] = dkc[coarse : coarse + half + TAIL, :].astype(bf16)
    back1_ref[base:, 128:256] = dvc[coarse : coarse + half + TAIL, :].astype(bf16)
    for slot, ref in ((2, back2_ref), (3, back3_ref)):
        at = slot * coarse
        above = at - coarse
        for cols, short in ((slice(0, 128), dkc), (slice(128, 256), dvc)):
            ref[0:coarse, cols] = short[at : at + coarse, :].astype(bf16)
            row = jnp.where(first, short[above : above + TAIL, :], 0.0)
            ref[coarse : coarse + TAIL, cols] = row.astype(bf16)


def finish_kernel(fine_ref, coarse_ref, back1_ref, back2_ref, back3_ref, out_ref, high, low):
    rows = fine_ref.shape[0]
    tokens = rows // PLANE_DEVS
    coarse = rows // SHORT
    half = coarse - WINDOW // SHORT
    step = BLOCK // SHORT
    base = WINDOW + TAIL
    part = half + TAIL
    ups = (back2_ref, back3_ref)
    total = coarse_ref[...]
    for up in ups:
        total += up[0:coarse, :].astype(f32)
    near = total[0:part, :] + back1_ref[base:, :].astype(f32)
    high[0:part, :], low[0:part, :] = split(near)
    high[part : part + half, :], low[part : part + half, :] = split(total[half:, :])
    extra = functools.reduce(jnp.add, [up[coarse : coarse + TAIL, :].astype(f32) for up in ups])
    high[part + half :, :], low[part + half :, :] = split(extra)
    taken = spreading()
    for block in range(rows // BLOCK):
        at = block * BLOCK
        late = at - (rows - WINDOW)
        below = block * step if late < 0 else part + late // SHORT
        spread = dot(taken, high[below : below + step + TAIL, :])
        spread += dot(taken, low[below : below + step + TAIL, :])
        result = fine_ref[at : at + BLOCK, :] + spread * (1.0 / SHORT)
        if late >= 0:
            result = result + back1_ref[late : late + BLOCK, :].astype(f32)
        out_ref[block, 0:tokens, :] = result.astype(bf16)
        out_ref[block, tokens:, :] = jnp.zeros((TAIL, 256), bf16)
    out_ref[PLANE_DEVS - 1, tokens:, :] = back1_ref[WINDOW:base, :]


def unpack_kernel(pair_ref, x_ref, q_ref, k_ref, v_ref):
    tokens = q_ref.shape[0]
    last = iota((TAIL, HEAD_DIM), 0) > TAIL - SHORT
    for slot in range(q_ref.shape[1] // HEAD_DIM):
        cols = pl.ds(slot * HEAD_DIM, HEAD_DIM)
        k_ref[:, cols] = x_ref[slot, 0:tokens, 0:128]
        v_ref[:, cols] = x_ref[slot, 0:tokens, 128:256]
        q_ref[0 : tokens - TAIL, cols] = pair_ref[slot, 0 : tokens - TAIL, 128:256]
        above = jnp.sum(x_ref[slot, tokens:, 0:128].astype(f32), 0, keepdims=True) * (1.0 / SHORT)
        rest = pair_ref[slot, tokens - TAIL :, 128:256].astype(f32)
        q_ref[tokens - TAIL :, cols] = (rest + jnp.where(last, above, 0.0)).astype(bf16)


def grad_product(halves, a_ref, b_ref, w_ref, total, start):
    at = pl.program_id(0)
    depth = w_ref.shape[1]
    for piece, ref in enumerate((a_ref, b_ref)):
        for half in range(halves):

            @pl.when(at == piece * halves + half)
            def _():
                product = dot_nt(w_ref[...], ref[:, half * depth : (half + 1) * depth])
                if piece + half > 0:
                    total[...] += product
                elif start is None:
                    total[...] = product
                else:
                    total[...] = start[...] + product


def grad_near_kernel(halves, order_ref, a_ref, b_ref, w_ref, total):
    grad_product(halves, a_ref, b_ref, w_ref, total, None)


def grad_far_kernel(halves, order_ref, a_ref, b_ref, w_ref, start, q_ref, out_ref, total):
    grad_product(halves, a_ref, b_ref, w_ref, total, start)

    @pl.when(pl.program_id(0) == pl.num_programs(0) - 1)
    def _():
        last = total.shape[0] // HEAD_DIM - 1
        for slot in range(PLANE_DEVS):
            head = slice(min(slot, last) * HEAD_DIM, (min(slot, last) + 1) * HEAD_DIM)
            out_ref[slot, :, 0:128] = q_ref[:, head]
            out_ref[slot, :, 128:256] = total[head, :].T.astype(bf16)


def grad_part(pieces, order, weight, rest=()):
    rows, width = pieces[0].shape
    depth = weight.shape[0]
    halves = 1
    tile = width // halves

    first = 2 if rest else 0

    def whole(shape):
        return pl.BlockSpec(shape, lambda i, o: (0,) * len(shape))

    packed = (PLANE_DEVS, rows, 2 * HEAD_DIM)
    return pl.pallas_call(
        functools.partial(grad_far_kernel if rest else grad_near_kernel, halves),
        out_shape=jax.ShapeDtypeStruct(packed, bf16) if rest else jax.ShapeDtypeStruct((depth, rows), f32),
        grid_spec=pltpu.PrefetchScalarGridSpec(
            num_scalar_prefetch=1,
            grid=(2 * halves,),
            in_specs=[whole((rows, width))] * 2
            + [pl.BlockSpec((depth, tile), lambda i, o: (0, o[first + i // halves] * halves + i % halves))]
            + [whole(x.shape) for x in rest],
            out_specs=whole(packed if rest else (depth, rows)),
            scratch_shapes=[pltpu.VMEM((depth, rows), f32)] if rest else [],
        ),
        compiler_params=pltpu.CompilerParams(vmem_limit_bytes=62 * 1024 * 1024),
    )(order, *pieces, weight, *rest)


def project_kernel(halves, order_ref, attn_ref, w_ref, *refs):
    send_ref, keep_ref, rows_ref = refs[-3:]
    at = pl.program_id(0)
    heads = w_ref.shape[0] // HEAD_DIM
    tile = w_ref.shape[1]

    @pl.when(at == 0)
    def _():
        for slot in range(heads):
            rows_ref[:, slot * HEAD_DIM : (slot + 1) * HEAD_DIM] = attn_ref[slot, :, 0:128]

    product = dot(rows_ref[...], w_ref[...]).astype(bf16)
    for half in range(halves):

        @pl.when(at == half)
        def _():
            send_ref[:, half * tile : (half + 1) * tile] = product

        @pl.when(at == halves + half)
        def _():
            keep_ref[:, half * tile : (half + 1) * tile] = product


def project(attn, order, last, weight, width, after):
    rows = attn.shape[1]
    depth = weight.shape[0]
    halves = 1
    tile = width // halves
    out = jax.ShapeDtypeStruct((rows, width), bf16)
    return pl.pallas_call(
        functools.partial(project_kernel, halves),
        out_shape=(out, out),
        grid_spec=pltpu.PrefetchScalarGridSpec(
            num_scalar_prefetch=1,
            grid=(2 * halves,),
            in_specs=[
                pl.BlockSpec(attn.shape, lambda i, o: (0, 0, 0)),
                pl.BlockSpec((depth, tile), lambda i, o: (0, o[last - i // halves] * halves + i % halves)),
            ]
            + [pl.BlockSpec(memory_space=pltpu.HBM)] * len(after),
            out_specs=[pl.BlockSpec((rows, width), lambda i, o: (0, 0))] * 2,
            scratch_shapes=[pltpu.VMEM((rows, depth), bf16)],
        ),
        compiler_params=pltpu.CompilerParams(vmem_limit_bytes=62 * 1024 * 1024),
    )(order, attn, weight, *after)


def swap(x, axis):
    return lax.ppermute(x, axis, [(0, 1), (1, 0)])


def planes_up(x, by):
    return lax.ppermute(x, "z", [(i, i + by) for i in range(PLANES) if 0 <= i + by < PLANES])


def in_plane(x):
    return lax.all_to_all(x, PLANE, 0, 0, tiled=True)


def column_blocks():
    xl, core = lax.axis_index("xl"), lax.axis_index("c")
    own, other = 2 * xl, 2 * (1 - xl)
    return jnp.stack([own + core, own + 1 - core, other + core, other + 1 - core]).astype(jnp.int32)


def gathered_grad(out_grad, out_weight, q_proj, blocks):
    far = swap(out_grad, "xl")
    near = swap(out_grad, "c")
    start = grad_part((out_grad, near), blocks, out_weight)
    far, start = lax.optimization_barrier((far, start))
    both = swap(far, "c")
    return start, grad_part((far, both), blocks, out_weight, (start, q_proj))


def projected(attn, out_weight, width, blocks, after):
    def share(last, attn):
        send, keep = project(attn, blocks, last, out_weight, width, after)
        return keep.astype(f32) + swap(send, "c").astype(f32)

    part = share(3, attn).astype(bf16)
    part, attn = lax.optimization_barrier((part, attn))
    far = swap(part, "xl")
    return (share(1, attn) + far.astype(f32)).astype(bf16)


def shards(q_proj, k_proj, v_proj, out_weight, out_grad):
    tokens, cols = q_proj.shape
    rows = tokens * PLANE_DEVS
    coarse = rows // SHORT
    total = PLANES * coarse
    z = lax.axis_index("z").astype(jnp.int32).reshape(1)

    def array(*shape, dtype=bf16):
        return jax.ShapeDtypeStruct(shape, dtype)

    in_place = pl.BlockSpec(memory_space=pltpu.HBM)
    whole = pl.BlockSpec(memory_space=pltpu.VMEM)
    packed = call(
        pack_kernel,
        array(PLANE_DEVS, tokens + TAIL, 2 * HEAD_DIM),
        62,
        in_specs=[in_place] * 3,
        out_specs=whole,
        scratch_shapes=[pltpu.SemaphoreType.DMA((PLANE_DEVS, 4))],
    )(q_proj, k_proj, v_proj)
    own = in_plane(packed)
    blocks = column_blocks()
    early, pair_packed = gathered_grad(out_grad, out_weight, q_proj, blocks)
    near_rows = WINDOW + 2 * TAIL + WINDOW // SHORT
    near, far = call(
        pool_kernel,
        (array(near_rows, 256), array(coarse + TAIL, 256)),
        16,
        in_specs=[whole, in_place],
    )(own, early)
    near_in = planes_up(near, 1)
    far3_in = lax.ppermute(far, "z", [(0, 3), (1, 0)])
    far2_in = lax.ppermute(far3_in, "z", [(3, 2), (0, 3)])
    pair = in_plane(pair_packed).reshape(rows, 2 * HEAD_DIM)

    attn, fine, short, back1, back2, back3 = call(
        attention_kernel,
        (
            array(rows, 256),
            array(rows, 256, dtype=f32),
            array(coarse, 256, dtype=f32),
            array(near_rows, 256),
            array(coarse + TAIL, 256),
            array(coarse + TAIL, 256),
        ),
        62,
        in_specs=[pl.BlockSpec(memory_space=pltpu.SMEM)] + [whole] * 6,
        out_specs=[whole] * 6,
        scratch_shapes=[
            pltpu.VMEM((WINDOW + rows, HEAD_DIM), bf16),
            pltpu.VMEM((WINDOW + rows, HEAD_DIM), bf16),
            pltpu.VMEM((HEAD_DIM, WINDOW + rows), bf16),
            pltpu.VMEM((HEAD_DIM, WINDOW + rows), bf16),
            pltpu.VMEM((total, HEAD_DIM), bf16),
            pltpu.VMEM((total, HEAD_DIM), bf16),
            pltpu.VMEM((HEAD_DIM, total), bf16),
            pltpu.VMEM((HEAD_DIM, total), bf16),
            pltpu.VMEM((coarse, HEAD_DIM), bf16),
            pltpu.VMEM((coarse, HEAD_DIM), bf16),
            pltpu.VMEM((WINDOW + rows, HEAD_DIM), f32),
            pltpu.VMEM((WINDOW + rows, HEAD_DIM), f32),
            pltpu.VMEM((total, HEAD_DIM), f32),
            pltpu.VMEM((total, HEAD_DIM), f32),
            pltpu.VMEM((HEAD_DIM, coarse), bf16),
            pltpu.VMEM((HEAD_DIM, coarse), bf16),
            pltpu.VMEM((WINDOW // SHORT + TAIL, 256), bf16),
            pltpu.VMEM((WINDOW // SHORT + TAIL, 256), bf16),
            pltpu.VMEM((coarse + TAIL, HEAD_DIM), bf16),
            pltpu.VMEM((coarse + TAIL, HEAD_DIM), bf16),
        ],
    )(z, own, far, near_in, far2_in, far3_in, pair)

    back1_in = planes_up(back1, -1)
    halfway = lax.ppermute(back2, "z", [(3, 0), (2, 3)])
    back3_in = lax.ppermute(back3, "z", [(3, 0)])
    back2_in = lax.ppermute(halfway, "z", [(0, 1), (3, 0)])
    attn_in = in_plane(attn.reshape(PLANE_DEVS, tokens, 256))
    finished = call(
        finish_kernel,
        array(PLANE_DEVS, tokens + TAIL, 256),
        32,
        scratch_shapes=[
            pltpu.VMEM((coarse + 2 * TAIL, 256), bf16),
            pltpu.VMEM((coarse + 2 * TAIL, 256), bf16),
        ],
    )(fine, short, back1_in, back2_in, back3_in)
    mixed_out = projected(
        attn_in, out_weight, out_grad.shape[1], blocks, (finished,)
    )
    returned = in_plane(finished)
    grads = call(unpack_kernel, (array(tokens, cols),) * 3, 16)(attn_in, returned)
    return (mixed_out, *grads)


def solution(mesh):
    fine_mesh = Mesh(np.asarray(mesh.devices).reshape(4, 4, 2, 2, 2), ("z", "y", "xh", "xl", "c"))
    both = P(("z", "y", "xh"), ("xl", "c"))
    in_specs = (both, both, both, P(("xl", "c"), None), both)
    return jax.shard_map(
        shards, mesh=fine_mesh, in_specs=in_specs, out_specs=(both,) * 4, check_vma=False
    )
```

time: 609 us -> 174 us (0.29)
  the two profiles are of different devices: /device:TPU:36 before, /device:TPU:4 now
where the time goes in v1:
time: 174 us; the launch traced here: 173 us
  waiting for transfers between devices  58 us (33%)
  Pallas kernels  55.9 us (32%)
  starting transfers between devices  51.6 us (30%)
  local copies, waits for them, and re-layouts  3.51 us (2%)
  other arithmetic  3.39 us (2%)
    all_to_all x4, starting transfers between devices, in_plane(): return lax.all_to_all(x, PLANE, 0, 0, tiled=True)  31.2 us
    pallas_call x1, Pallas kernels, shards(): call(attention_kernel, (array(rows, 256), array(rows, 256, dtype=f32), ar...  25.6 us
    ppermute x6, waiting for transfers between devices, swap(): return lax.ppermute(x, axis, [(0, 1), (1, 0)])  18.7 us
    pallas_call x2, Pallas kernels, project(): pl.pallas_call(functools.partial(project_kernel, halves), out_shape=(out,...  11.8 us
    all_to_all x4, waiting for transfers between devices, in_plane(): return lax.all_to_all(x, PLANE, 0, 0, tiled=True)  11.5 us
    pallas_call x2, Pallas kernels, grad_part(): pl.pallas_call(functools.partial(grad_far_kernel if rest else grad_near_k...  11.2 us
    ppermute x1, waiting for transfers between devices, shards(): halfway = lax.ppermute(back2, 'z', [(3, 0), (2, 3)])  9.73 us
    ppermute x1, waiting for transfers between devices, shards(): far3_in = lax.ppermute(far, 'z', [(0, 3), (1, 0)])  5.98 us
  transfers between devices with their start and end apart: 17, of which 10 were waited for; matrix products, arithmetic and copies ran while one was open for 0% of the time, Pallas kernels for 14%

profile of v1, /device:TPU:4, one launch (start us, length us, event | category | flops | bytes accessed | tf_op | source)
XLA Modules:
  0.0 173.2 jit_solution(5578282002837284106)
XLA Ops:
  0.6 0.1 collective-permute-start.1
  0.7 1.3 collective-permute-start
  2.0 2.7 %shard_map.84 = bf16[8,272,256]{2,1,0:T(8,128)(2,1)} custom-call(bf16[256,768]{1,0:T(8,128)(2,1)} %q_ref.3, bf16[256,768]{1,0:T(8,128)(2,1)} %k_ref.1, bf16[256,768]{1,0:T(8,128)(2,1)} %v_ref.1), custom_call_target="tpu_custom_call" | custom-call | tf_op jit(solution)/shard_map/pallas_call | solution.py:553
  4.7 7.4 %all-to-all-start = ((bf16[8,272,256]{2,1,0:T(8,128)(2,1)}), bf16[8,272,256]{2,1,0:T(8,128)(2,1)S(1)}, u32[]{:S(2)}, u32[]{:S(2)}) async-start(bf16[8,272,256]{2,1,0:T(8,128)(2,1)} %shard_map.84), calls=%async_computation | async-start | bytes 2228224 | tf_op jit(solution)/shard_map/all_to_all | solution.py:512
  12.1 0.7 pad_add_fusion.order_ref
  12.8 0.0 collective-permute-done.1.b_ref
  12.8 5.3 %shard_map.85.after_ref.start = f32[768,256]{1,0:T(8,128)} custom-call(s32[4]{0:T(128)} %pad_add_fusion.order_ref, bf16[256,1536]{1,0:T(8,128)(2,1)} %a_ref.1, bf16[256,1536]{1,0:T(8,128)(2,1)} %collective-permute-done.1.b_ref, bf16[768,6144]{1,0:T(8,128)(2,1)} %w_ref.7), custom_call_target="tpu_custom_call" | custom-call | tf_op jit(solution)/shard_map/pallas_call | solution.py:440
  18.1 3.3 %collective-permute-done.a_ref = bf16[256,1536]{1,0:T(8,128)(2,1)S(1)} collective-permute-done((bf16[256,1536]{1,0:T(8,128)(2,1)}, bf16[256,1536]{1,0:T(8,128)(2,1)S(1)}, u32[]{:S(2)}, u32[]{:S(2)}) %collective-permute-start) | collective-permute-done | bytes 786464 | tf_op jit(solution)/shard_map/ppermute | solution.py:504
  21.4 0.0 collective-permute-start.5
  21.4 2.4 %collective-permute-done.5.b_ref = bf16[256,1536]{1,0:T(8,128)(2,1)} collective-permute-done((bf16[256,1536]{1,0:T(8,128)(2,1)S(1)}, bf16[256,1536]{1,0:T(8,128)(2,1)}, u32[]{:S(2)}, u32[]{:S(2)}) %collective-permute-start.5) | collective-permute-done | bytes 786464 | tf_op jit(solution)/shard_map/ppermute | solution.py:504
  23.8 5.9 %shard_map.87 = bf16[8,256,256]{2,1,0:T(8,128)(2,1)} custom-call(s32[4]{0:T(128)} %pad_add_fusion.order_ref, bf16[256,1536]{1,0:T(8,128)(2,1)} %copy-done.7, bf16[256,1536]{1,0:T(8,128)(2,1)} %collective-permute-done.5.b_ref, bf16[768,6144]{1,0:T(8,128)(2,1)} %w_ref.7, f32[768,256]{1,0:T(8,128)} %shard_map.85.after_ref.start, bf16[256,768]{1,0:T(8,128)(2,1)} %q_ref.3), custom_call_target="tpu_custom_call" | custom-call | tf_op jit(solution)/shard_map/pallas_call | solution.py:440
  29.7 3.2 %all-to-all-done.x_ref = bf16[8,272,256]{2,1,0:T(8,128)(2,1)S(1)} async-done(((bf16[8,272,256]{2,1,0:T(8,128)(2,1)}), bf16[8,272,256]{2,1,0:T(8,128)(2,1)S(1)}, u32[]{:S(2)}, u32[]{:S(2)}) %all-to-all-start) | async-done | bytes 1114144 | tf_op jit(solution)/shard_map/all_to_all | solution.py:512
  32.9 9.2 %all-to-all-start.1 = ((bf16[8,256,256]{2,1,0:T(8,128)(2,1)}), bf16[8,256,256]{2,1,0:T(8,128)(2,1)}, u32[]{:S(2)}, u32[]{:S(2)}) async-start(bf16[8,256,256]{2,1,0:T(8,128)(2,1)} %shard_map.87), calls=%async_computation.1 | async-start | bytes 2097152 | tf_op jit(solution)/shard_map/all_to_all | solution.py:512
  42.1 0.3 shard_map.86
  42.5 0.0 copy-start.6
  42.5 3.9 %collective-permute-start.2 = (bf16[1312,256]{1,0:T(8,128)(2,1)S(1)}, bf16[1312,256]{1,0:T(8,128)(2,1)S(1)}, u32[]{:S(2)}, u32[]{:S(2)}) collective-permute-start(bf16[1312,256]{1,0:T(8,128)(2,1)S(1)} %get-tuple-element.25), channel_id=1, source_target_pairs={{0,32},{32,64},{64,96},{1,33},{33,65},{65,97},{2,34},{34,66},{66,9... | collective-permute-start | bytes 2015240 | tf_op jit(solution)/shard_map/ppermute | solution.py:508
  46.3 3.4 %collective-permute-start.3 = (bf16[528,256]{1,0:T(8,128)(2,1)S(1)}, bf16[528,256]{1,0:T(8,128)(2,1)S(1)}, u32[]{:S(2)}, u32[]{:S(2)}) collective-permute-start(bf16[528,256]{1,0:T(8,128)(2,1)S(1)} %get-tuple-element.24.own_ref), channel_id=1, source_target_pairs={{0,96},{32,0},{1,97},{33,1},{2,98},{34,2},{3,99},{35,3},{4,100},{3... | collective-permute-start | bytes 811016 | tf_op jit(solution)/shard_map/ppermute | solution.py:572
  49.7 6.0 %collective-permute-done.3.far3_ref = bf16[528,256]{1,0:T(8,128)(2,1)S(1)} collective-permute-done((bf16[528,256]{1,0:T(8,128)(2,1)S(1)}, bf16[528,256]{1,0:T(8,128)(2,1)S(1)}, u32[]{:S(2)}, u32[]{:S(2)}) %collective-permute-start.3) | collective-permute-done | bytes 270368 | tf_op jit(solution)/shard_map/ppermute | solution.py:572
  55.7 4.9 %collective-permute-start.4 = (bf16[528,256]{1,0:T(8,128)(2,1)S(1)}, bf16[528,256]{1,0:T(8,128)(2,1)S(1)}, u32[]{:S(2)}, u32[]{:S(2)}) collective-permute-start(bf16[528,256]{1,0:T(8,128)(2,1)S(1)} %collective-permute-done.3.far3_ref), channel_id=1, source_target_pairs={{96,64},{0,96},{97,65},{1,97},{98,66},{2,98},{99,67},{3,99},{100,6... | collective-permute-start | bytes 811016 | tf_op jit(solution)/shard_map/ppermute | solution.py:573
  60.6 4.4 %collective-permute-done.4.far2_ref = bf16[528,256]{1,0:T(8,128)(2,1)S(1)} collective-permute-done((bf16[528,256]{1,0:T(8,128)(2,1)S(1)}, bf16[528,256]{1,0:T(8,128)(2,1)S(1)}, u32[]{:S(2)}, u32[]{:S(2)}) %collective-permute-start.4) | collective-permute-done | bytes 270368 | tf_op jit(solution)/shard_map/ppermute | solution.py:573
  65.0 0.7 copy-done.12
  65.7 0.2 copy-done.10
  65.9 25.6 %shard_map.88 = (bf16[2048,256]{1,0:T(8,128)(2,1)}, f32[2048,256]{1,0:T(8,128)}, f32[512,256]{1,0:T(8,128)}, bf16[1312,256]{1,0:T(8,128)(2,1)}, bf16[528,256]{1,0:T(8,128)(2,1)}, /*index=5*/bf16[528,256]{1,0:T(8,128)(2,1)}) custom-call(s32[1]{0:T(128)} %bitcast.4.z_ref, bf16[8,272,256]{2,1,0:T(8,128)(2,1)} %copy-done.2, bf16[528,256]{1,0:T(8,128)(2,1)} %copy-done.6, ...), custom_call_target="tpu_custom_call" | custom-call | tf_op jit(solution)/shard_map/pallas_call | solution.py:576
  91.6 7.3 %all-to-all-start.2 = ((bf16[8,256,256]{2,1,0:T(8,128)(2,1)}), bf16[8,256,256]{2,1,0:T(8,128)(2,1)S(1)}, u32[]{:S(2)}, u32[]{:S(2)}) async-start(bf16[8,256,256]{2,1,0:T(8,128)(2,1)} %bitcast.7), calls=%async_computation.2 | async-start | bytes 2097152 | tf_op jit(solution)/shard_map/all_to_all | solution.py:512
  98.8 1.3 collective-permute-start.6
  100.1 1.3 collective-permute-start.7
  101.4 1.3 collective-permute-start.9
  102.7 9.7 %collective-permute-done.7 = bf16[528,256]{1,0:T(8,128)(2,1)S(1)} collective-permute-done((bf16[528,256]{1,0:T(8,128)(2,1)}, bf16[528,256]{1,0:T(8,128)(2,1)S(1)}, u32[]{:S(2)}, u32[]{:S(2)}) %collective-permute-start.7) | collective-permute-done | bytes 270368 | tf_op jit(solution)/shard_map/ppermute | solution.py:614
  112.5 1.9 %collective-permute-start.8 = (bf16[528,256]{1,0:T(8,128)(2,1)S(1)}, bf16[528,256]{1,0:T(8,128)(2,1)S(1)}, u32[]{:S(2)}, u32[]{:S(2)}) collective-permute-start(bf16[528,256]{1,0:T(8,128)(2,1)S(1)} %collective-permute-done.7), channel_id=1, source_target_pairs={{0,32},{96,0},{1,33},{97,1},{2,34},{98,2},{3,35},{99,3},{4,36},{10... | collective-permute-start | bytes 811016 | tf_op jit(solution)/shard_map/ppermute | solution.py:616
  114.4 3.8 %collective-permute-done.9.back3_ref = bf16[528,256]{1,0:T(8,128)(2,1)S(1)} collective-permute-done((bf16[528,256]{1,0:T(8,128)(2,1)S(1)}, bf16[528,256]{1,0:T(8,128)(2,1)S(1)}, u32[]{:S(2)}, u32[]{:S(2)}) %collective-permute-start.9) | collective-permute-done | bytes 270368 | tf_op jit(solution)/shard_map/ppermute | solution.py:615
  118.2 3.8 %collective-permute-done.8.back2_ref = bf16[528,256]{1,0:T(8,128)(2,1)S(1)} collective-permute-done((bf16[528,256]{1,0:T(8,128)(2,1)S(1)}, bf16[528,256]{1,0:T(8,128)(2,1)S(1)}, u32[]{:S(2)}, u32[]{:S(2)}) %collective-permute-start.8) | collective-permute-done | bytes 270368 | tf_op jit(solution)/shard_map/ppermute | solution.py:616
  122.0 1.6 copy-done.4
  123.6 1.8 %shard_map.89.refs_0_ = bf16[8,272,256]{2,1,0:T(8,128)(2,1)} custom-call(f32[2048,256]{1,0:T(8,128)S(1)} %copy-done.4, f32[512,256]{1,0:T(8,128)S(1)} %copy-done.5, bf16[1312,256]{1,0:T(8,128)(2,1)S(1)} %collective-permute-done.6.back1_ref, bf16[528,256]{1,0:T(8,128)(2,1)S(1)} %collective-permute-done.8.back2_ref, ...), custom_call_target="tpu_custom_call" | custom-call | tf_op jit(solution)/shard_map/pallas_call | solution.py:618
  125.4 0.0 all-to-all-done.2.attn_ref.pair_ref
  125.4 1.0 copy-done
  126.4 5.6 %shard_map.90 = (bf16[256,1536]{1,0:T(8,128)(2,1)}, bf16[256,1536]{1,0:T(8,128)(2,1)}) custom-call(s32[4]{0:T(128)} %pad_add_fusion.order_ref, bf16[8,256,256]{2,1,0:T(8,128)(2,1)} %copy-done, bf16[768,6144]{1,0:T(8,128)(2,1)} %w_ref.7, bf16[8,272,256]{2,1,0:T(8,128)(2,1)} %shard_map.89.refs_0_), custom_call_target="tpu_custom_call" | custom-call | tf_op jit(solution)/shard_map/pallas_call | solution.py:485
  131.9 0.0 collective-permute-start.10
  131.9 7.4 %all-to-all-start.3 = ((bf16[8,272,256]{2,1,0:T(8,128)(2,1)}), bf16[8,272,256]{2,1,0:T(8,128)(2,1)}, u32[]{:S(2)}, u32[]{:S(2)}) async-start(bf16[8,272,256]{2,1,0:T(8,128)(2,1)} %shard_map.89.refs_0_), calls=%async_computation.3 | async-start | bytes 2228224 | tf_op jit(solution)/shard_map/all_to_all | solution.py:512
  139.3 0.0 collective-permute-done.10
  139.3 0.2 add_convert_fusion.1
  139.5 6.2 %shard_map.91 = (bf16[256,1536]{1,0:T(8,128)(2,1)}, bf16[256,1536]{1,0:T(8,128)(2,1)}) custom-call(s32[4]{0:T(128)} %pad_add_fusion.order_ref, bf16[8,256,256]{2,1,0:T(8,128)(2,1)} %copy-done, bf16[768,6144]{1,0:T(8,128)(2,1)} %w_ref.7, bf16[8,272,256]{2,1,0:T(8,128)(2,1)} %shard_map.89.refs_0_), custom_call_target="tpu_custom_call" | custom-call | tf_op jit(solution)/shard_map/pallas_call | solution.py:485
  145.7 0.0 collective-permute-start.11
  145.7 1.1 collective-permute-start.12
  146.8 8.3 %all-to-all-done.3.x_ref = bf16[8,272,256]{2,1,0:T(8,128)(2,1)} async-done(((bf16[8,272,256]{2,1,0:T(8,128)(2,1)}), bf16[8,272,256]{2,1,0:T(8,128)(2,1)}, u32[]{:S(2)}, u32[]{:S(2)}) %all-to-all-start.3) | async-done | bytes 1114144 | tf_op jit(solution)/shard_map/all_to_all | solution.py:512
  155.2 2.5 %shard_map.92 = (bf16[256,768]{1,0:T(8,128)(2,1)}, bf16[256,768]{1,0:T(8,128)(2,1)}, bf16[256,768]{1,0:T(8,128)(2,1)}) custom-call(bf16[8,256,256]{2,1,0:T(8,128)(2,1)S(1)} %copy-done.1, bf16[8,272,256]{2,1,0:T(8,128)(2,1)} %all-to-all-done.3.x_ref), custom_call_target="tpu_custom_call" | custom-call | tf_op jit(solution)/shard_map/pallas_call | solution.py:631
  157.6 0.0 collective-permute-done.11
  157.6 13.0 %collective-permute-done.12 = bf16[256,1536]{1,0:T(8,128)(2,1)} collective-permute-done((bf16[256,1536]{1,0:T(8,128)(2,1)S(1)}, bf16[256,1536]{1,0:T(8,128)(2,1)}, u32[]{:S(2)}, u32[]{:S(2)}) %collective-permute-start.12) | collective-permute-done | bytes 786464 | tf_op jit(solution)/shard_map/ppermute | solution.py:504
  170.6 2.5 %add_convert_fusion = bf16[256,1536]{1,0:T(8,128)(2,1)} fusion(bf16[256,1536]{1,0:T(8,128)(2,1)} %collective-permute-done.12, bf16[256,1536]{1,0:T(8,128)(2,1)} %collective-permute-done.11, bf16[256,1536]{1,0:T(8,128)(2,1)S(1)} %copy-done.8), kind=kLoop, calls=%fused_computation | loop fusion | flops 2359296 | bytes 3145728 | tf_op jit(solution)/shard_map/convert_element_type | solution.py:538
  (28 shorter events, 0.1 us)
Async XLA Ops:
  0.6 12.2 %collective-permute-start.1 = (bf16[256,1536]{1,0:T(8,128)(2,1)}, bf16[256,1536]{1,0:T(8,128)(2,1)}, u32[]{:S(2)}, u32[]{:S(2)}) collective-permute-start(bf16[256,1536]{1,0:T(8,128)(2,1)} %a_ref.1), channel_id=1, source_target_pairs={{0,1},{1,0},{2,3},{3,2},{4,5},{5,4},{6,7},{7,6},{8,9},{9,8},{10,11... | collective-permute-start | bytes 2359304 | tf_op jit(solution)/shard_map/ppermute | solution.py:504
  0.7 20.6 %collective-permute-start = (bf16[256,1536]{1,0:T(8,128)(2,1)}, bf16[256,1536]{1,0:T(8,128)(2,1)S(1)}, u32[]{:S(2)}, u32[]{:S(2)}) collective-permute-start(bf16[256,1536]{1,0:T(8,128)(2,1)} %a_ref.1), channel_id=1, source_target_pairs={{0,2},{2,0},{1,3},{3,1},{4,6},{6,4},{5,7},{7,5},{8,10},{10,8},{9,1... | collective-permute-start | bytes 2359304 | tf_op jit(solution)/shard_map/ppermute | solution.py:504
  4.7 28.2 %all-to-all-start = ((bf16[8,272,256]{2,1,0:T(8,128)(2,1)}), bf16[8,272,256]{2,1,0:T(8,128)(2,1)S(1)}, u32[]{:S(2)}, u32[]{:S(2)}) async-start(bf16[8,272,256]{2,1,0:T(8,128)(2,1)} %shard_map.84), calls=%async_computation | async-start | bytes 2228224 | tf_op jit(solution)/shard_map/all_to_all | solution.py:512
  21.4 2.4 %copy-start.7 = (bf16[256,1536]{1,0:T(8,128)(2,1)}, bf16[256,1536]{1,0:T(8,128)(2,1)S(1)}, u32[]{:S(2)}) copy-start(bf16[256,1536]{1,0:T(8,128)(2,1)S(1)} %collective-permute-done.a_ref) | copy-start | bytes 2359300
  21.4 2.4 %collective-permute-start.5 = (bf16[256,1536]{1,0:T(8,128)(2,1)S(1)}, bf16[256,1536]{1,0:T(8,128)(2,1)}, u32[]{:S(2)}, u32[]{:S(2)}) collective-permute-start(bf16[256,1536]{1,0:T(8,128)(2,1)S(1)} %collective-permute-done.a_ref), channel_id=1, source_target_pairs={{0,1},{1,0},{2,3},{3,2},{4,5},{5,4},{6,7},{7,6},{8,9},{9,8},{10,11... | collective-permute-start | bytes 2359304 | tf_op jit(solution)/shard_map/ppermute | solution.py:504
  29.7 12.4 %copy-start.3 = (f32[768,256]{1,0:T(8,128)S(1)}, f32[768,256]{1,0:T(8,128)}, u32[]{:S(2)}) copy-start(f32[768,256]{1,0:T(8,128)} %shard_map.85.after_ref.start) | copy-start | bytes 2359300
  32.9 9.5 %copy-start.2 = (bf16[8,272,256]{2,1,0:T(8,128)(2,1)}, bf16[8,272,256]{2,1,0:T(8,128)(2,1)S(1)}, u32[]{:S(2)}) copy-start(bf16[8,272,256]{2,1,0:T(8,128)(2,1)S(1)} %all-to-all-done.x_ref) | copy-start | bytes 3342340
  32.9 32.1 %all-to-all-start.1 = ((bf16[8,256,256]{2,1,0:T(8,128)(2,1)}), bf16[8,256,256]{2,1,0:T(8,128)(2,1)}, u32[]{:S(2)}, u32[]{:S(2)}) async-start(bf16[8,256,256]{2,1,0:T(8,128)(2,1)} %shard_map.87), calls=%async_computation.1 | async-start | bytes 2097152 | tf_op jit(solution)/shard_map/all_to_all | solution.py:512
  42.5 22.5 %copy-start.6 = (bf16[528,256]{1,0:T(8,128)(2,1)}, bf16[528,256]{1,0:T(8,128)(2,1)S(1)}, u32[]{:S(2)}) copy-start(bf16[528,256]{1,0:T(8,128)(2,1)S(1)} %get-tuple-element.24.own_ref) | copy-start | bytes 811012
  42.5 22.5 %collective-permute-start.2 = (bf16[1312,256]{1,0:T(8,128)(2,1)S(1)}, bf16[1312,256]{1,0:T(8,128)(2,1)S(1)}, u32[]{:S(2)}, u32[]{:S(2)}) collective-permute-start(bf16[1312,256]{1,0:T(8,128)(2,1)S(1)} %get-tuple-element.25), channel_id=1, source_target_pairs={{0,32},{32,64},{64,96},{1,33},{33,65},{65,97},{2,34},{34,66},{66,9... | collective-permute-start | bytes 2015240 | tf_op jit(solution)/shard_map/ppermute | solution.py:508
  46.3 9.4 %collective-permute-start.3 = (bf16[528,256]{1,0:T(8,128)(2,1)S(1)}, bf16[528,256]{1,0:T(8,128)(2,1)S(1)}, u32[]{:S(2)}, u32[]{:S(2)}) collective-permute-start(bf16[528,256]{1,0:T(8,128)(2,1)S(1)} %get-tuple-element.24.own_ref), channel_id=1, source_target_pairs={{0,96},{32,0},{1,97},{33,1},{2,98},{34,2},{3,99},{35,3},{4,100},{3... | collective-permute-start | bytes 811016 | tf_op jit(solution)/shard_map/ppermute | solution.py:572
  55.7 9.3 %copy-start.11 = (bf16[528,256]{1,0:T(8,128)(2,1)}, bf16[528,256]{1,0:T(8,128)(2,1)S(1)}, u32[]{:S(2)}) copy-start(bf16[528,256]{1,0:T(8,128)(2,1)S(1)} %collective-permute-done.3.far3_ref) | copy-start | bytes 811012
  55.7 9.3 %collective-permute-start.4 = (bf16[528,256]{1,0:T(8,128)(2,1)S(1)}, bf16[528,256]{1,0:T(8,128)(2,1)S(1)}, u32[]{:S(2)}, u32[]{:S(2)}) collective-permute-start(bf16[528,256]{1,0:T(8,128)(2,1)S(1)} %collective-permute-done.3.far3_ref), channel_id=1, source_target_pairs={{96,64},{0,96},{97,65},{1,97},{98,66},{2,98},{99,67},{3,99},{100,6... | collective-permute-start | bytes 811016 | tf_op jit(solution)/shard_map/ppermute | solution.py:573
  65.0 0.7 copy-start.12
  65.0 0.9 copy-start.10
  91.5 7.3 %copy-start.13 = (bf16[1312,256]{1,0:T(8,128)(2,1)S(1)}, bf16[1312,256]{1,0:T(8,128)(2,1)}, u32[]{:S(2)}) copy-start(bf16[1312,256]{1,0:T(8,128)(2,1)} %get-tuple-element.30) | copy-start | bytes 2015236
  91.6 9.9 %copy-start.14 = (bf16[528,256]{1,0:T(8,128)(2,1)S(1)}, bf16[528,256]{1,0:T(8,128)(2,1)}, u32[]{:S(2)}) copy-start(bf16[528,256]{1,0:T(8,128)(2,1)} %get-tuple-element.32) | copy-start | bytes 811012
  91.6 30.5 %copy-start.5 = (f32[512,256]{1,0:T(8,128)S(1)}, f32[512,256]{1,0:T(8,128)}, u32[]{:S(2)}) copy-start(f32[512,256]{1,0:T(8,128)} %get-tuple-element.29.coarse_ref) | copy-start | bytes 1572868
  91.6 33.8 %all-to-all-start.2 = ((bf16[8,256,256]{2,1,0:T(8,128)(2,1)}), bf16[8,256,256]{2,1,0:T(8,128)(2,1)S(1)}, u32[]{:S(2)}, u32[]{:S(2)}) async-start(bf16[8,256,256]{2,1,0:T(8,128)(2,1)} %bitcast.7), calls=%async_computation.2 | async-start | bytes 2097152 | tf_op jit(solution)/shard_map/all_to_all | solution.py:512
  98.8 23.2 %collective-permute-start.6 = (bf16[1312,256]{1,0:T(8,128)(2,1)S(1)}, bf16[1312,256]{1,0:T(8,128)(2,1)S(1)}, u32[]{:S(2)}, u32[]{:S(2)}) collective-permute-start(bf16[1312,256]{1,0:T(8,128)(2,1)S(1)} %copy-done.13), channel_id=1, source_target_pairs={{32,0},{64,32},{96,64},{33,1},{65,33},{97,65},{34,2},{66,34},{98,6... | collective-permute-start | bytes 2015240 | tf_op jit(solution)/shard_map/ppermute | solution.py:508
  100.1 12.3 %collective-permute-start.7 = (bf16[528,256]{1,0:T(8,128)(2,1)}, bf16[528,256]{1,0:T(8,128)(2,1)S(1)}, u32[]{:S(2)}, u32[]{:S(2)}) collective-permute-start(bf16[528,256]{1,0:T(8,128)(2,1)} %get-tuple-element.31), channel_id=1, source_target_pairs={{96,0},{64,96},{97,1},{65,97},{98,2},{66,98},{99,3},{67,99},{100,4... | collective-permute-start | bytes 811016 | tf_op jit(solution)/shard_map/ppermute | solution.py:614
  101.4 16.8 %collective-permute-start.9 = (bf16[528,256]{1,0:T(8,128)(2,1)S(1)}, bf16[528,256]{1,0:T(8,128)(2,1)S(1)}, u32[]{:S(2)}, u32[]{:S(2)}) collective-permute-start(bf16[528,256]{1,0:T(8,128)(2,1)S(1)} %copy-done.14), channel_id=1, source_target_pairs={{96,0},{97,1},{98,2},{99,3},{100,4},{101,5},{102,6},{103,7},{104,8... | collective-permute-start | bytes 811016 | tf_op jit(solution)/shard_map/ppermute | solution.py:615
  112.5 9.6 %collective-permute-start.8 = (bf16[528,256]{1,0:T(8,128)(2,1)S(1)}, bf16[528,256]{1,0:T(8,128)(2,1)S(1)}, u32[]{:S(2)}, u32[]{:S(2)}) collective-permute-start(bf16[528,256]{1,0:T(8,128)(2,1)S(1)} %collective-permute-done.7), channel_id=1, source_target_pairs={{0,32},{96,0},{1,33},{97,1},{2,34},{98,2},{3,35},{99,3},{4,36},{10... | collective-permute-start | bytes 811016 | tf_op jit(solution)/shard_map/ppermute | solution.py:616
  122.0 1.6 copy-start.4
  125.4 1.0 copy-start
  131.9 7.4 %copy-start.9 = (bf16[256,1536]{1,0:T(8,128)(2,1)S(1)}, bf16[256,1536]{1,0:T(8,128)(2,1)}, u32[]{:S(2)}) copy-start(bf16[256,1536]{1,0:T(8,128)(2,1)} %get-tuple-element.33) | copy-start | bytes 2359300
  131.9 7.4 %collective-permute-start.10 = (bf16[256,1536]{1,0:T(8,128)(2,1)}, bf16[256,1536]{1,0:T(8,128)(2,1)S(1)}, u32[]{:S(2)}, u32[]{:S(2)}) collective-permute-start(bf16[256,1536]{1,0:T(8,128)(2,1)} %get-tuple-element.34), channel_id=1, source_target_pairs={{0,1},{1,0},{2,3},{3,2},{4,5},{5,4},{6,7},{7,6},{8,9},{9,8},{10,11... | collective-permute-start | bytes 2359304 | tf_op jit(solution)/shard_map/ppermute | solution.py:504
  131.9 23.2 %all-to-all-start.3 = ((bf16[8,272,256]{2,1,0:T(8,128)(2,1)}), bf16[8,272,256]{2,1,0:T(8,128)(2,1)}, u32[]{:S(2)}, u32[]{:S(2)}) async-start(bf16[8,272,256]{2,1,0:T(8,128)(2,1)} %shard_map.89.refs_0_), calls=%async_computation.3 | async-start | bytes 2228224 | tf_op jit(solution)/shard_map/all_to_all | solution.py:512
  139.5 15.7 %copy-start.1 = (bf16[8,256,256]{2,1,0:T(8,128)(2,1)S(1)}, bf16[8,256,256]{2,1,0:T(8,128)(2,1)}, u32[]{:S(2)}) copy-start(bf16[8,256,256]{2,1,0:T(8,128)(2,1)} %copy-done) | copy-start | bytes 3145732
  145.7 24.9 %copy-start.8 = (bf16[256,1536]{1,0:T(8,128)(2,1)S(1)}, bf16[256,1536]{1,0:T(8,128)(2,1)}, u32[]{:S(2)}) copy-start(bf16[256,1536]{1,0:T(8,128)(2,1)} %get-tuple-element.36) | copy-start | bytes 2359300
  145.7 11.9 %collective-permute-start.11 = (bf16[256,1536]{1,0:T(8,128)(2,1)}, bf16[256,1536]{1,0:T(8,128)(2,1)}, u32[]{:S(2)}, u32[]{:S(2)}) collective-permute-start(bf16[256,1536]{1,0:T(8,128)(2,1)} %get-tuple-element.37), channel_id=1, source_target_pairs={{0,1},{1,0},{2,3},{3,2},{4,5},{5,4},{6,7},{7,6},{8,9},{9,8},{10,11... | collective-permute-start | bytes 2359304 | tf_op jit(solution)/shard_map/ppermute | solution.py:504
  145.7 24.9 %collective-permute-start.12 = (bf16[256,1536]{1,0:T(8,128)(2,1)S(1)}, bf16[256,1536]{1,0:T(8,128)(2,1)}, u32[]{:S(2)}, u32[]{:S(2)}) collective-permute-start(bf16[256,1536]{1,0:T(8,128)(2,1)S(1)} %add_convert_fusion.1), channel_id=1, source_target_pairs={{0,2},{2,0},{1,3},{3,1},{4,6},{6,4},{5,7},{7,5},{8,10},{10,8},{9,1... | collective-permute-start | bytes 2359304 | tf_op jit(solution)/shard_map/ppermute | solution.py:504

commit v2 on v1

--- a/solution.py
+++ b/solution.py
@@ -118,6 +118,75 @@
     return jnp.where(iota(head.shape, 0) == 0, head + lacking, head).astype(bf16)
 
 
+def transposed(ref, out, count):
+    def body(i, carry):
+        at = pl.multiple_of(i * BLOCK, BLOCK)
+        out[:, pl.ds(at, BLOCK)] = ref[pl.ds(at, BLOCK), :].T
+        return carry
+
+    lax.fori_loop(0, count, body, 0)
+
+
+def weights(scores, biases, factor):
+    tops = [jnp.max(s, 0, keepdims=True) + b for s, b in zip(scores, biases)]
+    top = functools.reduce(jnp.maximum, tops)
+    exps = [jnp.exp2((s - (top - b)) * factor) for s, b in zip(scores, biases)]
+    total = functools.reduce(jnp.add, [jnp.sum(e, 0, keepdims=True) for e in exps])
+    inverse = 1.0 / total
+    return jnp.concatenate([e * inverse for e in exps], 0)
+
+
+def window_block(at, query, grad, biases, kx, vx, kxt, vxt, dk, dv):
+    span = WINDOW + BLOCK
+    reach = WINDOW // BLOCK
+    row_at, col_at = iota((BLOCK, BLOCK), 0), iota((BLOCK, BLOCK), 1)
+    scores = []
+    for piece in range(reach + 1):
+        s = dot_nt(kx[pl.ds(pl.multiple_of(at + piece * BLOCK, BLOCK), BLOCK), :], query)
+        if piece == 0:
+            s = jnp.where(row_at > col_at, s, FAR)
+        if piece == reach:
+            s = jnp.where(row_at <= col_at, s, FAR)
+        scores.append(s)
+    probs = weights(scores, biases, SCALE * LOG2E)
+    rounded = probs.astype(bf16)
+    out_t = dot(vxt[:, pl.ds(at, span)], rounded)
+    delta = jnp.sum(grad.astype(f32).T * out_t, 0, keepdims=True)
+    grad_probs = dot_nt(vx[pl.ds(at, span), :], grad)
+    grad_scores = (probs * (grad_probs - delta)).astype(bf16)
+    dk[pl.ds(at, span), :] += dot(grad_scores, query)
+    dv[pl.ds(at, span), :] += dot(rounded, grad)
+    return out_t, dot(kxt[:, pl.ds(at, span)], grad_scores).T * SCALE
+
+
+def own_kernel(x_ref, pair_ref, part_ref, sums_ref, kx, vx, kxt, vxt, dk, dv):
+    rows = pair_ref.shape[0]
+    tokens = rows // PLANE_DEVS
+    for slot in range(PLANE_DEVS):
+        at = slot * tokens
+        kx[at : at + tokens, :] = x_ref[slot, 0:tokens, 0:128]
+        vx[at : at + tokens, :] = x_ref[slot, 0:tokens, 128:256]
+    transposed(kx, kxt, rows // BLOCK)
+    transposed(vx, vxt, rows // BLOCK)
+    dk[...] = jnp.zeros_like(dk)
+    dv[...] = jnp.zeros_like(dv)
+
+    def body(block, carry):
+        at = pl.multiple_of(block * BLOCK, BLOCK)
+        own = pl.ds(pl.multiple_of(WINDOW + at, BLOCK), BLOCK)
+        biases = [0.0] * (WINDOW // BLOCK + 1)
+        out_t, query_grad = window_block(
+            at, pair_ref[own, 0:128], pair_ref[own, 128:256], biases, kx, vx, kxt, vxt, dk, dv
+        )
+        part_ref[pl.ds(at, BLOCK), 0:128] = out_t.T
+        part_ref[pl.ds(at, BLOCK), 128:256] = query_grad
+        return carry
+
+    lax.fori_loop(0, (rows - WINDOW) // BLOCK, body, 0, unroll=4)
+    sums_ref[:, 0:128] = dk[...] * SCALE
+    sums_ref[:, 128:256] = dv[...]
+
+
 def attention_kernel(
     z_ref,
     x_ref,
@@ -126,6 +195,7 @@
     far2_ref,
     far3_ref,
     pair_ref,
+    part_ref,
     attn_ref,
     fine_ref,
     coarse_ref,
@@ -159,26 +229,17 @@
     coarse = rows // SHORT
     half = WINDOW // SHORT
     step = BLOCK // SHORT
-    span = WINDOW + BLOCK
     reach = WINDOW // BLOCK
 
     kx[0:WINDOW, :] = near_ref[0:WINDOW, 0:128]
     vx[0:WINDOW, :] = near_ref[0:WINDOW, 128:256]
-    for slot in range(PLANE_DEVS):
+    for slot in range((rows - WINDOW) // tokens):
         at = WINDOW + slot * tokens
         kx[at : at + tokens, :] = x_ref[slot, 0:tokens, 0:128]
         vx[at : at + tokens, :] = x_ref[slot, 0:tokens, 128:256]
 
-    def transposed(ref, out, count):
-        def body(i, carry):
-            at = pl.multiple_of(i * BLOCK, BLOCK)
-            out[:, pl.ds(at, BLOCK)] = ref[pl.ds(at, BLOCK), :].T
-            return carry
-
-        lax.fori_loop(0, count, body, 0)
-
-    transposed(kx, kxt, (WINDOW + rows) // BLOCK)
-    transposed(vx, vxt, (WINDOW + rows) // BLOCK)
+    transposed(kx, kxt, rows // BLOCK)
+    transposed(vx, vxt, rows // BLOCK)
 
     tails = [
         near_ref[WINDOW - TAIL : WINDOW, :],
@@ -215,14 +276,6 @@
         gp[block * step : (block + 1) * step, :] = dot(
             taken, pair_ref[at : at + BLOCK, 128:256]
         ).astype(bf16)
-
-    def weights(scores, biases, factor):
-        tops = [jnp.max(s, 0, keepdims=True) + b for s, b in zip(scores, biases)]
-        top = functools.reduce(jnp.maximum, tops)
-        exps = [jnp.exp2((s - (top - b)) * factor) for s, b in zip(scores, biases)]
-        total = functools.reduce(jnp.add, [jnp.sum(e, 0, keepdims=True) for e in exps])
-        inverse = 1.0 / total
-        return jnp.concatenate([e * inverse for e in exps], 0)
 
     row_at, col_at = iota((BLOCK, BLOCK), 0), iota((BLOCK, BLOCK), 1)
     diagonal = row_at <= col_at
@@ -275,43 +328,33 @@
     dkx[...] = jnp.zeros_like(dkx)
     dvx[...] = jnp.zeros_like(dvx)
 
-    def window(block, carry):
-        at = pl.multiple_of(block * BLOCK, BLOCK)
-        query = pair_ref[pl.ds(at, BLOCK), 0:128]
-        grad = pair_ref[pl.ds(at, BLOCK), 128:256]
-        scores, biases = [], []
-        for piece in range(reach + 1):
-            key = kx[pl.ds(pl.multiple_of(at + piece * BLOCK, BLOCK), BLOCK), :]
-            s = dot_nt(key, query)
-            if piece == 0:
-                s = jnp.where(row_at > col_at, s, FAR)
-            if piece == reach:
-                s = jnp.where(diagonal, s, FAR)
-            scores.append(s)
-            biases.append(jnp.where((z == 0) & (block + piece < reach), FAR, 0.0))
-        probs = weights(scores, biases, SCALE * LOG2E)
-        rounded = probs.astype(bf16)
-        out_t = dot(vxt[:, pl.ds(at, span)], rounded)
-        grad_t = grad.astype(f32).T
-        delta = jnp.sum(grad_t * out_t, 0, keepdims=True)
+    def short_out(block):
         pair = pl.multiple_of(block // 2 * (2 * step), 2 * step)
         shape = (2 * step, BLOCK)
         spread = ones_where(iota(shape, 0) == block % 2 * step + iota(shape, 1) // SHORT)
         short_t = dot(high_t[:, pl.ds(pair, 2 * step)], spread)
-        short_t += dot(low_t[:, pl.ds(pair, 2 * step)], spread)
-        attn_ref[pl.ds(at, BLOCK), 0:128] = (out_t + short_t).T.astype(bf16)
-        grad_probs = dot_nt(vx[pl.ds(at, span), :], grad)
-        grad_scores = (probs * (grad_probs - delta)).astype(bf16)
-        query_grad = dot(kxt[:, pl.ds(at, span)], grad_scores).T * SCALE
+        return short_t + dot(low_t[:, pl.ds(pair, 2 * step)], spread)
+
+    def short_query_grad(block):
         below = pl.ds(pl.multiple_of(block * step, step), step + TAIL)
         spread = dot(spreading(), query_high[below, :]) + dot(spreading(), query_low[below, :])
-        query_grad += spread * (1.0 / SHORT)
-        attn_ref[pl.ds(at, BLOCK), 128:256] = query_grad.astype(bf16)
-        dkx[pl.ds(at, span), :] += dot(grad_scores, query)
-        dvx[pl.ds(at, span), :] += dot(rounded, grad)
+        return spread * (1.0 / SHORT)
+
+    def window(block, carry):
+        at = pl.multiple_of(block * BLOCK, BLOCK)
+        here = pl.ds(at, BLOCK)
+        biases = [jnp.where((z == 0) & (block + piece < reach), FAR, 0.0) for piece in range(reach + 1)]
+        out_t, query_grad = window_block(
+            at, pair_ref[here, 0:128], pair_ref[here, 128:256], biases, kx, vx, kxt, vxt, dkx, dvx
+        )
+        attn_ref[here, 0:128] = (out_t + short_out(block)).T.astype(bf16)
+        attn_ref[here, 128:256] = (query_grad + short_query_grad(block)).astype(bf16)
+        late = pl.ds(pl.multiple_of(WINDOW + at, BLOCK), BLOCK)
+        attn_ref[late, 0:128] = (part_ref[here, 0:128] + short_out(block + reach).T).astype(bf16)
+        attn_ref[late, 128:256] = (part_ref[here, 128:256] + short_query_grad(block + reach)).astype(bf16)
         return carry
 
-    lax.fori_loop(0, rows // BLOCK, window, 0, unroll=8)
+    lax.fori_loop(0, reach, window, 0, unroll=4)
     fine_ref[:, 0:128] = dkx[WINDOW:, :] * SCALE
     fine_ref[:, 128:256] = dvx[WINDOW:, :]
 
@@ -347,8 +390,10 @@
             ref[coarse : coarse + TAIL, cols] = row.astype(bf16)
 
 
-def finish_kernel(fine_ref, coarse_ref, back1_ref, back2_ref, back3_ref, out_ref, high, low):
-    rows = fine_ref.shape[0]
+def finish_kernel(
+    sums_ref, fine_ref, coarse_ref, back1_ref, back2_ref, back3_ref, out_ref, high, low
+):
+    rows = sums_ref.shape[0]
     tokens = rows // PLANE_DEVS
     coarse = rows // SHORT
     half = coarse - WINDOW // SHORT
@@ -371,8 +416,10 @@
         below = block * step if late < 0 else part + late // SHORT
         spread = dot(taken, high[below : below + step + TAIL, :])
         spread += dot(taken, low[below : below + step + TAIL, :])
-        result = fine_ref[at : at + BLOCK, :] + spread * (1.0 / SHORT)
-        if late >= 0:
+        result = sums_ref[at : at + BLOCK, :] + spread * (1.0 / SHORT)
+        if late < 0:
+            result = result + fine_ref[at : at + BLOCK, :]
+        else:
             result = result + back1_ref[late : late + BLOCK, :].astype(f32)
         out_ref[block, 0:tokens, :] = result.astype(bf16)
         out_ref[block, tokens:, :] = jnp.zeros((TAIL, 256), bf16)
@@ -573,32 +620,42 @@
     far2_in = lax.ppermute(far3_in, "z", [(3, 2), (0, 3)])
     pair = in_plane(pair_packed).reshape(rows, 2 * HEAD_DIM)
 
+    part, sums = call(
+        own_kernel,
+        (array(rows - WINDOW, 256, dtype=f32), array(rows, 256, dtype=f32)),
+        56,
+        in_specs=[whole] * 2,
+        out_specs=[whole] * 2,
+        scratch_shapes=[pltpu.VMEM((rows, HEAD_DIM), bf16)] * 2
+        + [pltpu.VMEM((HEAD_DIM, rows), bf16)] * 2
+        + [pltpu.VMEM((rows, HEAD_DIM), f32)] * 2,
+    )(own, pair)
     attn, fine, short, back1, back2, back3 = call(
         attention_kernel,
         (
             array(rows, 256),
-            array(rows, 256, dtype=f32),
+            array(rows - WINDOW, 256, dtype=f32),
             array(coarse, 256, dtype=f32),
             array(near_rows, 256),
             array(coarse + TAIL, 256),
             array(coarse + TAIL, 256),
         ),
         62,
-        in_specs=[pl.BlockSpec(memory_space=pltpu.SMEM)] + [whole] * 6,
+        in_specs=[pl.BlockSpec(memory_space=pltpu.SMEM)] + [whole] * 7,
         out_specs=[whole] * 6,
         scratch_shapes=[
-            pltpu.VMEM((WINDOW + rows, HEAD_DIM), bf16),
-            pltpu.VMEM((WINDOW + rows, HEAD_DIM), bf16),
-            pltpu.VMEM((HEAD_DIM, WINDOW + rows), bf16),
-            pltpu.VMEM((HEAD_DIM, WINDOW + rows), bf16),
+            pltpu.VMEM((rows, HEAD_DIM), bf16),
+            pltpu.VMEM((rows, HEAD_DIM), bf16),
+            pltpu.VMEM((HEAD_DIM, rows), bf16),
+            pltpu.VMEM((HEAD_DIM, rows), bf16),
             pltpu.VMEM((total, HEAD_DIM), bf16),
             pltpu.VMEM((total, HEAD_DIM), bf16),
             pltpu.VMEM((HEAD_DIM, total), bf16),
             pltpu.VMEM((HEAD_DIM, total), bf16),
             pltpu.VMEM((coarse, HEAD_DIM), bf16),
             pltpu.VMEM((coarse, HEAD_DIM), bf16),
-            pltpu.VMEM((WINDOW + rows, HEAD_DIM), f32),
-            pltpu.VMEM((WINDOW + rows, HEAD_DIM), f32),
+            pltpu.VMEM((rows, HEAD_DIM), f32),
+            pltpu.VMEM((rows, HEAD_DIM), f32),
             pltpu.VMEM((total, HEAD_DIM), f32),
             pltpu.VMEM((total, HEAD_DIM), f32),
             pltpu.VMEM((HEAD_DIM, coarse), bf16),
@@ -608,7 +665,7 @@
             pltpu.VMEM((coarse + TAIL, HEAD_DIM), bf16),
             pltpu.VMEM((coarse + TAIL, HEAD_DIM), bf16),
         ],
-    )(z, own, far, near_in, far2_in, far3_in, pair)
+    )(z, own, far, near_in, far2_in, far3_in, pair, part)
 
     back1_in = planes_up(back1, -1)
     halfway = lax.ppermute(back2, "z", [(3, 0), (2, 3)])
@@ -623,7 +680,7 @@
             pltpu.VMEM((coarse + 2 * TAIL, 256), bf16),
             pltpu.VMEM((coarse + 2 * TAIL, 256), bf16),
         ],
-    )(fine, short, back1_in, back2_in, back3_in)
+    )(sums, fine, short, back1_in, back2_in, back3_in)
     mixed_out = projected(
         attn_in, out_weight, out_grad.shape[1], blocks, (finished,)
     )

time: 174 us -> 173 us (level)
  waiting for transfers between devices: 58 us -> 53.5 us
  Pallas kernels: 55.9 us -> 59.1 us
    ppermute x1, waiting for transfers between devices: 4.41 us -> 0.01 us  [shards(): far2_in = lax.ppermute(far3_in, 'z', [(3, 2), (0, 3)])]
    pallas_call x1 -> x2, Pallas kernels: 25.6 us -> 28.6 us  [the longest x1 18.2 us: shards(): call(attention_kernel, (array(rows, 256), array(rows - WINDOW, 256, dtype...]
  transfers between devices with their start and end apart: 17 -> 17, of which waited for: 10 -> 9; matrix products, arithmetic and copies ran while one was open for 0% -> 0% of each run, Pallas kernels for 14% -> 20%
where the time goes in v2:
time: 173 us; the launch traced here: 172 us
  Pallas kernels  59.1 us (34%)
  waiting for transfers between devices  53.5 us (31%)
  starting transfers between devices  51.6 us (30%)
  local copies, waits for them, and re-layouts  3.49 us (2%)
  other arithmetic  3.34 us (2%)
    all_to_all x4, starting transfers between devices, in_plane(): return lax.all_to_all(x, PLANE, 0, 0, tiled=True)  31.3 us
    ppermute x6, waiting for transfers between devices, swap(): return lax.ppermute(x, axis, [(0, 1), (1, 0)])  18.7 us
    pallas_call x1, Pallas kernels, shards(): call(attention_kernel, (array(rows, 256), array(rows - WINDOW, 256, dtype...  18.2 us
    pallas_call x2, Pallas kernels, project(): pl.pallas_call(functools.partial(project_kernel, halves), out_shape=(out,...  12 us
    all_to_all x4, waiting for transfers between devices, in_plane(): return lax.all_to_all(x, PLANE, 0, 0, tiled=True)  11.7 us
    pallas_call x2, Pallas kernels, grad_part(): pl.pallas_call(functools.partial(grad_far_kernel if rest else grad_near_k...  11.2 us
    pallas_call x1, Pallas kernels, shards(): call(own_kernel, (array(rows - WINDOW, 256, dtype=f32), array(rows, 256,...  10.4 us
    ppermute x1, waiting for transfers between devices, shards(): halfway = lax.ppermute(back2, 'z', [(3, 0), (2, 3)])  9.58 us
  transfers between devices with their start and end apart: 17, of which 9 were waited for; matrix products, arithmetic and copies ran while one was open for 0% of the time, Pallas kernels for 20%

profile of v2, /device:TPU:4, one launch (start us, length us, event | category | flops | bytes accessed | tf_op | source)
XLA Modules:
  0.0 171.8 jit_solution(12937588512431171754)
XLA Ops:
  0.6 0.1 collective-permute-start.1
  0.7 1.3 collective-permute-start
  2.0 2.7 %shard_map.84 = bf16[8,272,256]{2,1,0:T(8,128)(2,1)} custom-call(bf16[256,768]{1,0:T(8,128)(2,1)} %q_ref.3, bf16[256,768]{1,0:T(8,128)(2,1)} %k_ref.1, bf16[256,768]{1,0:T(8,128)(2,1)} %v_ref.1), custom_call_target="tpu_custom_call" | custom-call | tf_op jit(solution)/shard_map/pallas_call | solution.py:600
  4.7 7.4 %all-to-all-start = ((bf16[8,272,256]{2,1,0:T(8,128)(2,1)}), bf16[8,272,256]{2,1,0:T(8,128)(2,1)S(1)}, u32[]{:S(2)}, u32[]{:S(2)}) async-start(bf16[8,272,256]{2,1,0:T(8,128)(2,1)} %shard_map.84), calls=%async_computation | async-start | bytes 2228224 | tf_op jit(solution)/shard_map/all_to_all | solution.py:559
  12.1 0.6 pad_add_fusion.order_ref
  12.7 5.3 %shard_map.85.after_ref.start = f32[768,256]{1,0:T(8,128)} custom-call(s32[4]{0:T(128)} %pad_add_fusion.order_ref, bf16[256,1536]{1,0:T(8,128)(2,1)} %a_ref.1, bf16[256,1536]{1,0:T(8,128)(2,1)} %collective-permute-done.1.b_ref, bf16[768,6144]{1,0:T(8,128)(2,1)} %w_ref.7), custom_call_target="tpu_custom_call" | custom-call | tf_op jit(solution)/shard_map/pallas_call | solution.py:487
  18.0 3.3 %collective-permute-done.a_ref = bf16[256,1536]{1,0:T(8,128)(2,1)S(1)} collective-permute-done((bf16[256,1536]{1,0:T(8,128)(2,1)}, bf16[256,1536]{1,0:T(8,128)(2,1)S(1)}, u32[]{:S(2)}, u32[]{:S(2)}) %collective-permute-start) | collective-permute-done | bytes 786464 | tf_op jit(solution)/shard_map/ppermute | solution.py:551
  21.4 0.0 collective-permute-start.5
  21.4 2.4 %collective-permute-done.5.b_ref = bf16[256,1536]{1,0:T(8,128)(2,1)} collective-permute-done((bf16[256,1536]{1,0:T(8,128)(2,1)S(1)}, bf16[256,1536]{1,0:T(8,128)(2,1)}, u32[]{:S(2)}, u32[]{:S(2)}) %collective-permute-start.5) | collective-permute-done | bytes 786464 | tf_op jit(solution)/shard_map/ppermute | solution.py:551
  23.8 5.9 %shard_map.87 = bf16[8,256,256]{2,1,0:T(8,128)(2,1)} custom-call(s32[4]{0:T(128)} %pad_add_fusion.order_ref, bf16[256,1536]{1,0:T(8,128)(2,1)} %copy-done.8, bf16[256,1536]{1,0:T(8,128)(2,1)} %collective-permute-done.5.b_ref, bf16[768,6144]{1,0:T(8,128)(2,1)} %w_ref.7, f32[768,256]{1,0:T(8,128)} %shard_map.85.after_ref.start, bf16[256,768]{1,0:T(8,128)(2,1)} %q_ref.3), custom_call_target="tpu_custom_call" | custom-call | tf_op jit(solution)/shard_map/pallas_call | solution.py:487
  29.7 3.2 %all-to-all-done.x_ref = bf16[8,272,256]{2,1,0:T(8,128)(2,1)S(1)} async-done(((bf16[8,272,256]{2,1,0:T(8,128)(2,1)}), bf16[8,272,256]{2,1,0:T(8,128)(2,1)S(1)}, u32[]{:S(2)}, u32[]{:S(2)}) %all-to-all-start) | async-done | bytes 1114144 | tf_op jit(solution)/shard_map/all_to_all | solution.py:559
  32.9 9.2 %all-to-all-start.1 = ((bf16[8,256,256]{2,1,0:T(8,128)(2,1)}), bf16[8,256,256]{2,1,0:T(8,128)(2,1)}, u32[]{:S(2)}, u32[]{:S(2)}) async-start(bf16[8,256,256]{2,1,0:T(8,128)(2,1)} %shard_map.87), calls=%async_computation.1 | async-start | bytes 2097152 | tf_op jit(solution)/shard_map/all_to_all | solution.py:559
  42.1 0.3 shard_map.86
  42.5 0.0 copy-start.7
  42.5 3.9 %collective-permute-start.2 = (bf16[1312,256]{1,0:T(8,128)(2,1)S(1)}, bf16[1312,256]{1,0:T(8,128)(2,1)S(1)}, u32[]{:S(2)}, u32[]{:S(2)}) collective-permute-start(bf16[1312,256]{1,0:T(8,128)(2,1)S(1)} %get-tuple-element.27), channel_id=1, source_target_pairs={{0,32},{32,64},{64,96},{1,33},{33,65},{65,97},{2,34},{34,66},{66,9... | collective-permute-start | bytes 2015240 | tf_op jit(solution)/shard_map/ppermute | solution.py:555
  46.3 3.4 %collective-permute-start.3 = (bf16[528,256]{1,0:T(8,128)(2,1)S(1)}, bf16[528,256]{1,0:T(8,128)(2,1)S(1)}, u32[]{:S(2)}, u32[]{:S(2)}) collective-permute-start(bf16[528,256]{1,0:T(8,128)(2,1)S(1)} %get-tuple-element.26.own_ref), channel_id=1, source_target_pairs={{0,96},{32,0},{1,97},{33,1},{2,98},{34,2},{3,99},{35,3},{4,100},{3... | collective-permute-start | bytes 811016 | tf_op jit(solution)/shard_map/ppermute | solution.py:619
  49.7 6.0 %collective-permute-done.3.far3_ref = bf16[528,256]{1,0:T(8,128)(2,1)S(1)} collective-permute-done((bf16[528,256]{1,0:T(8,128)(2,1)S(1)}, bf16[528,256]{1,0:T(8,128)(2,1)S(1)}, u32[]{:S(2)}, u32[]{:S(2)}) %collective-permute-start.3) | collective-permute-done | bytes 270368 | tf_op jit(solution)/shard_map/ppermute | solution.py:619
  55.7 4.9 %collective-permute-start.4 = (bf16[528,256]{1,0:T(8,128)(2,1)S(1)}, bf16[528,256]{1,0:T(8,128)(2,1)S(1)}, u32[]{:S(2)}, u32[]{:S(2)}) collective-permute-start(bf16[528,256]{1,0:T(8,128)(2,1)S(1)} %collective-permute-done.3.far3_ref), channel_id=1, source_target_pairs={{96,64},{0,96},{97,65},{1,97},{98,66},{2,98},{99,67},{3,99},{100,6... | collective-permute-start | bytes 811016 | tf_op jit(solution)/shard_map/ppermute | solution.py:620
  60.6 0.0 all-to-all-done.1
  60.6 10.4 %shard_map.88 = (f32[1024,256]{1,0:T(8,128)}, f32[2048,256]{1,0:T(8,128)}) custom-call(bf16[8,272,256]{2,1,0:T(8,128)(2,1)} %copy-done, bf16[2048,256]{1,0:T(8,128)(2,1)} %bitcast.5.pair_ref), custom_call_target="tpu_custom_call" | custom-call | tf_op jit(solution)/shard_map/pallas_call | solution.py:623
  71.0 0.0 collective-permute-done.4.far2_ref
  71.0 0.0 collective-permute-done.2.near_ref
  71.0 0.0 copy-start.11
  71.0 0.7 copy-done.13
  71.7 0.2 copy-done.11
  71.9 18.2 %shard_map.89 = (bf16[2048,256]{1,0:T(8,128)(2,1)}, f32[1024,256]{1,0:T(8,128)}, f32[512,256]{1,0:T(8,128)}, bf16[1312,256]{1,0:T(8,128)(2,1)}, bf16[528,256]{1,0:T(8,128)(2,1)}, /*index=5*/bf16[528,256]{1,0:T(8,128)(2,1)}) custom-call(s32[1]{0:T(128)} %bitcast.4.z_ref, bf16[8,272,256]{2,1,0:T(8,128)(2,1)} %copy-done, bf16[528,256]{1,0:T(8,128)(2,1)} %copy-done.7, ...), custom_call_target="tpu_custom_call" | custom-call | tf_op jit(solution)/shard_map/pallas_call | solution.py:633
  90.2 7.4 %all-to-all-start.2 = ((bf16[8,256,256]{2,1,0:T(8,128)(2,1)}), bf16[8,256,256]{2,1,0:T(8,128)(2,1)S(1)}, u32[]{:S(2)}, u32[]{:S(2)}) async-start(bf16[8,256,256]{2,1,0:T(8,128)(2,1)} %bitcast.7), calls=%async_computation.2 | async-start | bytes 2097152 | tf_op jit(solution)/shard_map/all_to_all | solution.py:559
  97.5 1.3 collective-permute-start.6
  98.8 1.3 collective-permute-start.7
  100.1 1.3 collective-permute-start.9
  101.4 9.6 %collective-permute-done.7 = bf16[528,256]{1,0:T(8,128)(2,1)S(1)} collective-permute-done((bf16[528,256]{1,0:T(8,128)(2,1)}, bf16[528,256]{1,0:T(8,128)(2,1)S(1)}, u32[]{:S(2)}, u32[]{:S(2)}) %collective-permute-start.7) | collective-permute-done | bytes 270368 | tf_op jit(solution)/shard_map/ppermute | solution.py:671
  111.0 1.9 %collective-permute-start.8 = (bf16[528,256]{1,0:T(8,128)(2,1)S(1)}, bf16[528,256]{1,0:T(8,128)(2,1)S(1)}, u32[]{:S(2)}, u32[]{:S(2)}) collective-permute-start(bf16[528,256]{1,0:T(8,128)(2,1)S(1)} %collective-permute-done.7), channel_id=1, source_target_pairs={{0,32},{96,0},{1,33},{97,1},{2,34},{98,2},{3,35},{99,3},{4,36},{10... | collective-permute-start | bytes 811016 | tf_op jit(solution)/shard_map/ppermute | solution.py:673
  112.9 3.8 %collective-permute-done.9.back3_ref = bf16[528,256]{1,0:T(8,128)(2,1)S(1)} collective-permute-done((bf16[528,256]{1,0:T(8,128)(2,1)S(1)}, bf16[528,256]{1,0:T(8,128)(2,1)S(1)}, u32[]{:S(2)}, u32[]{:S(2)}) %collective-permute-start.9) | collective-permute-done | bytes 270368 | tf_op jit(solution)/shard_map/ppermute | solution.py:672
  116.7 3.8 %collective-permute-done.8.back2_ref = bf16[528,256]{1,0:T(8,128)(2,1)S(1)} collective-permute-done((bf16[528,256]{1,0:T(8,128)(2,1)S(1)}, bf16[528,256]{1,0:T(8,128)(2,1)S(1)}, u32[]{:S(2)}, u32[]{:S(2)}) %collective-permute-start.8) | collective-permute-done | bytes 270368 | tf_op jit(solution)/shard_map/ppermute | solution.py:673
  120.6 1.6 copy-done.4
  122.2 1.8 %shard_map.90.refs_0_ = bf16[8,272,256]{2,1,0:T(8,128)(2,1)} custom-call(f32[2048,256]{1,0:T(8,128)S(1)} %copy-done.4, f32[1024,256]{1,0:T(8,128)S(1)} %copy-done.5, f32[512,256]{1,0:T(8,128)S(1)} %copy-done.6, bf16[1312,256]{1,0:T(8,128)(2,1)S(1)} %collective-permute-done.6.back1_ref, bf16[528,256]{1,0:T(8,128)(2,1)S(1)} %collective-permute-done.8.back2_ref, ...), custom_call_target="tpu_custom_call" | custom-call | tf_op jit(solution)/shard_map/pallas_call | solution.py:675
  124.0 0.0 all-to-all-done.2.attn_ref.pair_ref
  124.0 1.0 copy-done.1
  124.9 5.8 %shard_map.91 = (bf16[256,1536]{1,0:T(8,128)(2,1)}, bf16[256,1536]{1,0:T(8,128)(2,1)}) custom-call(s32[4]{0:T(128)} %pad_add_fusion.order_ref, bf16[8,256,256]{2,1,0:T(8,128)(2,1)} %copy-done.1, bf16[768,6144]{1,0:T(8,128)(2,1)} %w_ref.7, bf16[8,272,256]{2,1,0:T(8,128)(2,1)} %shard_map.90.refs_0_), custom_call_target="tpu_custom_call" | custom-call | tf_op jit(solution)/shard_map/pallas_call | solution.py:532
  130.7 0.0 collective-permute-start.10
  130.7 7.4 %all-to-all-start.3 = ((bf16[8,272,256]{2,1,0:T(8,128)(2,1)}), bf16[8,272,256]{2,1,0:T(8,128)(2,1)}, u32[]{:S(2)}, u32[]{:S(2)}) async-start(bf16[8,272,256]{2,1,0:T(8,128)(2,1)} %shard_map.90.refs_0_), calls=%async_computation.3 | async-start | bytes 2228224 | tf_op jit(solution)/shard_map/all_to_all | solution.py:559
  138.1 0.2 add_convert_fusion.1
  138.3 6.2 %shard_map.92 = (bf16[256,1536]{1,0:T(8,128)(2,1)}, bf16[256,1536]{1,0:T(8,128)(2,1)}) custom-call(s32[4]{0:T(128)} %pad_add_fusion.order_ref, bf16[8,256,256]{2,1,0:T(8,128)(2,1)} %copy-done.1, bf16[768,6144]{1,0:T(8,128)(2,1)} %w_ref.7, bf16[8,272,256]{2,1,0:T(8,128)(2,1)} %shard_map.90.refs_0_), custom_call_target="tpu_custom_call" | custom-call | tf_op jit(solution)/shard_map/pallas_call | solution.py:532
  144.5 1.0 collective-permute-start.12
  145.5 8.4 %all-to-all-done.3.x_ref = bf16[8,272,256]{2,1,0:T(8,128)(2,1)} async-done(((bf16[8,272,256]{2,1,0:T(8,128)(2,1)}), bf16[8,272,256]{2,1,0:T(8,128)(2,1)}, u32[]{:S(2)}, u32[]{:S(2)}) %all-to-all-start.3) | async-done | bytes 1114144 | tf_op jit(solution)/shard_map/all_to_all | solution.py:559
  153.9 2.5 %shard_map.93 = (bf16[256,768]{1,0:T(8,128)(2,1)}, bf16[256,768]{1,0:T(8,128)(2,1)}, bf16[256,768]{1,0:T(8,128)(2,1)}) custom-call(bf16[8,256,256]{2,1,0:T(8,128)(2,1)S(1)} %copy-done.2, bf16[8,272,256]{2,1,0:T(8,128)(2,1)} %all-to-all-done.3.x_ref), custom_call_target="tpu_custom_call" | custom-call | tf_op jit(solution)/shard_map/pallas_call | solution.py:688
  156.4 12.9 %collective-permute-done.12 = bf16[256,1536]{1,0:T(8,128)(2,1)} collective-permute-done((bf16[256,1536]{1,0:T(8,128)(2,1)S(1)}, bf16[256,1536]{1,0:T(8,128)(2,1)}, u32[]{:S(2)}, u32[]{:S(2)}) %collective-permute-start.12) | collective-permute-done | bytes 786464 | tf_op jit(solution)/shard_map/ppermute | solution.py:551
  169.3 2.5 %add_convert_fusion = bf16[256,1536]{1,0:T(8,128)(2,1)} fusion(bf16[256,1536]{1,0:T(8,128)(2,1)} %collective-permute-done.12, bf16[256,1536]{1,0:T(8,128)(2,1)} %collective-permute-done.11, bf16[256,1536]{1,0:T(8,128)(2,1)S(1)} %copy-done.9), kind=kLoop, calls=%fused_computation | loop fusion | flops 2359296 | bytes 3145728 | tf_op jit(solution)/shard_map/convert_element_type | solution.py:585
  (29 shorter events, 0.1 us)
Async XLA Ops:
  0.6 12.1 %collective-permute-start.1 = (bf16[256,1536]{1,0:T(8,128)(2,1)}, bf16[256,1536]{1,0:T(8,128)(2,1)}, u32[]{:S(2)}, u32[]{:S(2)}) collective-permute-start(bf16[256,1536]{1,0:T(8,128)(2,1)} %a_ref.1), channel_id=1, source_target_pairs={{0,1},{1,0},{2,3},{3,2},{4,5},{5,4},{6,7},{7,6},{8,9},{9,8},{10,11... | collective-permute-start | bytes 2359304 | tf_op jit(solution)/shard_map/ppermute | solution.py:551
  0.7 20.6 %collective-permute-start = (bf16[256,1536]{1,0:T(8,128)(2,1)}, bf16[256,1536]{1,0:T(8,128)(2,1)S(1)}, u32[]{:S(2)}, u32[]{:S(2)}) collective-permute-start(bf16[256,1536]{1,0:T(8,128)(2,1)} %a_ref.1), channel_id=1, source_target_pairs={{0,2},{2,0},{1,3},{3,1},{4,6},{6,4},{5,7},{7,5},{8,10},{10,8},{9,1... | collective-permute-start | bytes 2359304 | tf_op jit(solution)/shard_map/ppermute | solution.py:551
  4.7 28.2 %all-to-all-start = ((bf16[8,272,256]{2,1,0:T(8,128)(2,1)}), bf16[8,272,256]{2,1,0:T(8,128)(2,1)S(1)}, u32[]{:S(2)}, u32[]{:S(2)}) async-start(bf16[8,272,256]{2,1,0:T(8,128)(2,1)} %shard_map.84), calls=%async_computation | async-start | bytes 2228224 | tf_op jit(solution)/shard_map/all_to_all | solution.py:559
  21.4 2.4 %copy-start.8 = (bf16[256,1536]{1,0:T(8,128)(2,1)}, bf16[256,1536]{1,0:T(8,128)(2,1)S(1)}, u32[]{:S(2)}) copy-start(bf16[256,1536]{1,0:T(8,128)(2,1)S(1)} %collective-permute-done.a_ref) | copy-start | bytes 2359300
  21.4 2.4 %collective-permute-start.5 = (bf16[256,1536]{1,0:T(8,128)(2,1)S(1)}, bf16[256,1536]{1,0:T(8,128)(2,1)}, u32[]{:S(2)}, u32[]{:S(2)}) collective-permute-start(bf16[256,1536]{1,0:T(8,128)(2,1)S(1)} %collective-permute-done.a_ref), channel_id=1, source_target_pairs={{0,1},{1,0},{2,3},{3,2},{4,5},{5,4},{6,7},{7,6},{8,9},{9,8},{10,11... | collective-permute-start | bytes 2359304 | tf_op jit(solution)/shard_map/ppermute | solution.py:551
  29.7 12.4 %copy-start.3 = (f32[768,256]{1,0:T(8,128)S(1)}, f32[768,256]{1,0:T(8,128)}, u32[]{:S(2)}) copy-start(f32[768,256]{1,0:T(8,128)} %shard_map.85.after_ref.start) | copy-start | bytes 2359300
  32.9 9.5 %copy-start = (bf16[8,272,256]{2,1,0:T(8,128)(2,1)}, bf16[8,272,256]{2,1,0:T(8,128)(2,1)S(1)}, u32[]{:S(2)}) copy-start(bf16[8,272,256]{2,1,0:T(8,128)(2,1)S(1)} %all-to-all-done.x_ref) | copy-start | bytes 3342340
  32.9 27.7 %all-to-all-start.1 = ((bf16[8,256,256]{2,1,0:T(8,128)(2,1)}), bf16[8,256,256]{2,1,0:T(8,128)(2,1)}, u32[]{:S(2)}, u32[]{:S(2)}) async-start(bf16[8,256,256]{2,1,0:T(8,128)(2,1)} %shard_map.87), calls=%async_computation.1 | async-start | bytes 2097152 | tf_op jit(solution)/shard_map/all_to_all | solution.py:559
  42.5 28.6 %copy-start.7 = (bf16[528,256]{1,0:T(8,128)(2,1)}, bf16[528,256]{1,0:T(8,128)(2,1)S(1)}, u32[]{:S(2)}) copy-start(bf16[528,256]{1,0:T(8,128)(2,1)S(1)} %get-tuple-element.26.own_ref) | copy-start | bytes 811012
  42.5 28.5 %collective-permute-start.2 = (bf16[1312,256]{1,0:T(8,128)(2,1)S(1)}, bf16[1312,256]{1,0:T(8,128)(2,1)S(1)}, u32[]{:S(2)}, u32[]{:S(2)}) collective-permute-start(bf16[1312,256]{1,0:T(8,128)(2,1)S(1)} %get-tuple-element.27), channel_id=1, source_target_pairs={{0,32},{32,64},{64,96},{1,33},{33,65},{65,97},{2,34},{34,66},{66,9... | collective-permute-start | bytes 2015240 | tf_op jit(solution)/shard_map/ppermute | solution.py:555
  46.3 9.4 %collective-permute-start.3 = (bf16[528,256]{1,0:T(8,128)(2,1)S(1)}, bf16[528,256]{1,0:T(8,128)(2,1)S(1)}, u32[]{:S(2)}, u32[]{:S(2)}) collective-permute-start(bf16[528,256]{1,0:T(8,128)(2,1)S(1)} %get-tuple-element.26.own_ref), channel_id=1, source_target_pairs={{0,96},{32,0},{1,97},{33,1},{2,98},{34,2},{3,99},{35,3},{4,100},{3... | collective-permute-start | bytes 811016 | tf_op jit(solution)/shard_map/ppermute | solution.py:619
  55.7 15.3 %copy-start.12 = (bf16[528,256]{1,0:T(8,128)(2,1)}, bf16[528,256]{1,0:T(8,128)(2,1)S(1)}, u32[]{:S(2)}) copy-start(bf16[528,256]{1,0:T(8,128)(2,1)S(1)} %collective-permute-done.3.far3_ref) | copy-start | bytes 811012
  55.7 15.3 %collective-permute-start.4 = (bf16[528,256]{1,0:T(8,128)(2,1)S(1)}, bf16[528,256]{1,0:T(8,128)(2,1)S(1)}, u32[]{:S(2)}, u32[]{:S(2)}) collective-permute-start(bf16[528,256]{1,0:T(8,128)(2,1)S(1)} %collective-permute-done.3.far3_ref), channel_id=1, source_target_pairs={{96,64},{0,96},{97,65},{1,97},{98,66},{2,98},{99,67},{3,99},{100,6... | collective-permute-start | bytes 811016 | tf_op jit(solution)/shard_map/ppermute | solution.py:620
  71.0 0.7 copy-start.13
  71.0 0.9 copy-start.11
  90.1 10.0 %copy-start.14 = (bf16[528,256]{1,0:T(8,128)(2,1)S(1)}, bf16[528,256]{1,0:T(8,128)(2,1)}, u32[]{:S(2)}) copy-start(bf16[528,256]{1,0:T(8,128)(2,1)} %get-tuple-element.36) | copy-start | bytes 811012
  90.1 30.4 %copy-start.5 = (f32[1024,256]{1,0:T(8,128)S(1)}, f32[1024,256]{1,0:T(8,128)}, u32[]{:S(2)}) copy-start(f32[1024,256]{1,0:T(8,128)} %get-tuple-element.32.fine_ref) | copy-start | bytes 3145732
  90.2 30.4 %copy-start.6 = (f32[512,256]{1,0:T(8,128)S(1)}, f32[512,256]{1,0:T(8,128)}, u32[]{:S(2)}) copy-start(f32[512,256]{1,0:T(8,128)} %get-tuple-element.33.coarse_ref) | copy-start | bytes 1572868
  90.2 33.8 %all-to-all-start.2 = ((bf16[8,256,256]{2,1,0:T(8,128)(2,1)}), bf16[8,256,256]{2,1,0:T(8,128)(2,1)S(1)}, u32[]{:S(2)}, u32[]{:S(2)}) async-start(bf16[8,256,256]{2,1,0:T(8,128)(2,1)} %bitcast.7), calls=%async_computation.2 | async-start | bytes 2097152 | tf_op jit(solution)/shard_map/all_to_all | solution.py:559
  97.5 23.0 %collective-permute-start.6 = (bf16[1312,256]{1,0:T(8,128)(2,1)}, bf16[1312,256]{1,0:T(8,128)(2,1)S(1)}, u32[]{:S(2)}, u32[]{:S(2)}) collective-permute-start(bf16[1312,256]{1,0:T(8,128)(2,1)} %get-tuple-element.34), channel_id=1, source_target_pairs={{32,0},{64,32},{96,64},{33,1},{65,33},{97,65},{34,2},{66,34},{98,6... | collective-permute-start | bytes 2015240 | tf_op jit(solution)/shard_map/ppermute | solution.py:555
  98.8 12.2 %collective-permute-start.7 = (bf16[528,256]{1,0:T(8,128)(2,1)}, bf16[528,256]{1,0:T(8,128)(2,1)S(1)}, u32[]{:S(2)}, u32[]{:S(2)}) collective-permute-start(bf16[528,256]{1,0:T(8,128)(2,1)} %get-tuple-element.35), channel_id=1, source_target_pairs={{96,0},{64,96},{97,1},{65,97},{98,2},{66,98},{99,3},{67,99},{100,4... | collective-permute-start | bytes 811016 | tf_op jit(solution)/shard_map/ppermute | solution.py:671
  100.1 16.6 %collective-permute-start.9 = (bf16[528,256]{1,0:T(8,128)(2,1)S(1)}, bf16[528,256]{1,0:T(8,128)(2,1)S(1)}, u32[]{:S(2)}, u32[]{:S(2)}) collective-permute-start(bf16[528,256]{1,0:T(8,128)(2,1)S(1)} %copy-done.14), channel_id=1, source_target_pairs={{96,0},{97,1},{98,2},{99,3},{100,4},{101,5},{102,6},{103,7},{104,8... | collective-permute-start | bytes 811016 | tf_op jit(solution)/shard_map/ppermute | solution.py:672
  111.0 9.6 %collective-permute-start.8 = (bf16[528,256]{1,0:T(8,128)(2,1)S(1)}, bf16[528,256]{1,0:T(8,128)(2,1)S(1)}, u32[]{:S(2)}, u32[]{:S(2)}) collective-permute-start(bf16[528,256]{1,0:T(8,128)(2,1)S(1)} %collective-permute-done.7), channel_id=1, source_target_pairs={{0,32},{96,0},{1,33},{97,1},{2,34},{98,2},{3,35},{99,3},{4,36},{10... | collective-permute-start | bytes 811016 | tf_op jit(solution)/shard_map/ppermute | solution.py:673
  120.6 1.6 copy-start.4
  124.0 1.0 copy-start.1
  130.7 7.4 %copy-start.10 = (bf16[256,1536]{1,0:T(8,128)(2,1)S(1)}, bf16[256,1536]{1,0:T(8,128)(2,1)}, u32[]{:S(2)}) copy-start(bf16[256,1536]{1,0:T(8,128)(2,1)} %get-tuple-element.37) | copy-start | bytes 2359300
  130.7 7.4 %collective-permute-start.10 = (bf16[256,1536]{1,0:T(8,128)(2,1)}, bf16[256,1536]{1,0:T(8,128)(2,1)S(1)}, u32[]{:S(2)}, u32[]{:S(2)}) collective-permute-start(bf16[256,1536]{1,0:T(8,128)(2,1)} %get-tuple-element.38), channel_id=1, source_target_pairs={{0,1},{1,0},{2,3},{3,2},{4,5},{5,4},{6,7},{7,6},{8,9},{9,8},{10,11... | collective-permute-start | bytes 2359304 | tf_op jit(solution)/shard_map/ppermute | solution.py:551
  130.7 23.2 %all-to-all-start.3 = ((bf16[8,272,256]{2,1,0:T(8,128)(2,1)}), bf16[8,272,256]{2,1,0:T(8,128)(2,1)}, u32[]{:S(2)}, u32[]{:S(2)}) async-start(bf16[8,272,256]{2,1,0:T(8,128)(2,1)} %shard_map.90.refs_0_), calls=%async_computation.3 | async-start | bytes 2228224 | tf_op jit(solution)/shard_map/all_to_all | solution.py:559
  138.3 15.7 %copy-start.2 = (bf16[8,256,256]{2,1,0:T(8,128)(2,1)S(1)}, bf16[8,256,256]{2,1,0:T(8,128)(2,1)}, u32[]{:S(2)}) copy-start(bf16[8,256,256]{2,1,0:T(8,128)(2,1)} %copy-done.1) | copy-start | bytes 3145732
  144.5 24.8 %copy-start.9 = (bf16[256,1536]{1,0:T(8,128)(2,1)S(1)}, bf16[256,1536]{1,0:T(8,128)(2,1)}, u32[]{:S(2)}) copy-start(bf16[256,1536]{1,0:T(8,128)(2,1)} %get-tuple-element.40) | copy-start | bytes 2359300
  144.5 11.9 %collective-permute-start.11 = (bf16[256,1536]{1,0:T(8,128)(2,1)}, bf16[256,1536]{1,0:T(8,128)(2,1)}, u32[]{:S(2)}, u32[]{:S(2)}) collective-permute-start(bf16[256,1536]{1,0:T(8,128)(2,1)} %get-tuple-element.41), channel_id=1, source_target_pairs={{0,1},{1,0},{2,3},{3,2},{4,5},{5,4},{6,7},{7,6},{8,9},{9,8},{10,11... | collective-permute-start | bytes 2359304 | tf_op jit(solution)/shard_map/ppermute | solution.py:551
  144.5 24.8 %collective-permute-start.12 = (bf16[256,1536]{1,0:T(8,128)(2,1)S(1)}, bf16[256,1536]{1,0:T(8,128)(2,1)}, u32[]{:S(2)}, u32[]{:S(2)}) collective-permute-start(bf16[256,1536]{1,0:T(8,128)(2,1)S(1)} %add_convert_fusion.1), channel_id=1, source_target_pairs={{0,2},{2,0},{1,3},{3,1},{4,6},{6,4},{5,7},{7,5},{8,10},{10,8},{9,1... | collective-permute-start | bytes 2359304 | tf_op jit(solution)/shard_map/ppermute | solution.py:551

commit v3 on v2

--- a/solution.py
+++ b/solution.py
@@ -616,8 +616,8 @@
         in_specs=[whole, in_place],
     )(own, early)
     near_in = planes_up(near, 1)
-    far3_in = lax.ppermute(far, "z", [(0, 3), (1, 0)])
-    far2_in = lax.ppermute(far3_in, "z", [(3, 2), (0, 3)])
+    far2_in = planes_up(far, 2)
+    far3_in = planes_up(far, 3)
     pair = in_plane(pair_packed).reshape(rows, 2 * HEAD_DIM)
 
     part, sums = call(
@@ -668,9 +668,8 @@
     )(z, own, far, near_in, far2_in, far3_in, pair, part)
 
     back1_in = planes_up(back1, -1)
-    halfway = lax.ppermute(back2, "z", [(3, 0), (2, 3)])
-    back3_in = lax.ppermute(back3, "z", [(3, 0)])
-    back2_in = lax.ppermute(halfway, "z", [(0, 1), (3, 0)])
+    back2_in = planes_up(back2, -2)
+    back3_in = planes_up(back3, -3)
     attn_in = in_plane(attn.reshape(PLANE_DEVS, tokens, 256))
     finished = call(
         finish_kernel,

time: 173 us -> 170 us (0.983)
  the two profiles are of different devices: /device:TPU:4 before, /device:TPU:36 now
where the time goes in v3:
time: 170 us; the launch traced here: 169 us
  Pallas kernels  59 us (35%)
  waiting for transfers between devices  58.1 us (34%)
  starting transfers between devices  44 us (26%)
  local copies, waits for them, and re-layouts  3.57 us (2%)
  other arithmetic  3.32 us (2%)
    all_to_all x4, starting transfers between devices, in_plane(): return lax.all_to_all(x, PLANE, 0, 0, tiled=True)  30.3 us
    ppermute x6, waiting for transfers between devices, planes_up(): lax.ppermute(x, 'z', [(i, i + by) for i in range(PLANES) if 0 <= i + by <...  20.9 us
    all_to_all x4, waiting for transfers between devices, in_plane(): return lax.all_to_all(x, PLANE, 0, 0, tiled=True)  18.6 us
    ppermute x6, waiting for transfers between devices, swap(): return lax.ppermute(x, axis, [(0, 1), (1, 0)])  18.6 us
    pallas_call x1, Pallas kernels, shards(): call(attention_kernel, (array(rows, 256), array(rows - WINDOW, 256, dtype...  18.2 us
    pallas_call x2, Pallas kernels, project(): pl.pallas_call(functools.partial(project_kernel, halves), out_shape=(out,...  12 us
    ppermute x6, starting transfers between devices, planes_up(): lax.ppermute(x, 'z', [(i, i + by) for i in range(PLANES) if 0 <= i + by <...  11.5 us
    pallas_call x2, Pallas kernels, grad_part(): pl.pallas_call(functools.partial(grad_far_kernel if rest else grad_near_k...  11.2 us
  transfers between devices with their start and end apart: 16, of which 7 were waited for; matrix products, arithmetic and copies ran while one was open for 0% of the time, Pallas kernels for 21%

profile of v3, /device:TPU:36, one launch (start us, length us, event | category | flops | bytes accessed | tf_op | source)
XLA Modules:
  0.0 168.9 jit_solution(10561494850025590882)
XLA Ops:
  0.6 0.1 collective-permute-start.1
  0.7 1.3 collective-permute-start
  2.0 2.7 %shard_map.84 = bf16[8,272,256]{2,1,0:T(8,128)(2,1)} custom-call(bf16[256,768]{1,0:T(8,128)(2,1)} %q_ref.3, bf16[256,768]{1,0:T(8,128)(2,1)} %k_ref.1, bf16[256,768]{1,0:T(8,128)(2,1)} %v_ref.1), custom_call_target="tpu_custom_call" | custom-call | tf_op jit(solution)/shard_map/pallas_call | solution.py:600
  4.7 7.4 %all-to-all-start = ((bf16[8,272,256]{2,1,0:T(8,128)(2,1)}), bf16[8,272,256]{2,1,0:T(8,128)(2,1)S(1)}, u32[]{:S(2)}, u32[]{:S(2)}) async-start(bf16[8,272,256]{2,1,0:T(8,128)(2,1)} %shard_map.84), calls=%async_computation | async-start | bytes 2228224 | tf_op jit(solution)/shard_map/all_to_all | solution.py:559
  12.1 0.6 pad_add_fusion.order_ref
  12.7 0.0 collective-permute-done.1.b_ref
  12.7 5.3 %shard_map.85.after_ref.start = f32[768,256]{1,0:T(8,128)} custom-call(s32[4]{0:T(128)} %pad_add_fusion.order_ref, bf16[256,1536]{1,0:T(8,128)(2,1)} %a_ref.1, bf16[256,1536]{1,0:T(8,128)(2,1)} %collective-permute-done.1.b_ref, bf16[768,6144]{1,0:T(8,128)(2,1)} %w_ref.7), custom_call_target="tpu_custom_call" | custom-call | tf_op jit(solution)/shard_map/pallas_call | solution.py:487
  18.0 3.4 %collective-permute-done.a_ref = bf16[256,1536]{1,0:T(8,128)(2,1)S(1)} collective-permute-done((bf16[256,1536]{1,0:T(8,128)(2,1)}, bf16[256,1536]{1,0:T(8,128)(2,1)S(1)}, u32[]{:S(2)}, u32[]{:S(2)}) %collective-permute-start) | collective-permute-done | bytes 786464 | tf_op jit(solution)/shard_map/ppermute | solution.py:551
  21.4 0.0 collective-permute-start.5
  21.4 2.4 %collective-permute-done.5.b_ref = bf16[256,1536]{1,0:T(8,128)(2,1)} collective-permute-done((bf16[256,1536]{1,0:T(8,128)(2,1)S(1)}, bf16[256,1536]{1,0:T(8,128)(2,1)}, u32[]{:S(2)}, u32[]{:S(2)}) %collective-permute-start.5) | collective-permute-done | bytes 786464 | tf_op jit(solution)/shard_map/ppermute | solution.py:551
  23.8 5.9 %shard_map.87 = bf16[8,256,256]{2,1,0:T(8,128)(2,1)} custom-call(s32[4]{0:T(128)} %pad_add_fusion.order_ref, bf16[256,1536]{1,0:T(8,128)(2,1)} %copy-done.8, bf16[256,1536]{1,0:T(8,128)(2,1)} %collective-permute-done.5.b_ref, bf16[768,6144]{1,0:T(8,128)(2,1)} %w_ref.7, f32[768,256]{1,0:T(8,128)} %shard_map.85.after_ref.start, bf16[256,768]{1,0:T(8,128)(2,1)} %q_ref.3), custom_call_target="tpu_custom_call" | custom-call | tf_op jit(solution)/shard_map/pallas_call | solution.py:487
  29.7 3.2 %all-to-all-done.x_ref = bf16[8,272,256]{2,1,0:T(8,128)(2,1)S(1)} async-done(((bf16[8,272,256]{2,1,0:T(8,128)(2,1)}), bf16[8,272,256]{2,1,0:T(8,128)(2,1)S(1)}, u32[]{:S(2)}, u32[]{:S(2)}) %all-to-all-start) | async-done | bytes 1114144 | tf_op jit(solution)/shard_map/all_to_all | solution.py:559
  32.9 9.2 %all-to-all-start.1 = ((bf16[8,256,256]{2,1,0:T(8,128)(2,1)}), bf16[8,256,256]{2,1,0:T(8,128)(2,1)}, u32[]{:S(2)}, u32[]{:S(2)}) async-start(bf16[8,256,256]{2,1,0:T(8,128)(2,1)} %shard_map.87), calls=%async_computation.1 | async-start | bytes 2097152 | tf_op jit(solution)/shard_map/all_to_all | solution.py:559
  42.1 0.3 shard_map.86
  42.5 0.0 copy-start.7
  42.5 3.8 %collective-permute-start.2 = (bf16[1312,256]{1,0:T(8,128)(2,1)S(1)}, bf16[1312,256]{1,0:T(8,128)(2,1)S(1)}, u32[]{:S(2)}, u32[]{:S(2)}) collective-permute-start(bf16[1312,256]{1,0:T(8,128)(2,1)S(1)} %get-tuple-element.27), channel_id=1, source_target_pairs={{0,32},{32,64},{64,96},{1,33},{33,65},{65,97},{2,34},{34,66},{66,9... | collective-permute-start | bytes 2015240 | tf_op jit(solution)/shard_map/ppermute | solution.py:555
  46.3 0.7 collective-permute-start.4
  47.0 3.0 %collective-permute-start.3 = (bf16[528,256]{1,0:T(8,128)(2,1)S(1)}, bf16[528,256]{1,0:T(8,128)(2,1)S(1)}, u32[]{:S(2)}, u32[]{:S(2)}) collective-permute-start(bf16[528,256]{1,0:T(8,128)(2,1)S(1)} %get-tuple-element.26.own_ref), channel_id=1, source_target_pairs={{0,64},{32,96},{1,65},{33,97},{2,66},{34,98},{3,67},{35,99},{4,68}... | collective-permute-start | bytes 811016 | tf_op jit(solution)/shard_map/ppermute | solution.py:555
  50.0 6.9 %all-to-all-done.1 = bf16[8,256,256]{2,1,0:T(8,128)(2,1)} async-done(((bf16[8,256,256]{2,1,0:T(8,128)(2,1)}), bf16[8,256,256]{2,1,0:T(8,128)(2,1)}, u32[]{:S(2)}, u32[]{:S(2)}) %all-to-all-start.1) | async-done | bytes 1048608 | tf_op jit(solution)/shard_map/all_to_all | solution.py:559
  56.8 10.4 %shard_map.88 = (f32[1024,256]{1,0:T(8,128)}, f32[2048,256]{1,0:T(8,128)}) custom-call(bf16[8,272,256]{2,1,0:T(8,128)(2,1)} %copy-done, bf16[2048,256]{1,0:T(8,128)(2,1)} %bitcast.5.pair_ref), custom_call_target="tpu_custom_call" | custom-call | tf_op jit(solution)/shard_map/pallas_call | solution.py:623
  67.3 0.0 collective-permute-done.4.far3_ref
  67.3 0.0 collective-permute-done.3.far2_ref
  67.3 0.0 copy-start.13
  67.3 0.0 collective-permute-done.2.near_ref
  67.3 0.0 copy-start.11
  67.3 0.7 copy-done.12
  68.0 0.1 copy-done.13
  68.1 0.2 copy-done.11
  68.3 18.2 %shard_map.89 = (bf16[2048,256]{1,0:T(8,128)(2,1)}, f32[1024,256]{1,0:T(8,128)}, f32[512,256]{1,0:T(8,128)}, bf16[1312,256]{1,0:T(8,128)(2,1)}, bf16[528,256]{1,0:T(8,128)(2,1)}, /*index=5*/bf16[528,256]{1,0:T(8,128)(2,1)}) custom-call(s32[1]{0:T(128)} %bitcast.4.z_ref, bf16[8,272,256]{2,1,0:T(8,128)(2,1)} %copy-done, bf16[528,256]{1,0:T(8,128)(2,1)} %copy-done.7, ...), custom_call_target="tpu_custom_call" | custom-call | tf_op jit(solution)/shard_map/pallas_call | solution.py:633
  86.5 6.3 %all-to-all-start.2 = ((bf16[8,256,256]{2,1,0:T(8,128)(2,1)}), bf16[8,256,256]{2,1,0:T(8,128)(2,1)S(1)}, u32[]{:S(2)}, u32[]{:S(2)}) async-start(bf16[8,256,256]{2,1,0:T(8,128)(2,1)} %bitcast.7), calls=%async_computation.2 | async-start | bytes 2097152 | tf_op jit(solution)/shard_map/all_to_all | solution.py:559
  92.9 2.0 %collective-permute-start.6 = (bf16[1312,256]{1,0:T(8,128)(2,1)}, bf16[1312,256]{1,0:T(8,128)(2,1)S(1)}, u32[]{:S(2)}, u32[]{:S(2)}) collective-permute-start(bf16[1312,256]{1,0:T(8,128)(2,1)} %get-tuple-element.34), channel_id=1, source_target_pairs={{32,0},{64,32},{96,64},{33,1},{65,33},{97,65},{34,2},{66,34},{98,6... | collective-permute-start | bytes 2015240 | tf_op jit(solution)/shard_map/ppermute | solution.py:555
  94.9 1.3 collective-permute-start.7
  96.2 0.7 collective-permute-start.8
  96.9 20.9 %collective-permute-done.7.back2_ref = bf16[528,256]{1,0:T(8,128)(2,1)S(1)} collective-permute-done((bf16[528,256]{1,0:T(8,128)(2,1)}, bf16[528,256]{1,0:T(8,128)(2,1)S(1)}, u32[]{:S(2)}, u32[]{:S(2)}) %collective-permute-start.7) | collective-permute-done | bytes 270368 | tf_op jit(solution)/shard_map/ppermute | solution.py:555
  117.7 0.0 collective-permute-done.8.back3_ref
  117.8 1.6 copy-done.4
  119.4 1.8 %shard_map.90.refs_0_ = bf16[8,272,256]{2,1,0:T(8,128)(2,1)} custom-call(f32[2048,256]{1,0:T(8,128)S(1)} %copy-done.4, f32[1024,256]{1,0:T(8,128)S(1)} %copy-done.5, f32[512,256]{1,0:T(8,128)S(1)} %copy-done.6, bf16[1312,256]{1,0:T(8,128)(2,1)S(1)} %collective-permute-done.6.back1_ref, bf16[528,256]{1,0:T(8,128)(2,1)S(1)} %collective-permute-done.7.back2_ref, ...), custom_call_target="tpu_custom_call" | custom-call | tf_op jit(solution)/shard_map/pallas_call | solution.py:674
  121.1 0.0 all-to-all-done.2.attn_ref.pair_ref
  121.1 1.0 copy-done.1
  122.1 5.8 %shard_map.91 = (bf16[256,1536]{1,0:T(8,128)(2,1)}, bf16[256,1536]{1,0:T(8,128)(2,1)}) custom-call(s32[4]{0:T(128)} %pad_add_fusion.order_ref, bf16[8,256,256]{2,1,0:T(8,128)(2,1)} %copy-done.1, bf16[768,6144]{1,0:T(8,128)(2,1)} %w_ref.7, bf16[8,272,256]{2,1,0:T(8,128)(2,1)} %shard_map.90.refs_0_), custom_call_target="tpu_custom_call" | custom-call | tf_op jit(solution)/shard_map/pallas_call | solution.py:532
  127.9 7.4 %all-to-all-start.3 = ((bf16[8,272,256]{2,1,0:T(8,128)(2,1)}), bf16[8,272,256]{2,1,0:T(8,128)(2,1)}, u32[]{:S(2)}, u32[]{:S(2)}) async-start(bf16[8,272,256]{2,1,0:T(8,128)(2,1)} %shard_map.90.refs_0_), calls=%async_computation.3 | async-start | bytes 2228224 | tf_op jit(solution)/shard_map/all_to_all | solution.py:559
  135.2 0.2 add_convert_fusion.1
  135.4 6.2 %shard_map.92 = (bf16[256,1536]{1,0:T(8,128)(2,1)}, bf16[256,1536]{1,0:T(8,128)(2,1)}) custom-call(s32[4]{0:T(128)} %pad_add_fusion.order_ref, bf16[8,256,256]{2,1,0:T(8,128)(2,1)} %copy-done.1, bf16[768,6144]{1,0:T(8,128)(2,1)} %w_ref.7, bf16[8,272,256]{2,1,0:T(8,128)(2,1)} %shard_map.90.refs_0_), custom_call_target="tpu_custom_call" | custom-call | tf_op jit(solution)/shard_map/pallas_call | solution.py:532
  141.7 0.9 collective-permute-start.11
  142.6 8.5 %all-to-all-done.3.x_ref = bf16[8,272,256]{2,1,0:T(8,128)(2,1)} async-done(((bf16[8,272,256]{2,1,0:T(8,128)(2,1)}), bf16[8,272,256]{2,1,0:T(8,128)(2,1)}, u32[]{:S(2)}, u32[]{:S(2)}) %all-to-all-start.3) | async-done | bytes 1114144 | tf_op jit(solution)/shard_map/all_to_all | solution.py:559
  151.1 2.5 %shard_map.93 = (bf16[256,768]{1,0:T(8,128)(2,1)}, bf16[256,768]{1,0:T(8,128)(2,1)}, bf16[256,768]{1,0:T(8,128)(2,1)}) custom-call(bf16[8,256,256]{2,1,0:T(8,128)(2,1)S(1)} %copy-done.2, bf16[8,272,256]{2,1,0:T(8,128)(2,1)} %all-to-all-done.3.x_ref), custom_call_target="tpu_custom_call" | custom-call | tf_op jit(solution)/shard_map/pallas_call | solution.py:687
  153.6 12.8 %collective-permute-done.11 = bf16[256,1536]{1,0:T(8,128)(2,1)} collective-permute-done((bf16[256,1536]{1,0:T(8,128)(2,1)S(1)}, bf16[256,1536]{1,0:T(8,128)(2,1)}, u32[]{:S(2)}, u32[]{:S(2)}) %collective-permute-start.11) | collective-permute-done | bytes 786464 | tf_op jit(solution)/shard_map/ppermute | solution.py:551
  166.4 2.5 %add_convert_fusion = bf16[256,1536]{1,0:T(8,128)(2,1)} fusion(bf16[256,1536]{1,0:T(8,128)(2,1)} %collective-permute-done.11, bf16[256,1536]{1,0:T(8,128)(2,1)} %collective-permute-done.10, bf16[256,1536]{1,0:T(8,128)(2,1)S(1)} %copy-done.9), kind=kLoop, calls=%fused_computation | loop fusion | flops 2359296 | bytes 3145728 | tf_op jit(solution)/shard_map/convert_element_type | solution.py:585
  (27 shorter events, 0.1 us)
Async XLA Ops:
  0.6 12.1 %collective-permute-start.1 = (bf16[256,1536]{1,0:T(8,128)(2,1)}, bf16[256,1536]{1,0:T(8,128)(2,1)}, u32[]{:S(2)}, u32[]{:S(2)}) collective-permute-start(bf16[256,1536]{1,0:T(8,128)(2,1)} %a_ref.1), channel_id=1, source_target_pairs={{0,1},{1,0},{2,3},{3,2},{4,5},{5,4},{6,7},{7,6},{8,9},{9,8},{10,11... | collective-permute-start | bytes 2359304 | tf_op jit(solution)/shard_map/ppermute | solution.py:551
  0.7 20.6 %collective-permute-start = (bf16[256,1536]{1,0:T(8,128)(2,1)}, bf16[256,1536]{1,0:T(8,128)(2,1)S(1)}, u32[]{:S(2)}, u32[]{:S(2)}) collective-permute-start(bf16[256,1536]{1,0:T(8,128)(2,1)} %a_ref.1), channel_id=1, source_target_pairs={{0,2},{2,0},{1,3},{3,1},{4,6},{6,4},{5,7},{7,5},{8,10},{10,8},{9,1... | collective-permute-start | bytes 2359304 | tf_op jit(solution)/shard_map/ppermute | solution.py:551
  4.7 28.2 %all-to-all-start = ((bf16[8,272,256]{2,1,0:T(8,128)(2,1)}), bf16[8,272,256]{2,1,0:T(8,128)(2,1)S(1)}, u32[]{:S(2)}, u32[]{:S(2)}) async-start(bf16[8,272,256]{2,1,0:T(8,128)(2,1)} %shard_map.84), calls=%async_computation | async-start | bytes 2228224 | tf_op jit(solution)/shard_map/all_to_all | solution.py:559
  21.4 2.4 %copy-start.8 = (bf16[256,1536]{1,0:T(8,128)(2,1)}, bf16[256,1536]{1,0:T(8,128)(2,1)S(1)}, u32[]{:S(2)}) copy-start(bf16[256,1536]{1,0:T(8,128)(2,1)S(1)} %collective-permute-done.a_ref) | copy-start | bytes 2359300
  21.4 2.4 %collective-permute-start.5 = (bf16[256,1536]{1,0:T(8,128)(2,1)S(1)}, bf16[256,1536]{1,0:T(8,128)(2,1)}, u32[]{:S(2)}, u32[]{:S(2)}) collective-permute-start(bf16[256,1536]{1,0:T(8,128)(2,1)S(1)} %collective-permute-done.a_ref), channel_id=1, source_target_pairs={{0,1},{1,0},{2,3},{3,2},{4,5},{5,4},{6,7},{7,6},{8,9},{9,8},{10,11... | collective-permute-start | bytes 2359304 | tf_op jit(solution)/shard_map/ppermute | solution.py:551
  29.7 12.4 %copy-start.3 = (f32[768,256]{1,0:T(8,128)S(1)}, f32[768,256]{1,0:T(8,128)}, u32[]{:S(2)}) copy-start(f32[768,256]{1,0:T(8,128)} %shard_map.85.after_ref.start) | copy-start | bytes 2359300
  32.9 9.5 %copy-start = (bf16[8,272,256]{2,1,0:T(8,128)(2,1)}, bf16[8,272,256]{2,1,0:T(8,128)(2,1)S(1)}, u32[]{:S(2)}) copy-start(bf16[8,272,256]{2,1,0:T(8,128)(2,1)S(1)} %all-to-all-done.x_ref) | copy-start | bytes 3342340
  32.9 23.9 %all-to-all-start.1 = ((bf16[8,256,256]{2,1,0:T(8,128)(2,1)}), bf16[8,256,256]{2,1,0:T(8,128)(2,1)}, u32[]{:S(2)}, u32[]{:S(2)}) async-start(bf16[8,256,256]{2,1,0:T(8,128)(2,1)} %shard_map.87), calls=%async_computation.1 | async-start | bytes 2097152 | tf_op jit(solution)/shard_map/all_to_all | solution.py:559
  42.5 24.8 %copy-start.7 = (bf16[528,256]{1,0:T(8,128)(2,1)}, bf16[528,256]{1,0:T(8,128)(2,1)S(1)}, u32[]{:S(2)}) copy-start(bf16[528,256]{1,0:T(8,128)(2,1)S(1)} %get-tuple-element.26.own_ref) | copy-start | bytes 811012
  42.5 24.8 %collective-permute-start.2 = (bf16[1312,256]{1,0:T(8,128)(2,1)S(1)}, bf16[1312,256]{1,0:T(8,128)(2,1)S(1)}, u32[]{:S(2)}, u32[]{:S(2)}) collective-permute-start(bf16[1312,256]{1,0:T(8,128)(2,1)S(1)} %get-tuple-element.27), channel_id=1, source_target_pairs={{0,32},{32,64},{64,96},{1,33},{33,65},{65,97},{2,34},{34,66},{66,9... | collective-permute-start | bytes 2015240 | tf_op jit(solution)/shard_map/ppermute | solution.py:555
  46.3 20.9 %collective-permute-start.4 = (bf16[528,256]{1,0:T(8,128)(2,1)S(1)}, bf16[528,256]{1,0:T(8,128)(2,1)S(1)}, u32[]{:S(2)}, u32[]{:S(2)}) collective-permute-start(bf16[528,256]{1,0:T(8,128)(2,1)S(1)} %get-tuple-element.26.own_ref), channel_id=1, source_target_pairs={{0,96},{1,97},{2,98},{3,99},{4,100},{5,101},{6,102},{7,103},{8,104... | collective-permute-start | bytes 811016 | tf_op jit(solution)/shard_map/ppermute | solution.py:555
  47.0 20.3 %collective-permute-start.3 = (bf16[528,256]{1,0:T(8,128)(2,1)S(1)}, bf16[528,256]{1,0:T(8,128)(2,1)S(1)}, u32[]{:S(2)}, u32[]{:S(2)}) collective-permute-start(bf16[528,256]{1,0:T(8,128)(2,1)S(1)} %get-tuple-element.26.own_ref), channel_id=1, source_target_pairs={{0,64},{32,96},{1,65},{33,97},{2,66},{34,98},{3,67},{35,99},{4,68}... | collective-permute-start | bytes 811016 | tf_op jit(solution)/shard_map/ppermute | solution.py:555
  67.3 0.7 copy-start.12
  67.3 0.8 copy-start.13
  67.3 1.0 copy-start.11
  86.5 9.7 %copy-start.14 = (bf16[528,256]{1,0:T(8,128)(2,1)S(1)}, bf16[528,256]{1,0:T(8,128)(2,1)}, u32[]{:S(2)}) copy-start(bf16[528,256]{1,0:T(8,128)(2,1)} %get-tuple-element.36) | copy-start | bytes 811012
  86.5 31.2 %copy-start.5 = (f32[1024,256]{1,0:T(8,128)S(1)}, f32[1024,256]{1,0:T(8,128)}, u32[]{:S(2)}) copy-start(f32[1024,256]{1,0:T(8,128)} %get-tuple-element.32.fine_ref) | copy-start | bytes 3145732
  86.5 31.2 %copy-start.6 = (f32[512,256]{1,0:T(8,128)S(1)}, f32[512,256]{1,0:T(8,128)}, u32[]{:S(2)}) copy-start(f32[512,256]{1,0:T(8,128)} %get-tuple-element.33.coarse_ref) | copy-start | bytes 1572868
  86.5 34.6 %all-to-all-start.2 = ((bf16[8,256,256]{2,1,0:T(8,128)(2,1)}), bf16[8,256,256]{2,1,0:T(8,128)(2,1)S(1)}, u32[]{:S(2)}, u32[]{:S(2)}) async-start(bf16[8,256,256]{2,1,0:T(8,128)(2,1)} %bitcast.7), calls=%async_computation.2 | async-start | bytes 2097152 | tf_op jit(solution)/shard_map/all_to_all | solution.py:559
  92.9 24.9 %collective-permute-start.6 = (bf16[1312,256]{1,0:T(8,128)(2,1)}, bf16[1312,256]{1,0:T(8,128)(2,1)S(1)}, u32[]{:S(2)}, u32[]{:S(2)}) collective-permute-start(bf16[1312,256]{1,0:T(8,128)(2,1)} %get-tuple-element.34), channel_id=1, source_target_pairs={{32,0},{64,32},{96,64},{33,1},{65,33},{97,65},{34,2},{66,34},{98,6... | collective-permute-start | bytes 2015240 | tf_op jit(solution)/shard_map/ppermute | solution.py:555
  94.9 22.9 %collective-permute-start.7 = (bf16[528,256]{1,0:T(8,128)(2,1)}, bf16[528,256]{1,0:T(8,128)(2,1)S(1)}, u32[]{:S(2)}, u32[]{:S(2)}) collective-permute-start(bf16[528,256]{1,0:T(8,128)(2,1)} %get-tuple-element.35), channel_id=1, source_target_pairs={{64,0},{96,32},{65,1},{97,33},{66,2},{98,34},{67,3},{99,35},{68,4}... | collective-permute-start | bytes 811016 | tf_op jit(solution)/shard_map/ppermute | solution.py:555
  96.2 21.6 %collective-permute-start.8 = (bf16[528,256]{1,0:T(8,128)(2,1)S(1)}, bf16[528,256]{1,0:T(8,128)(2,1)S(1)}, u32[]{:S(2)}, u32[]{:S(2)}) collective-permute-start(bf16[528,256]{1,0:T(8,128)(2,1)S(1)} %copy-done.14), channel_id=1, source_target_pairs={{96,0},{97,1},{98,2},{99,3},{100,4},{101,5},{102,6},{103,7},{104,8... | collective-permute-start | bytes 811016 | tf_op jit(solution)/shard_map/ppermute | solution.py:555
  117.8 1.6 copy-start.4
  121.1 1.0 copy-start.1
  127.9 7.4 %copy-start.10 = (bf16[256,1536]{1,0:T(8,128)(2,1)S(1)}, bf16[256,1536]{1,0:T(8,128)(2,1)}, u32[]{:S(2)}) copy-start(bf16[256,1536]{1,0:T(8,128)(2,1)} %get-tuple-element.37) | copy-start | bytes 2359300
  127.9 7.4 %collective-permute-start.9 = (bf16[256,1536]{1,0:T(8,128)(2,1)}, bf16[256,1536]{1,0:T(8,128)(2,1)S(1)}, u32[]{:S(2)}, u32[]{:S(2)}) collective-permute-start(bf16[256,1536]{1,0:T(8,128)(2,1)} %get-tuple-element.38), channel_id=1, source_target_pairs={{0,1},{1,0},{2,3},{3,2},{4,5},{5,4},{6,7},{7,6},{8,9},{9,8},{10,11... | collective-permute-start | bytes 2359304 | tf_op jit(solution)/shard_map/ppermute | solution.py:551
  127.9 23.2 %all-to-all-start.3 = ((bf16[8,272,256]{2,1,0:T(8,128)(2,1)}), bf16[8,272,256]{2,1,0:T(8,128)(2,1)}, u32[]{:S(2)}, u32[]{:S(2)}) async-start(bf16[8,272,256]{2,1,0:T(8,128)(2,1)} %shard_map.90.refs_0_), calls=%async_computation.3 | async-start | bytes 2228224 | tf_op jit(solution)/shard_map/all_to_all | solution.py:559
  135.4 15.7 %copy-start.2 = (bf16[8,256,256]{2,1,0:T(8,128)(2,1)S(1)}, bf16[8,256,256]{2,1,0:T(8,128)(2,1)}, u32[]{:S(2)}) copy-start(bf16[8,256,256]{2,1,0:T(8,128)(2,1)} %copy-done.1) | copy-start | bytes 3145732
  141.7 24.7 %copy-start.9 = (bf16[256,1536]{1,0:T(8,128)(2,1)S(1)}, bf16[256,1536]{1,0:T(8,128)(2,1)}, u32[]{:S(2)}) copy-start(bf16[256,1536]{1,0:T(8,128)(2,1)} %get-tuple-element.40) | copy-start | bytes 2359300
  141.7 11.9 %collective-permute-start.10 = (bf16[256,1536]{1,0:T(8,128)(2,1)}, bf16[256,1536]{1,0:T(8,128)(2,1)}, u32[]{:S(2)}, u32[]{:S(2)}) collective-permute-start(bf16[256,1536]{1,0:T(8,128)(2,1)} %get-tuple-element.41), channel_id=1, source_target_pairs={{0,1},{1,0},{2,3},{3,2},{4,5},{5,4},{6,7},{7,6},{8,9},{9,8},{10,11... | collective-permute-start | bytes 2359304 | tf_op jit(solution)/shard_map/ppermute | solution.py:551
  141.7 24.7 %collective-permute-start.11 = (bf16[256,1536]{1,0:T(8,128)(2,1)S(1)}, bf16[256,1536]{1,0:T(8,128)(2,1)}, u32[]{:S(2)}, u32[]{:S(2)}) collective-permute-start(bf16[256,1536]{1,0:T(8,128)(2,1)S(1)} %add_convert_fusion.1), channel_id=1, source_target_pairs={{0,2},{2,0},{1,3},{3,1},{4,6},{6,4},{5,7},{7,5},{8,10},{10,8},{9,1... | collective-permute-start | bytes 2359304 | tf_op jit(solution)/shard_map/ppermute | solution.py:551

commit v4 on v3

--- a/solution.py
+++ b/solution.py
@@ -391,7 +391,7 @@
 
 
 def finish_kernel(
-    sums_ref, fine_ref, coarse_ref, back1_ref, back2_ref, back3_ref, out_ref, high, low
+    sums_ref, fine_ref, coarse_ref, back1_ref, back2_ref, back3_ref, round_ref, out_ref, high, low
 ):
     rows = sums_ref.shape[0]
     tokens = rows // PLANE_DEVS
@@ -400,7 +400,7 @@
     step = BLOCK // SHORT
     base = WINDOW + TAIL
     part = half + TAIL
-    ups = (back2_ref, back3_ref)
+    ups = (back2_ref, back3_ref, round_ref)
     total = coarse_ref[...]
     for up in ups:
         total += up[0:coarse, :].astype(f32)
@@ -668,8 +668,10 @@
     )(z, own, far, near_in, far2_in, far3_in, pair, part)
 
     back1_in = planes_up(back1, -1)
-    back2_in = planes_up(back2, -2)
+    halfway = lax.ppermute(back2, "z", [(3, 0)])
     back3_in = planes_up(back3, -3)
+    back2_in = lax.ppermute(back2, "z", [(2, 0)])
+    round_in = lax.ppermute(halfway, "z", [(0, 1)])
     attn_in = in_plane(attn.reshape(PLANE_DEVS, tokens, 256))
     finished = call(
         finish_kernel,
@@ -679,7 +681,7 @@
             pltpu.VMEM((coarse + 2 * TAIL, 256), bf16),
             pltpu.VMEM((coarse + 2 * TAIL, 256), bf16),
         ],
-    )(sums, fine, short, back1_in, back2_in, back3_in)
+    )(sums, fine, short, back1_in, back2_in, back3_in, round_in)
     mixed_out = projected(
         attn_in, out_weight, out_grad.shape[1], blocks, (finished,)
     )

time: 170 us -> 171 us (level)
    ppermute x6 -> x5, waiting for transfers between devices: 20.9 us -> 0.01 us  [planes_up(): lax.ppermute(x, 'z', [(i, i + by) for i in range(PLANES) if 0 <= i + by <...]
    ppermute x0 -> x3, waiting for transfers between devices: none -> 20.7 us  [the longest x1 20.7 us: shards(): round_in = lax.ppermute(halfway, 'z', [(0, 1)])]
    ppermute x0 -> x3, starting transfers between devices: none -> 2.65 us  [the longest x1 1.29 us: shards(): round_in = lax.ppermute(halfway, 'z', [(0, 1)])]
    ppermute x6 -> x5, starting transfers between devices: 11.5 us -> 10.2 us  [planes_up(): lax.ppermute(x, 'z', [(i, i + by) for i in range(PLANES) if 0 <= i + by <...]
  transfers between devices with their start and end apart: 16 -> 18, of which waited for: 7 -> 7; matrix products, arithmetic and copies ran while one was open for 0% -> 0% of each run, Pallas kernels for 21% -> 21%
where the time goes in v4:
time: 171 us; the launch traced here: 170 us
  Pallas kernels  59.2 us (35%)
  waiting for transfers between devices  57.8 us (34%)
  starting transfers between devices  45.4 us (27%)
  local copies, waits for them, and re-layouts  3.56 us (2%)
  other arithmetic  3.35 us (2%)
    all_to_all x4, starting transfers between devices, in_plane(): return lax.all_to_all(x, PLANE, 0, 0, tiled=True)  30.3 us
    ppermute x1, waiting for transfers between devices, shards(): round_in = lax.ppermute(halfway, 'z', [(0, 1)])  20.7 us
    all_to_all x4, waiting for transfers between devices, in_plane(): return lax.all_to_all(x, PLANE, 0, 0, tiled=True)  18.6 us
    ppermute x6, waiting for transfers between devices, swap(): return lax.ppermute(x, axis, [(0, 1), (1, 0)])  18.5 us
    pallas_call x1, Pallas kernels, shards(): call(attention_kernel, (array(rows, 256), array(rows - WINDOW, 256, dtype...  18.2 us
    pallas_call x2, Pallas kernels, project(): pl.pallas_call(functools.partial(project_kernel, halves), out_shape=(out,...  12 us
    pallas_call x2, Pallas kernels, grad_part(): pl.pallas_call(functools.partial(grad_far_kernel if rest else grad_near_k...  11.2 us
    pallas_call x1, Pallas kernels, shards(): call(own_kernel, (array(rows - WINDOW, 256, dtype=f32), array(rows, 256,...  10.4 us
  transfers between devices with their start and end apart: 18, of which 7 were waited for; matrix products, arithmetic and copies ran while one was open for 0% of the time, Pallas kernels for 21%

profile of v4, /device:TPU:36, one launch (start us, length us, event | category | flops | bytes accessed | tf_op | source)
XLA Modules:
  0.0 170.2 jit_solution(416403625292261194)
XLA Ops:
  0.6 0.1 collective-permute-start.1
  0.7 1.3 collective-permute-start
  2.0 2.7 %shard_map.84 = bf16[8,272,256]{2,1,0:T(8,128)(2,1)} custom-call(bf16[256,768]{1,0:T(8,128)(2,1)} %q_ref.3, bf16[256,768]{1,0:T(8,128)(2,1)} %k_ref.1, bf16[256,768]{1,0:T(8,128)(2,1)} %v_ref.1), custom_call_target="tpu_custom_call" | custom-call | tf_op jit(solution)/shard_map/pallas_call | solution.py:600
  4.7 7.4 %all-to-all-start = ((bf16[8,272,256]{2,1,0:T(8,128)(2,1)}), bf16[8,272,256]{2,1,0:T(8,128)(2,1)S(1)}, u32[]{:S(2)}, u32[]{:S(2)}) async-start(bf16[8,272,256]{2,1,0:T(8,128)(2,1)} %shard_map.84), calls=%async_computation | async-start | bytes 2228224 | tf_op jit(solution)/shard_map/all_to_all | solution.py:559
  12.1 0.6 pad_add_fusion.order_ref
  12.8 0.0 collective-permute-done.1.b_ref
  12.8 5.3 %shard_map.85.after_ref.start = f32[768,256]{1,0:T(8,128)} custom-call(s32[4]{0:T(128)} %pad_add_fusion.order_ref, bf16[256,1536]{1,0:T(8,128)(2,1)} %a_ref.1, bf16[256,1536]{1,0:T(8,128)(2,1)} %collective-permute-done.1.b_ref, bf16[768,6144]{1,0:T(8,128)(2,1)} %w_ref.7), custom_call_target="tpu_custom_call" | custom-call | tf_op jit(solution)/shard_map/pallas_call | solution.py:487
  18.1 3.3 %collective-permute-done.a_ref = bf16[256,1536]{1,0:T(8,128)(2,1)S(1)} collective-permute-done((bf16[256,1536]{1,0:T(8,128)(2,1)}, bf16[256,1536]{1,0:T(8,128)(2,1)S(1)}, u32[]{:S(2)}, u32[]{:S(2)}) %collective-permute-start) | collective-permute-done | bytes 786464 | tf_op jit(solution)/shard_map/ppermute | solution.py:551
  21.4 0.0 collective-permute-start.5
  21.4 2.4 %collective-permute-done.5.b_ref = bf16[256,1536]{1,0:T(8,128)(2,1)} collective-permute-done((bf16[256,1536]{1,0:T(8,128)(2,1)S(1)}, bf16[256,1536]{1,0:T(8,128)(2,1)}, u32[]{:S(2)}, u32[]{:S(2)}) %collective-permute-start.5) | collective-permute-done | bytes 786464 | tf_op jit(solution)/shard_map/ppermute | solution.py:551
  23.8 5.9 %shard_map.87 = bf16[8,256,256]{2,1,0:T(8,128)(2,1)} custom-call(s32[4]{0:T(128)} %pad_add_fusion.order_ref, bf16[256,1536]{1,0:T(8,128)(2,1)} %copy-done.8, bf16[256,1536]{1,0:T(8,128)(2,1)} %collective-permute-done.5.b_ref, bf16[768,6144]{1,0:T(8,128)(2,1)} %w_ref.7, f32[768,256]{1,0:T(8,128)} %shard_map.85.after_ref.start, bf16[256,768]{1,0:T(8,128)(2,1)} %q_ref.3), custom_call_target="tpu_custom_call" | custom-call | tf_op jit(solution)/shard_map/pallas_call | solution.py:487
  29.7 3.2 %all-to-all-done.x_ref = bf16[8,272,256]{2,1,0:T(8,128)(2,1)S(1)} async-done(((bf16[8,272,256]{2,1,0:T(8,128)(2,1)}), bf16[8,272,256]{2,1,0:T(8,128)(2,1)S(1)}, u32[]{:S(2)}, u32[]{:S(2)}) %all-to-all-start) | async-done | bytes 1114144 | tf_op jit(solution)/shard_map/all_to_all | solution.py:559
  32.9 9.2 %all-to-all-start.1 = ((bf16[8,256,256]{2,1,0:T(8,128)(2,1)}), bf16[8,256,256]{2,1,0:T(8,128)(2,1)}, u32[]{:S(2)}, u32[]{:S(2)}) async-start(bf16[8,256,256]{2,1,0:T(8,128)(2,1)} %shard_map.87), calls=%async_computation.1 | async-start | bytes 2097152 | tf_op jit(solution)/shard_map/all_to_all | solution.py:559
  42.1 0.3 shard_map.86
  42.5 0.0 copy-start.7
  42.5 3.8 %collective-permute-start.2 = (bf16[1312,256]{1,0:T(8,128)(2,1)S(1)}, bf16[1312,256]{1,0:T(8,128)(2,1)S(1)}, u32[]{:S(2)}, u32[]{:S(2)}) collective-permute-start(bf16[1312,256]{1,0:T(8,128)(2,1)S(1)} %get-tuple-element.27), channel_id=1, source_target_pairs={{0,32},{32,64},{64,96},{1,33},{33,65},{65,97},{2,34},{34,66},{66,9... | collective-permute-start | bytes 2015240 | tf_op jit(solution)/shard_map/ppermute | solution.py:555
  46.3 0.7 collective-permute-start.4
  47.0 3.0 %collective-permute-start.3 = (bf16[528,256]{1,0:T(8,128)(2,1)S(1)}, bf16[528,256]{1,0:T(8,128)(2,1)S(1)}, u32[]{:S(2)}, u32[]{:S(2)}) collective-permute-start(bf16[528,256]{1,0:T(8,128)(2,1)S(1)} %get-tuple-element.26.own_ref), channel_id=1, source_target_pairs={{0,64},{32,96},{1,65},{33,97},{2,66},{34,98},{3,67},{35,99},{4,68}... | collective-permute-start | bytes 811016 | tf_op jit(solution)/shard_map/ppermute | solution.py:555
  50.0 6.9 %all-to-all-done.1 = bf16[8,256,256]{2,1,0:T(8,128)(2,1)} async-done(((bf16[8,256,256]{2,1,0:T(8,128)(2,1)}), bf16[8,256,256]{2,1,0:T(8,128)(2,1)}, u32[]{:S(2)}, u32[]{:S(2)}) %all-to-all-start.1) | async-done | bytes 1048608 | tf_op jit(solution)/shard_map/all_to_all | solution.py:559
  56.8 10.4 %shard_map.88 = (f32[1024,256]{1,0:T(8,128)}, f32[2048,256]{1,0:T(8,128)}) custom-call(bf16[8,272,256]{2,1,0:T(8,128)(2,1)} %copy-done, bf16[2048,256]{1,0:T(8,128)(2,1)} %bitcast.5.pair_ref), custom_call_target="tpu_custom_call" | custom-call | tf_op jit(solution)/shard_map/pallas_call | solution.py:623
  67.2 0.0 collective-permute-done.4.far3_ref
  67.3 0.0 collective-permute-done.3.far2_ref
  67.3 0.0 copy-start.13
  67.3 0.0 collective-permute-done.2.near_ref
  67.3 0.0 copy-start.11
  67.3 0.7 copy-done.12
  68.0 0.1 copy-done.13
  68.0 0.2 copy-done.11
  68.3 18.2 %shard_map.89 = (bf16[2048,256]{1,0:T(8,128)(2,1)}, f32[1024,256]{1,0:T(8,128)}, f32[512,256]{1,0:T(8,128)}, bf16[1312,256]{1,0:T(8,128)(2,1)}, bf16[528,256]{1,0:T(8,128)(2,1)}, /*index=5*/bf16[528,256]{1,0:T(8,128)(2,1)}) custom-call(s32[1]{0:T(128)} %bitcast.4.z_ref, bf16[8,272,256]{2,1,0:T(8,128)(2,1)} %copy-done, bf16[528,256]{1,0:T(8,128)(2,1)} %copy-done.7, ...), custom_call_target="tpu_custom_call" | custom-call | tf_op jit(solution)/shard_map/pallas_call | solution.py:633
  86.5 6.3 %all-to-all-start.2 = ((bf16[8,256,256]{2,1,0:T(8,128)(2,1)}), bf16[8,256,256]{2,1,0:T(8,128)(2,1)S(1)}, u32[]{:S(2)}, u32[]{:S(2)}) async-start(bf16[8,256,256]{2,1,0:T(8,128)(2,1)} %bitcast.7), calls=%async_computation.2 | async-start | bytes 2097152 | tf_op jit(solution)/shard_map/all_to_all | solution.py:559
  92.9 2.0 %collective-permute-start.6 = (bf16[1312,256]{1,0:T(8,128)(2,1)}, bf16[1312,256]{1,0:T(8,128)(2,1)S(1)}, u32[]{:S(2)}, u32[]{:S(2)}) collective-permute-start(bf16[1312,256]{1,0:T(8,128)(2,1)} %get-tuple-element.34), channel_id=1, source_target_pairs={{32,0},{64,32},{96,64},{33,1},{65,33},{97,65},{34,2},{66,34},{98,6... | collective-permute-start | bytes 2015240 | tf_op jit(solution)/shard_map/ppermute | solution.py:555
  94.9 0.7 collective-permute-start.9
  95.6 0.7 collective-permute-start.7
  96.3 0.7 collective-permute-start.8
  97.0 1.3 collective-permute-start.10
  98.3 20.7 %collective-permute-done.10.round_ref = bf16[528,256]{1,0:T(8,128)(2,1)S(1)} collective-permute-done((bf16[528,256]{1,0:T(8,128)(2,1)S(1)}, bf16[528,256]{1,0:T(8,128)(2,1)S(1)}, u32[]{:S(2)}, u32[]{:S(2)}) %collective-permute-start.10) | collective-permute-done | bytes 270368 | tf_op jit(solution)/shard_map/ppermute | solution.py:674
  119.0 1.6 copy-done.4
  120.5 1.9 %shard_map.90.refs_0_ = bf16[8,272,256]{2,1,0:T(8,128)(2,1)} custom-call(f32[2048,256]{1,0:T(8,128)S(1)} %copy-done.4, f32[1024,256]{1,0:T(8,128)S(1)} %copy-done.5, f32[512,256]{1,0:T(8,128)S(1)} %copy-done.6, bf16[1312,256]{1,0:T(8,128)(2,1)S(1)} %collective-permute-done.6.back1_ref, bf16[528,256]{1,0:T(8,128)(2,1)S(1)} %collective-permute-done.7.back2_ref, ...), custom_call_target="tpu_custom_call" | custom-call | tf_op jit(solution)/shard_map/pallas_call | solution.py:676
  122.4 1.0 copy-done.1
  123.4 5.8 %shard_map.91 = (bf16[256,1536]{1,0:T(8,128)(2,1)}, bf16[256,1536]{1,0:T(8,128)(2,1)}) custom-call(s32[4]{0:T(128)} %pad_add_fusion.order_ref, bf16[8,256,256]{2,1,0:T(8,128)(2,1)} %copy-done.1, bf16[768,6144]{1,0:T(8,128)(2,1)} %w_ref.7, bf16[8,272,256]{2,1,0:T(8,128)(2,1)} %shard_map.90.refs_0_), custom_call_target="tpu_custom_call" | custom-call | tf_op jit(solution)/shard_map/pallas_call | solution.py:532
  129.2 7.4 %all-to-all-start.3 = ((bf16[8,272,256]{2,1,0:T(8,128)(2,1)}), bf16[8,272,256]{2,1,0:T(8,128)(2,1)}, u32[]{:S(2)}, u32[]{:S(2)}) async-start(bf16[8,272,256]{2,1,0:T(8,128)(2,1)} %shard_map.90.refs_0_), calls=%async_computation.3 | async-start | bytes 2228224 | tf_op jit(solution)/shard_map/all_to_all | solution.py:559
  136.5 0.2 add_convert_fusion.1
  136.7 6.3 %shard_map.92 = (bf16[256,1536]{1,0:T(8,128)(2,1)}, bf16[256,1536]{1,0:T(8,128)(2,1)}) custom-call(s32[4]{0:T(128)} %pad_add_fusion.order_ref, bf16[8,256,256]{2,1,0:T(8,128)(2,1)} %copy-done.1, bf16[768,6144]{1,0:T(8,128)(2,1)} %w_ref.7, bf16[8,272,256]{2,1,0:T(8,128)(2,1)} %shard_map.90.refs_0_), custom_call_target="tpu_custom_call" | custom-call | tf_op jit(solution)/shard_map/pallas_call | solution.py:532
  143.0 0.9 collective-permute-start.13
  143.9 8.5 %all-to-all-done.3.x_ref = bf16[8,272,256]{2,1,0:T(8,128)(2,1)} async-done(((bf16[8,272,256]{2,1,0:T(8,128)(2,1)}), bf16[8,272,256]{2,1,0:T(8,128)(2,1)}, u32[]{:S(2)}, u32[]{:S(2)}) %all-to-all-start.3) | async-done | bytes 1114144 | tf_op jit(solution)/shard_map/all_to_all | solution.py:559
  152.4 2.5 %shard_map.93 = (bf16[256,768]{1,0:T(8,128)(2,1)}, bf16[256,768]{1,0:T(8,128)(2,1)}, bf16[256,768]{1,0:T(8,128)(2,1)}) custom-call(bf16[8,256,256]{2,1,0:T(8,128)(2,1)S(1)} %copy-done.2, bf16[8,272,256]{2,1,0:T(8,128)(2,1)} %all-to-all-done.3.x_ref), custom_call_target="tpu_custom_call" | custom-call | tf_op jit(solution)/shard_map/pallas_call | solution.py:689
  154.9 12.8 %collective-permute-done.13 = bf16[256,1536]{1,0:T(8,128)(2,1)} collective-permute-done((bf16[256,1536]{1,0:T(8,128)(2,1)S(1)}, bf16[256,1536]{1,0:T(8,128)(2,1)}, u32[]{:S(2)}, u32[]{:S(2)}) %collective-permute-start.13) | collective-permute-done | bytes 786464 | tf_op jit(solution)/shard_map/ppermute | solution.py:551
  167.7 2.5 %add_convert_fusion = bf16[256,1536]{1,0:T(8,128)(2,1)} fusion(bf16[256,1536]{1,0:T(8,128)(2,1)} %collective-permute-done.13, bf16[256,1536]{1,0:T(8,128)(2,1)} %collective-permute-done.12, bf16[256,1536]{1,0:T(8,128)(2,1)S(1)} %copy-done.9), kind=kLoop, calls=%fused_computation | loop fusion | flops 2359296 | bytes 3145728 | tf_op jit(solution)/shard_map/convert_element_type | solution.py:585
  (31 shorter events, 0.1 us)
Async XLA Ops:
  0.6 12.1 %collective-permute-start.1 = (bf16[256,1536]{1,0:T(8,128)(2,1)}, bf16[256,1536]{1,0:T(8,128)(2,1)}, u32[]{:S(2)}, u32[]{:S(2)}) collective-permute-start(bf16[256,1536]{1,0:T(8,128)(2,1)} %a_ref.1), channel_id=1, source_target_pairs={{0,1},{1,0},{2,3},{3,2},{4,5},{5,4},{6,7},{7,6},{8,9},{9,8},{10,11... | collective-permute-start | bytes 2359304 | tf_op jit(solution)/shard_map/ppermute | solution.py:551
  0.7 20.6 %collective-permute-start = (bf16[256,1536]{1,0:T(8,128)(2,1)}, bf16[256,1536]{1,0:T(8,128)(2,1)S(1)}, u32[]{:S(2)}, u32[]{:S(2)}) collective-permute-start(bf16[256,1536]{1,0:T(8,128)(2,1)} %a_ref.1), channel_id=1, source_target_pairs={{0,2},{2,0},{1,3},{3,1},{4,6},{6,4},{5,7},{7,5},{8,10},{10,8},{9,1... | collective-permute-start | bytes 2359304 | tf_op jit(solution)/shard_map/ppermute | solution.py:551
  4.7 28.2 %all-to-all-start = ((bf16[8,272,256]{2,1,0:T(8,128)(2,1)}), bf16[8,272,256]{2,1,0:T(8,128)(2,1)S(1)}, u32[]{:S(2)}, u32[]{:S(2)}) async-start(bf16[8,272,256]{2,1,0:T(8,128)(2,1)} %shard_map.84), calls=%async_computation | async-start | bytes 2228224 | tf_op jit(solution)/shard_map/all_to_all | solution.py:559
  21.4 2.4 %copy-start.8 = (bf16[256,1536]{1,0:T(8,128)(2,1)}, bf16[256,1536]{1,0:T(8,128)(2,1)S(1)}, u32[]{:S(2)}) copy-start(bf16[256,1536]{1,0:T(8,128)(2,1)S(1)} %collective-permute-done.a_ref) | copy-start | bytes 2359300
  21.4 2.4 %collective-permute-start.5 = (bf16[256,1536]{1,0:T(8,128)(2,1)S(1)}, bf16[256,1536]{1,0:T(8,128)(2,1)}, u32[]{:S(2)}, u32[]{:S(2)}) collective-permute-start(bf16[256,1536]{1,0:T(8,128)(2,1)S(1)} %collective-permute-done.a_ref), channel_id=1, source_target_pairs={{0,1},{1,0},{2,3},{3,2},{4,5},{5,4},{6,7},{7,6},{8,9},{9,8},{10,11... | collective-permute-start | bytes 2359304 | tf_op jit(solution)/shard_map/ppermute | solution.py:551
  29.7 12.4 %copy-start.3 = (f32[768,256]{1,0:T(8,128)S(1)}, f32[768,256]{1,0:T(8,128)}, u32[]{:S(2)}) copy-start(f32[768,256]{1,0:T(8,128)} %shard_map.85.after_ref.start) | copy-start | bytes 2359300
  32.9 9.5 %copy-start = (bf16[8,272,256]{2,1,0:T(8,128)(2,1)}, bf16[8,272,256]{2,1,0:T(8,128)(2,1)S(1)}, u32[]{:S(2)}) copy-start(bf16[8,272,256]{2,1,0:T(8,128)(2,1)S(1)} %all-to-all-done.x_ref) | copy-start | bytes 3342340
  32.9 23.9 %all-to-all-start.1 = ((bf16[8,256,256]{2,1,0:T(8,128)(2,1)}), bf16[8,256,256]{2,1,0:T(8,128)(2,1)}, u32[]{:S(2)}, u32[]{:S(2)}) async-start(bf16[8,256,256]{2,1,0:T(8,128)(2,1)} %shard_map.87), calls=%async_computation.1 | async-start | bytes 2097152 | tf_op jit(solution)/shard_map/all_to_all | solution.py:559
  42.5 24.8 %copy-start.7 = (bf16[528,256]{1,0:T(8,128)(2,1)}, bf16[528,256]{1,0:T(8,128)(2,1)S(1)}, u32[]{:S(2)}) copy-start(bf16[528,256]{1,0:T(8,128)(2,1)S(1)} %get-tuple-element.26.own_ref) | copy-start | bytes 811012
  42.5 24.8 %collective-permute-start.2 = (bf16[1312,256]{1,0:T(8,128)(2,1)S(1)}, bf16[1312,256]{1,0:T(8,128)(2,1)S(1)}, u32[]{:S(2)}, u32[]{:S(2)}) collective-permute-start(bf16[1312,256]{1,0:T(8,128)(2,1)S(1)} %get-tuple-element.27), channel_id=1, source_target_pairs={{0,32},{32,64},{64,96},{1,33},{33,65},{65,97},{2,34},{34,66},{66,9... | collective-permute-start | bytes 2015240 | tf_op jit(solution)/shard_map/ppermute | solution.py:555
  46.3 20.9 %collective-permute-start.4 = (bf16[528,256]{1,0:T(8,128)(2,1)S(1)}, bf16[528,256]{1,0:T(8,128)(2,1)S(1)}, u32[]{:S(2)}, u32[]{:S(2)}) collective-permute-start(bf16[528,256]{1,0:T(8,128)(2,1)S(1)} %get-tuple-element.26.own_ref), channel_id=1, source_target_pairs={{0,96},{1,97},{2,98},{3,99},{4,100},{5,101},{6,102},{7,103},{8,104... | collective-permute-start | bytes 811016 | tf_op jit(solution)/shard_map/ppermute | solution.py:555
  47.0 20.3 %collective-permute-start.3 = (bf16[528,256]{1,0:T(8,128)(2,1)S(1)}, bf16[528,256]{1,0:T(8,128)(2,1)S(1)}, u32[]{:S(2)}, u32[]{:S(2)}) collective-permute-start(bf16[528,256]{1,0:T(8,128)(2,1)S(1)} %get-tuple-element.26.own_ref), channel_id=1, source_target_pairs={{0,64},{32,96},{1,65},{33,97},{2,66},{34,98},{3,67},{35,99},{4,68}... | collective-permute-start | bytes 811016 | tf_op jit(solution)/shard_map/ppermute | solution.py:555
  67.2 0.7 copy-start.12
  67.3 0.8 copy-start.13
  67.3 1.0 copy-start.11
  86.5 8.4 %copy-start.14 = (bf16[528,256]{1,0:T(8,128)(2,1)S(1)}, bf16[528,256]{1,0:T(8,128)(2,1)}, u32[]{:S(2)}) copy-start(bf16[528,256]{1,0:T(8,128)(2,1)} %get-tuple-element.35) | copy-start | bytes 811012
  86.5 32.4 %copy-start.5 = (f32[1024,256]{1,0:T(8,128)S(1)}, f32[1024,256]{1,0:T(8,128)}, u32[]{:S(2)}) copy-start(f32[1024,256]{1,0:T(8,128)} %get-tuple-element.32.fine_ref) | copy-start | bytes 3145732
  86.5 32.4 %copy-start.6 = (f32[512,256]{1,0:T(8,128)S(1)}, f32[512,256]{1,0:T(8,128)}, u32[]{:S(2)}) copy-start(f32[512,256]{1,0:T(8,128)} %get-tuple-element.33.coarse_ref) | copy-start | bytes 1572868
  86.5 35.9 %all-to-all-start.2 = ((bf16[8,256,256]{2,1,0:T(8,128)(2,1)}), bf16[8,256,256]{2,1,0:T(8,128)(2,1)S(1)}, u32[]{:S(2)}, u32[]{:S(2)}) async-start(bf16[8,256,256]{2,1,0:T(8,128)(2,1)} %bitcast.7), calls=%async_computation.2 | async-start | bytes 2097152 | tf_op jit(solution)/shard_map/all_to_all | solution.py:559
  92.9 26.1 %collective-permute-start.6 = (bf16[1312,256]{1,0:T(8,128)(2,1)}, bf16[1312,256]{1,0:T(8,128)(2,1)S(1)}, u32[]{:S(2)}, u32[]{:S(2)}) collective-permute-start(bf16[1312,256]{1,0:T(8,128)(2,1)} %get-tuple-element.34), channel_id=1, source_target_pairs={{32,0},{64,32},{96,64},{33,1},{65,33},{97,65},{34,2},{66,34},{98,6... | collective-permute-start | bytes 2015240 | tf_op jit(solution)/shard_map/ppermute | solution.py:555
  94.9 2.1 %collective-permute-start.9 = (bf16[528,256]{1,0:T(8,128)(2,1)S(1)}, bf16[528,256]{1,0:T(8,128)(2,1)S(1)}, u32[]{:S(2)}, u32[]{:S(2)}) collective-permute-start(bf16[528,256]{1,0:T(8,128)(2,1)S(1)} %copy-done.14), channel_id=1, source_target_pairs={{96,0},{97,1},{98,2},{99,3},{100,4},{101,5},{102,6},{103,7},{104,8... | collective-permute-start | bytes 811016 | tf_op jit(solution)/shard_map/ppermute | solution.py:671
  95.6 2.7 %collective-permute-start.7 = (bf16[528,256]{1,0:T(8,128)(2,1)S(1)}, bf16[528,256]{1,0:T(8,128)(2,1)S(1)}, u32[]{:S(2)}, u32[]{:S(2)}) collective-permute-start(bf16[528,256]{1,0:T(8,128)(2,1)S(1)} %copy-done.14), channel_id=1, source_target_pairs={{64,0},{65,1},{66,2},{67,3},{68,4},{69,5},{70,6},{71,7},{72,8},{73... | collective-permute-start | bytes 811016 | tf_op jit(solution)/shard_map/ppermute | solution.py:673
  96.3 2.0 %collective-permute-start.8 = (bf16[528,256]{1,0:T(8,128)(2,1)}, bf16[528,256]{1,0:T(8,128)(2,1)S(1)}, u32[]{:S(2)}, u32[]{:S(2)}) collective-permute-start(bf16[528,256]{1,0:T(8,128)(2,1)} %get-tuple-element.36), channel_id=1, source_target_pairs={{96,0},{97,1},{98,2},{99,3},{100,4},{101,5},{102,6},{103,7},{104,8... | collective-permute-start | bytes 811016 | tf_op jit(solution)/shard_map/ppermute | solution.py:555
  97.0 22.0 %collective-permute-start.10 = (bf16[528,256]{1,0:T(8,128)(2,1)S(1)}, bf16[528,256]{1,0:T(8,128)(2,1)S(1)}, u32[]{:S(2)}, u32[]{:S(2)}) collective-permute-start(bf16[528,256]{1,0:T(8,128)(2,1)S(1)} %collective-permute-done.9), channel_id=1, source_target_pairs={{0,32},{1,33},{2,34},{3,35},{4,36},{5,37},{6,38},{7,39},{8,40},{9,... | collective-permute-start | bytes 811016 | tf_op jit(solution)/shard_map/ppermute | solution.py:674
  119.0 1.6 copy-start.4
  122.4 1.0 copy-start.1
  129.2 7.4 %copy-start.10 = (bf16[256,1536]{1,0:T(8,128)(2,1)S(1)}, bf16[256,1536]{1,0:T(8,128)(2,1)}, u32[]{:S(2)}) copy-start(bf16[256,1536]{1,0:T(8,128)(2,1)} %get-tuple-element.37) | copy-start | bytes 2359300
  129.2 7.4 %collective-permute-start.11 = (bf16[256,1536]{1,0:T(8,128)(2,1)}, bf16[256,1536]{1,0:T(8,128)(2,1)S(1)}, u32[]{:S(2)}, u32[]{:S(2)}) collective-permute-start(bf16[256,1536]{1,0:T(8,128)(2,1)} %get-tuple-element.38), channel_id=1, source_target_pairs={{0,1},{1,0},{2,3},{3,2},{4,5},{5,4},{6,7},{7,6},{8,9},{9,8},{10,11... | collective-permute-start | bytes 2359304 | tf_op jit(solution)/shard_map/ppermute | solution.py:551
  129.2 23.2 %all-to-all-start.3 = ((bf16[8,272,256]{2,1,0:T(8,128)(2,1)}), bf16[8,272,256]{2,1,0:T(8,128)(2,1)}, u32[]{:S(2)}, u32[]{:S(2)}) async-start(bf16[8,272,256]{2,1,0:T(8,128)(2,1)} %shard_map.90.refs_0_), calls=%async_computation.3 | async-start | bytes 2228224 | tf_op jit(solution)/shard_map/all_to_all | solution.py:559
  136.7 15.7 %copy-start.2 = (bf16[8,256,256]{2,1,0:T(8,128)(2,1)S(1)}, bf16[8,256,256]{2,1,0:T(8,128)(2,1)}, u32[]{:S(2)}) copy-start(bf16[8,256,256]{2,1,0:T(8,128)(2,1)} %copy-done.1) | copy-start | bytes 3145732
  143.0 24.7 %copy-start.9 = (bf16[256,1536]{1,0:T(8,128)(2,1)S(1)}, bf16[256,1536]{1,0:T(8,128)(2,1)}, u32[]{:S(2)}) copy-start(bf16[256,1536]{1,0:T(8,128)(2,1)} %get-tuple-element.40) | copy-start | bytes 2359300
  143.0 11.9 %collective-permute-start.12 = (bf16[256,1536]{1,0:T(8,128)(2,1)}, bf16[256,1536]{1,0:T(8,128)(2,1)}, u32[]{:S(2)}, u32[]{:S(2)}) collective-permute-start(bf16[256,1536]{1,0:T(8,128)(2,1)} %get-tuple-element.41), channel_id=1, source_target_pairs={{0,1},{1,0},{2,3},{3,2},{4,5},{5,4},{6,7},{7,6},{8,9},{9,8},{10,11... | collective-permute-start | bytes 2359304 | tf_op jit(solution)/shard_map/ppermute | solution.py:551
  143.0 24.7 %collective-permute-start.13 = (bf16[256,1536]{1,0:T(8,128)(2,1)S(1)}, bf16[256,1536]{1,0:T(8,128)(2,1)}, u32[]{:S(2)}, u32[]{:S(2)}) collective-permute-start(bf16[256,1536]{1,0:T(8,128)(2,1)S(1)} %add_convert_fusion.1), channel_id=1, source_target_pairs={{0,2},{2,0},{1,3},{3,1},{4,6},{6,4},{5,7},{7,5},{8,10},{10,8},{9,1... | collective-permute-start | bytes 2359304 | tf_op jit(solution)/shard_map/ppermute | solution.py:551

commit v5 on v3

--- a/solution.py
+++ b/solution.py
@@ -187,59 +187,40 @@
     sums_ref[:, 128:256] = dv[...]
 
 
-def attention_kernel(
+def short_kernel(
     z_ref,
-    x_ref,
     own_ref,
     near_ref,
     far2_ref,
     far3_ref,
     pair_ref,
-    part_ref,
-    attn_ref,
-    fine_ref,
+    after_ref,
     coarse_ref,
-    back1_ref,
     back2_ref,
     back3_ref,
-    kx,
-    vx,
-    kxt,
-    vxt,
+    slot1_ref,
+    high,
+    low,
+    high_t,
+    low_t,
+    query_high,
+    query_low,
     kc,
     vc,
     kct,
     vct,
     pq,
     gp,
-    dkx,
-    dvx,
     dkc,
     dvc,
-    high_t,
-    low_t,
-    high,
-    low,
-    query_high,
-    query_low,
 ):
+    del after_ref
     z = z_ref[0]
     rows = pair_ref.shape[0]
-    tokens = rows // PLANE_DEVS
     coarse = rows // SHORT
     half = WINDOW // SHORT
     step = BLOCK // SHORT
     reach = WINDOW // BLOCK
-
-    kx[0:WINDOW, :] = near_ref[0:WINDOW, 0:128]
-    vx[0:WINDOW, :] = near_ref[0:WINDOW, 128:256]
-    for slot in range((rows - WINDOW) // tokens):
-        at = WINDOW + slot * tokens
-        kx[at : at + tokens, :] = x_ref[slot, 0:tokens, 0:128]
-        vx[at : at + tokens, :] = x_ref[slot, 0:tokens, 128:256]
-
-    transposed(kx, kxt, rows // BLOCK)
-    transposed(vx, vxt, rows // BLOCK)
 
     tails = [
         near_ref[WINDOW - TAIL : WINDOW, :],
@@ -325,20 +306,63 @@
     coarse_ref[:, 0:128] = dkc[0:coarse, :]
     coarse_ref[:, 128:256] = dvc[0:coarse, :]
 
+    first = iota((TAIL, HEAD_DIM), 0) == 0
+    for cols, short in ((slice(0, 128), dkc), (slice(128, 256), dvc)):
+        high[0:half, cols], low[0:half, cols] = split(short[2 * coarse - half : 2 * coarse, :])
+        above = jnp.where(first, short[0:TAIL, :], 0.0)
+        high[half:, cols], low[half:, cols] = split(above)
+    slot1_ref[:, 0:128] = dkc[coarse : coarse + half + TAIL, :].astype(bf16)
+    slot1_ref[:, 128:256] = dvc[coarse : coarse + half + TAIL, :].astype(bf16)
+    for slot, ref in ((2, back2_ref), (3, back3_ref)):
+        at = slot * coarse
+        above = at - coarse
+        for cols, short in ((slice(0, 128), dkc), (slice(128, 256), dvc)):
+            ref[0:coarse, cols] = short[at : at + coarse, :].astype(bf16)
+            row = jnp.where(first, short[above : above + TAIL, :], 0.0)
+            ref[coarse : coarse + TAIL, cols] = row.astype(bf16)
+
+
+def attention_kernel(
+    z_ref,
+    x_ref,
+    near_ref,
+    pair_ref,
+    slot1_ref,
+    high,
+    low,
+    high_t,
+    low_t,
+    query_high,
+    query_low,
+    attn_ref,
+    fine_ref,
+    back1_ref,
+    kx,
+    vx,
+    kxt,
+    vxt,
+    dkx,
+    dvx,
+):
+    z = z_ref[0]
+    rows = pair_ref.shape[0]
+    tokens = rows // PLANE_DEVS
+    step = BLOCK // SHORT
+    reach = WINDOW // BLOCK
+    base = WINDOW + TAIL
+
+    kx[0:WINDOW, :] = near_ref[0:WINDOW, 0:128]
+    vx[0:WINDOW, :] = near_ref[0:WINDOW, 128:256]
+    for slot in range((rows - WINDOW) // tokens):
+        at = WINDOW + slot * tokens
+        kx[at : at + tokens, :] = x_ref[slot, 0:tokens, 0:128]
+        vx[at : at + tokens, :] = x_ref[slot, 0:tokens, 128:256]
+
+    transposed(kx, kxt, rows // BLOCK)
+    transposed(vx, vxt, rows // BLOCK)
+
     dkx[...] = jnp.zeros_like(dkx)
     dvx[...] = jnp.zeros_like(dvx)
-
-    def short_out(block):
-        pair = pl.multiple_of(block // 2 * (2 * step), 2 * step)
-        shape = (2 * step, BLOCK)
-        spread = ones_where(iota(shape, 0) == block % 2 * step + iota(shape, 1) // SHORT)
-        short_t = dot(high_t[:, pl.ds(pair, 2 * step)], spread)
-        return short_t + dot(low_t[:, pl.ds(pair, 2 * step)], spread)
-
-    def short_query_grad(block):
-        below = pl.ds(pl.multiple_of(block * step, step), step + TAIL)
-        spread = dot(spreading(), query_high[below, :]) + dot(spreading(), query_low[below, :])
-        return spread * (1.0 / SHORT)
 
     def window(block, carry):
         at = pl.multiple_of(block * BLOCK, BLOCK)
@@ -347,22 +371,16 @@
         out_t, query_grad = window_block(
             at, pair_ref[here, 0:128], pair_ref[here, 128:256], biases, kx, vx, kxt, vxt, dkx, dvx
         )
-        attn_ref[here, 0:128] = (out_t + short_out(block)).T.astype(bf16)
-        attn_ref[here, 128:256] = (query_grad + short_query_grad(block)).astype(bf16)
-        late = pl.ds(pl.multiple_of(WINDOW + at, BLOCK), BLOCK)
-        attn_ref[late, 0:128] = (part_ref[here, 0:128] + short_out(block + reach).T).astype(bf16)
-        attn_ref[late, 128:256] = (part_ref[here, 128:256] + short_query_grad(block + reach)).astype(bf16)
+        attn_ref[here, 0:128] = (out_t + short_out(block, high_t, low_t)).T.astype(bf16)
+        attn_ref[here, 128:256] = (
+            query_grad + short_query_grad(block, query_high, query_low)
+        ).astype(bf16)
         return carry
 
     lax.fori_loop(0, reach, window, 0, unroll=4)
     fine_ref[:, 0:128] = dkx[WINDOW:, :] * SCALE
     fine_ref[:, 128:256] = dvx[WINDOW:, :]
 
-    first = iota((TAIL, HEAD_DIM), 0) == 0
-    for cols, short in ((slice(0, 128), dkc), (slice(128, 256), dvc)):
-        high[0:half, cols], low[0:half, cols] = split(short[2 * coarse - half : 2 * coarse, :])
-        above = jnp.where(first, short[0:TAIL, :], 0.0)
-        high[half:, cols], low[half:, cols] = split(above)
     taken = spreading()
     for piece in range(reach):
         at = piece * BLOCK
@@ -376,18 +394,41 @@
         back1_ref[at : at + BLOCK, 128:256] = (
             dvx[at : at + BLOCK, :] + spread[:, 128:256]
         ).astype(bf16)
+    first = iota((TAIL, HEAD_DIM), 0) == 0
     query_row = jnp.where(first, query_high[0:TAIL, :].astype(f32), 0.0).astype(bf16)
     back1_ref[WINDOW:base, 0:128] = query_row
     back1_ref[WINDOW:base, 128:256] = query_row
-    back1_ref[base:, 0:128] = dkc[coarse : coarse + half + TAIL, :].astype(bf16)
-    back1_ref[base:, 128:256] = dvc[coarse : coarse + half + TAIL, :].astype(bf16)
-    for slot, ref in ((2, back2_ref), (3, back3_ref)):
-        at = slot * coarse
-        above = at - coarse
-        for cols, short in ((slice(0, 128), dkc), (slice(128, 256), dvc)):
-            ref[0:coarse, cols] = short[at : at + coarse, :].astype(bf16)
-            row = jnp.where(first, short[above : above + TAIL, :], 0.0)
-            ref[coarse : coarse + TAIL, cols] = row.astype(bf16)
+    back1_ref[base:, :] = slot1_ref[...]
+
+
+def short_out(block, high_t, low_t):
+    step = BLOCK // SHORT
+    pair = pl.multiple_of(block // 2 * (2 * step), 2 * step)
+    shape = (2 * step, BLOCK)
+    spread = ones_where(iota(shape, 0) == block % 2 * step + iota(shape, 1) // SHORT)
+    short_t = dot(high_t[:, pl.ds(pair, 2 * step)], spread)
+    return short_t + dot(low_t[:, pl.ds(pair, 2 * step)], spread)
+
+
+def short_query_grad(block, high, low):
+    step = BLOCK // SHORT
+    below = pl.ds(pl.multiple_of(block * step, step), step + TAIL)
+    spread = dot(spreading(), high[below, :]) + dot(spreading(), low[below, :])
+    return spread * (1.0 / SHORT)
+
+
+def late_kernel(early_ref, part_ref, high_t, low_t, high, low, after2_ref, after3_ref, attn_ref):
+    del after2_ref, after3_ref
+    count = early_ref.shape[0]
+    attn_ref[0:count, :] = early_ref[...]
+    for block in range(part_ref.shape[0] // BLOCK):
+        here = slice(block * BLOCK, (block + 1) * BLOCK)
+        late = slice(count + block * BLOCK, count + (block + 1) * BLOCK)
+        place = block + count // BLOCK
+        attn_ref[late, 0:128] = (part_ref[here, 0:128] + short_out(place, high_t, low_t).T).astype(bf16)
+        attn_ref[late, 128:256] = (
+            part_ref[here, 128:256] + short_query_grad(place, high, low)
+        ).astype(bf16)
 
 
 def finish_kernel(
@@ -630,46 +671,49 @@
         + [pltpu.VMEM((HEAD_DIM, rows), bf16)] * 2
         + [pltpu.VMEM((rows, HEAD_DIM), f32)] * 2,
     )(own, pair)
-    attn, fine, short, back1, back2, back3 = call(
-        attention_kernel,
+    scalar = pl.BlockSpec(memory_space=pltpu.SMEM)
+    half = WINDOW // SHORT + TAIL
+    short, back2, back3, *tables = call(
+        short_kernel,
         (
-            array(rows, 256),
-            array(rows - WINDOW, 256, dtype=f32),
             array(coarse, 256, dtype=f32),
-            array(near_rows, 256),
             array(coarse + TAIL, 256),
             array(coarse + TAIL, 256),
+            array(half, 256),
+            array(half, 256),
+            array(half, 256),
+            array(HEAD_DIM, coarse),
+            array(HEAD_DIM, coarse),
+            array(coarse + TAIL, HEAD_DIM),
+            array(coarse + TAIL, HEAD_DIM),
         ),
-        62,
-        in_specs=[pl.BlockSpec(memory_space=pltpu.SMEM)] + [whole] * 7,
-        out_specs=[whole] * 6,
-        scratch_shapes=[
-            pltpu.VMEM((rows, HEAD_DIM), bf16),
-            pltpu.VMEM((rows, HEAD_DIM), bf16),
-            pltpu.VMEM((HEAD_DIM, rows), bf16),
-            pltpu.VMEM((HEAD_DIM, rows), bf16),
-            pltpu.VMEM((total, HEAD_DIM), bf16),
-            pltpu.VMEM((total, HEAD_DIM), bf16),
-            pltpu.VMEM((HEAD_DIM, total), bf16),
-            pltpu.VMEM((HEAD_DIM, total), bf16),
-            pltpu.VMEM((coarse, HEAD_DIM), bf16),
-            pltpu.VMEM((coarse, HEAD_DIM), bf16),
-            pltpu.VMEM((rows, HEAD_DIM), f32),
-            pltpu.VMEM((rows, HEAD_DIM), f32),
-            pltpu.VMEM((total, HEAD_DIM), f32),
-            pltpu.VMEM((total, HEAD_DIM), f32),
-            pltpu.VMEM((HEAD_DIM, coarse), bf16),
-            pltpu.VMEM((HEAD_DIM, coarse), bf16),
-            pltpu.VMEM((WINDOW // SHORT + TAIL, 256), bf16),
-            pltpu.VMEM((WINDOW // SHORT + TAIL, 256), bf16),
-            pltpu.VMEM((coarse + TAIL, HEAD_DIM), bf16),
-            pltpu.VMEM((coarse + TAIL, HEAD_DIM), bf16),
-        ],
-    )(z, own, far, near_in, far2_in, far3_in, pair, part)
-
-    back1_in = planes_up(back1, -1)
+        56,
+        in_specs=[scalar] + [whole] * 5 + [in_place],
+        out_specs=[whole] * 10,
+        scratch_shapes=[pltpu.VMEM((total, HEAD_DIM), bf16)] * 2
+        + [pltpu.VMEM((HEAD_DIM, total), bf16)] * 2
+        + [pltpu.VMEM((coarse, HEAD_DIM), bf16)] * 2
+        + [pltpu.VMEM((total, HEAD_DIM), f32)] * 2,
+    )(z, far, near_in, far2_in, far3_in, pair, part)
     back2_in = planes_up(back2, -2)
     back3_in = planes_up(back3, -3)
+    early, fine, back1 = call(
+        attention_kernel,
+        (array(rows - WINDOW, 256), array(rows - WINDOW, 256, dtype=f32), array(near_rows, 256)),
+        56,
+        in_specs=[scalar] + [whole] * 10,
+        out_specs=[whole] * 3,
+        scratch_shapes=[pltpu.VMEM((rows, HEAD_DIM), bf16)] * 2
+        + [pltpu.VMEM((HEAD_DIM, rows), bf16)] * 2
+        + [pltpu.VMEM((rows, HEAD_DIM), f32)] * 2,
+    )(z, own, near_in, pair, *tables)
+    back1_in = planes_up(back1, -1)
+    attn = call(
+        late_kernel,
+        array(rows, 256),
+        56,
+        in_specs=[whole] * 6 + [in_place] * 2,
+    )(early, part, *tables[3:], back2_in, back3_in)
     attn_in = in_plane(attn.reshape(PLANE_DEVS, tokens, 256))
     finished = call(
         finish_kernel,

time: 170 us -> 176 us (1.035); the launches traced: 169 us -> 173 us
  waiting for transfers between devices: 58.1 us -> 51 us
  Pallas kernels: 59 us -> 63.8 us
  starting transfers between devices: 44 us -> 48.2 us
  local copies, waits for them, and re-layouts: 3.57 us -> 5.57 us
    ppermute x6, waiting for transfers between devices: 20.9 us -> 14 us  [planes_up(): lax.ppermute(x, 'z', [(i, i + by) for i in range(PLANES) if 0 <= i + by <...]
    pallas_call x1 -> x3, Pallas kernels: 18.2 us -> 23.1 us  [the longest x1 10.9 us: shards(): call(attention_kernel, (array(rows - WINDOW, 256), array(rows - WINDOW, 2...]
    ppermute x6, starting transfers between devices: 11.5 us -> 15.7 us  [planes_up(): lax.ppermute(x, 'z', [(i, i + by) for i in range(PLANES) if 0 <= i + by <...]
    unnamed x30 -> x38, local copies, waits for them, and re-layouts: 3.57 us -> 5.57 us
  transfers between devices with their start and end apart: 16 -> 16, of which waited for: 7 -> 7; matrix products, arithmetic and copies ran while one was open for 0% -> 0% of each run, Pallas kernels for 21% -> 27%
where the time goes in v5:
time: 176 us; the launch traced here: 173 us
  Pallas kernels  63.8 us (36%)
  waiting for transfers between devices  51 us (29%)
  starting transfers between devices  48.2 us (27%)
  local copies, waits for them, and re-layouts  5.57 us (3%)
  other arithmetic  3.34 us (2%)
    all_to_all x4, starting transfers between devices, in_plane(): return lax.all_to_all(x, PLANE, 0, 0, tiled=True)  30.3 us
    ppermute x6, waiting for transfers between devices, swap(): return lax.ppermute(x, axis, [(0, 1), (1, 0)])  18.6 us
    all_to_all x4, waiting for transfers between devices, in_plane(): return lax.all_to_all(x, PLANE, 0, 0, tiled=True)  18.5 us
    ppermute x6, starting transfers between devices, planes_up(): lax.ppermute(x, 'z', [(i, i + by) for i in range(PLANES) if 0 <= i + by <...  15.7 us
    ppermute x6, waiting for transfers between devices, planes_up(): lax.ppermute(x, 'z', [(i, i + by) for i in range(PLANES) if 0 <= i + by <...  14 us
    pallas_call x2, Pallas kernels, project(): pl.pallas_call(functools.partial(project_kernel, halves), out_shape=(out,...  11.8 us
    pallas_call x2, Pallas kernels, grad_part(): pl.pallas_call(functools.partial(grad_far_kernel if rest else grad_near_k...  11.1 us
    pallas_call x1, Pallas kernels, shards(): call(attention_kernel, (array(rows - WINDOW, 256), array(rows - WINDOW, 2...  10.9 us
  transfers between devices with their start and end apart: 16, of which 7 were waited for; matrix products, arithmetic and copies ran while one was open for 0% of the time, Pallas kernels for 27%

profile of v5, /device:TPU:36, one launch (start us, length us, event | category | flops | bytes accessed | tf_op | source)
XLA Modules:
  0.0 172.8 jit_solution(12195804720143608160)
XLA Ops:
  0.6 0.1 collective-permute-start.1
  0.7 1.3 collective-permute-start
  2.0 2.7 %shard_map.84 = bf16[8,272,256]{2,1,0:T(8,128)(2,1)} custom-call(bf16[256,768]{1,0:T(8,128)(2,1)} %q_ref.3, bf16[256,768]{1,0:T(8,128)(2,1)} %k_ref.1, bf16[256,768]{1,0:T(8,128)(2,1)} %v_ref.1), custom_call_target="tpu_custom_call" | custom-call | tf_op jit(solution)/shard_map/pallas_call | solution.py:641
  4.7 7.4 %all-to-all-start = ((bf16[8,272,256]{2,1,0:T(8,128)(2,1)}), bf16[8,272,256]{2,1,0:T(8,128)(2,1)S(1)}, u32[]{:S(2)}, u32[]{:S(2)}) async-start(bf16[8,272,256]{2,1,0:T(8,128)(2,1)} %shard_map.84), calls=%async_computation | async-start | bytes 2228224 | tf_op jit(solution)/shard_map/all_to_all | solution.py:600
  12.1 0.6 pad_add_fusion.order_ref
  12.7 0.0 collective-permute-done.1.b_ref
  12.7 5.3 %shard_map.85.after_ref.start = f32[768,256]{1,0:T(8,128)} custom-call(s32[4]{0:T(128)} %pad_add_fusion.order_ref, bf16[256,1536]{1,0:T(8,128)(2,1)} %a_ref.1, bf16[256,1536]{1,0:T(8,128)(2,1)} %collective-permute-done.1.b_ref, bf16[768,6144]{1,0:T(8,128)(2,1)} %w_ref.7), custom_call_target="tpu_custom_call" | custom-call | tf_op jit(solution)/shard_map/pallas_call | solution.py:528
  18.0 3.3 %collective-permute-done.a_ref = bf16[256,1536]{1,0:T(8,128)(2,1)S(1)} collective-permute-done((bf16[256,1536]{1,0:T(8,128)(2,1)}, bf16[256,1536]{1,0:T(8,128)(2,1)S(1)}, u32[]{:S(2)}, u32[]{:S(2)}) %collective-permute-start) | collective-permute-done | bytes 786464 | tf_op jit(solution)/shard_map/ppermute | solution.py:592
  21.4 2.4 %collective-permute-done.3.b_ref = bf16[256,1536]{1,0:T(8,128)(2,1)} collective-permute-done((bf16[256,1536]{1,0:T(8,128)(2,1)S(1)}, bf16[256,1536]{1,0:T(8,128)(2,1)}, u32[]{:S(2)}, u32[]{:S(2)}) %collective-permute-start.3) | collective-permute-done | bytes 786464 | tf_op jit(solution)/shard_map/ppermute | solution.py:592
  23.8 5.8 %shard_map.87 = bf16[8,256,256]{2,1,0:T(8,128)(2,1)} custom-call(s32[4]{0:T(128)} %pad_add_fusion.order_ref, bf16[256,1536]{1,0:T(8,128)(2,1)} %copy-done.13, bf16[256,1536]{1,0:T(8,128)(2,1)} %collective-permute-done.3.b_ref, bf16[768,6144]{1,0:T(8,128)(2,1)} %w_ref.7, f32[768,256]{1,0:T(8,128)} %shard_map.85.after_ref.start, bf16[256,768]{1,0:T(8,128)(2,1)} %q_ref.3), custom_call_target="tpu_custom_call" | custom-call | tf_op jit(solution)/shard_map/pallas_call | solution.py:528
  29.6 3.3 %all-to-all-done.x_ref = bf16[8,272,256]{2,1,0:T(8,128)(2,1)S(1)} async-done(((bf16[8,272,256]{2,1,0:T(8,128)(2,1)}), bf16[8,272,256]{2,1,0:T(8,128)(2,1)S(1)}, u32[]{:S(2)}, u32[]{:S(2)}) %all-to-all-start) | async-done | bytes 1114144 | tf_op jit(solution)/shard_map/all_to_all | solution.py:600
  32.9 9.2 %all-to-all-start.1 = ((bf16[8,256,256]{2,1,0:T(8,128)(2,1)}), bf16[8,256,256]{2,1,0:T(8,128)(2,1)}, u32[]{:S(2)}, u32[]{:S(2)}) async-start(bf16[8,256,256]{2,1,0:T(8,128)(2,1)} %shard_map.87), calls=%async_computation.1 | async-start | bytes 2097152 | tf_op jit(solution)/shard_map/all_to_all | solution.py:600
  42.1 0.3 shard_map.86
  42.5 0.0 copy-start.11
  42.5 3.8 %collective-permute-start.2 = (bf16[1312,256]{1,0:T(8,128)(2,1)S(1)}, bf16[1312,256]{1,0:T(8,128)(2,1)S(1)}, u32[]{:S(2)}, u32[]{:S(2)}) collective-permute-start(bf16[1312,256]{1,0:T(8,128)(2,1)S(1)} %get-tuple-element.33), channel_id=1, source_target_pairs={{0,32},{32,64},{64,96},{1,33},{33,65},{65,97},{2,34},{34,66},{66,9... | collective-permute-start | bytes 2015240 | tf_op jit(solution)/shard_map/ppermute | solution.py:596
  46.3 0.7 collective-permute-start.5
  47.0 3.2 %collective-permute-start.4 = (bf16[528,256]{1,0:T(8,128)(2,1)S(1)}, bf16[528,256]{1,0:T(8,128)(2,1)S(1)}, u32[]{:S(2)}, u32[]{:S(2)}) collective-permute-start(bf16[528,256]{1,0:T(8,128)(2,1)S(1)} %get-tuple-element.35.own_ref), channel_id=1, source_target_pairs={{0,64},{32,96},{1,65},{33,97},{2,66},{34,98},{3,67},{35,99},{4,68}... | collective-permute-start | bytes 811016 | tf_op jit(solution)/shard_map/ppermute | solution.py:596
  50.2 6.7 %all-to-all-done.1 = bf16[8,256,256]{2,1,0:T(8,128)(2,1)} async-done(((bf16[8,256,256]{2,1,0:T(8,128)(2,1)}), bf16[8,256,256]{2,1,0:T(8,128)(2,1)}, u32[]{:S(2)}, u32[]{:S(2)}) %all-to-all-start.1) | async-done | bytes 1048608 | tf_op jit(solution)/shard_map/all_to_all | solution.py:600
  56.9 10.5 %shard_map.88 = (f32[1024,256]{1,0:T(8,128)}, f32[2048,256]{1,0:T(8,128)}) custom-call(bf16[8,272,256]{2,1,0:T(8,128)(2,1)} %copy-done, bf16[2048,256]{1,0:T(8,128)(2,1)} %bitcast.5.pair_ref), custom_call_target="tpu_custom_call" | custom-call | tf_op jit(solution)/shard_map/pallas_call | solution.py:664
  67.4 0.0 copy-start.17
  67.4 0.0 copy-start.12
  67.4 0.7 copy-done.16
  68.1 0.1 copy-done.17
  68.2 0.2 copy-done.12
  68.4 9.2 %shard_map.89 = (f32[512,256]{1,0:T(8,128)}, bf16[528,256]{1,0:T(8,128)(2,1)}, bf16[528,256]{1,0:T(8,128)(2,1)}, bf16[272,256]{1,0:T(8,128)(2,1)}, bf16[272,256]...) custom-call(s32[1]{0:T(128)} %bitcast.4.z_ref, ...), custom_call_target="tpu_custom_call" | custom-call | tf_op jit(solution)/shard_map/pallas_call | solution.py:676
  77.6 1.3 collective-permute-start.6
  78.9 0.9 collective-permute-start.7
  79.8 10.9 %shard_map.90 = (bf16[1024,256]{1,0:T(8,128)(2,1)}, f32[1024,256]{1,0:T(8,128)}, bf16[1312,256]{1,0:T(8,128)(2,1)}) custom-call(s32[1]{0:T(128)} %bitcast.4.z_ref, bf16[8,272,256]{2,1,0:T(8,128)(2,1)} %copy-done, bf16[1312,256]{1,0:T(8,128)(2,1)} %copy-done.12, bf16[2048,256]{1,0:T(8,128)(2,1)} %bitcast.5.pair_ref, ...), custom_call_target="tpu_custom_call" | custom-call | tf_op jit(solution)/shard_map/pallas_call | solution.py:700
  90.7 0.0 copy-start.7
  90.8 0.7 copy-done.5
  91.4 0.1 copy-done.7
  91.5 3.0 %shard_map.91 = bf16[2048,256]{1,0:T(8,128)(2,1)} custom-call(bf16[1024,256]{1,0:T(8,128)(2,1)} %get-tuple-element.44.early_ref, f32[1024,256]{1,0:T(8,128)} %get-tuple-element.36.after_ref.part_ref, bf16[128,512]{1,0:T(8,128)(2,1)} %get-tuple-element.40.high_t, bf16[128,512]{1,0:T(8,128)(2,1)} %get-tuple-element.41.low_t, ...), custom_call_target="tpu_custom_call" | custom-call | tf_op jit(solution)/shard_map/pallas_call | solution.py:711
  94.5 6.3 %all-to-all-start.2 = ((bf16[8,256,256]{2,1,0:T(8,128)(2,1)}), bf16[8,256,256]{2,1,0:T(8,128)(2,1)S(1)}, u32[]{:S(2)}, u32[]{:S(2)}) async-start(bf16[8,256,256]{2,1,0:T(8,128)(2,1)} %bitcast.7), calls=%async_computation.2 | async-start | bytes 2097152 | tf_op jit(solution)/shard_map/all_to_all | solution.py:600
  100.8 5.8 %collective-permute-start.8 = (bf16[1312,256]{1,0:T(8,128)(2,1)S(1)}, bf16[1312,256]{1,0:T(8,128)(2,1)S(1)}, u32[]{:S(2)}, u32[]{:S(2)}) collective-permute-start(bf16[1312,256]{1,0:T(8,128)(2,1)S(1)} %copy-done.18), channel_id=1, source_target_pairs={{32,0},{64,32},{96,64},{33,1},{65,33},{97,65},{34,2},{66,34},{98,6... | collective-permute-start | bytes 2015240 | tf_op jit(solution)/shard_map/ppermute | solution.py:596
  106.7 13.9 %collective-permute-done.8.back1_ref = bf16[1312,256]{1,0:T(8,128)(2,1)S(1)} collective-permute-done((bf16[1312,256]{1,0:T(8,128)(2,1)S(1)}, bf16[1312,256]{1,0:T(8,128)(2,1)S(1)}, u32[]{:S(2)}, u32[]{:S(2)}) %collective-permute-start.8) | collective-permute-done | bytes 671776 | tf_op jit(solution)/shard_map/ppermute | solution.py:596
  120.7 1.6 copy-done.4
  122.2 1.2 copy-done.9
  123.5 1.8 %shard_map.92.refs_0_ = bf16[8,272,256]{2,1,0:T(8,128)(2,1)} custom-call(f32[2048,256]{1,0:T(8,128)S(1)} %copy-done.4, f32[1024,256]{1,0:T(8,128)S(1)} %copy-done.9, f32[512,256]{1,0:T(8,128)S(1)} %copy-done.10, bf16[1312,256]{1,0:T(8,128)(2,1)S(1)} %collective-permute-done.8.back1_ref, bf16[528,256]{1,0:T(8,128)(2,1)S(1)} %copy-done.6, ...), custom_call_target="tpu_custom_call" | custom-call | tf_op jit(solution)/shard_map/pallas_call | solution.py:718
  125.2 1.0 copy-done.1
  126.2 5.6 %shard_map.93 = (bf16[256,1536]{1,0:T(8,128)(2,1)}, bf16[256,1536]{1,0:T(8,128)(2,1)}) custom-call(s32[4]{0:T(128)} %pad_add_fusion.order_ref, bf16[8,256,256]{2,1,0:T(8,128)(2,1)} %copy-done.1, bf16[768,6144]{1,0:T(8,128)(2,1)} %w_ref.7, bf16[8,272,256]{2,1,0:T(8,128)(2,1)} %shard_map.92.refs_0_), custom_call_target="tpu_custom_call" | custom-call | tf_op jit(solution)/shard_map/pallas_call | solution.py:573
  131.8 7.4 %all-to-all-start.3 = ((bf16[8,272,256]{2,1,0:T(8,128)(2,1)}), bf16[8,272,256]{2,1,0:T(8,128)(2,1)}, u32[]{:S(2)}, u32[]{:S(2)}) async-start(bf16[8,272,256]{2,1,0:T(8,128)(2,1)} %shard_map.92.refs_0_), calls=%async_computation.3 | async-start | bytes 2228224 | tf_op jit(solution)/shard_map/all_to_all | solution.py:600
  139.1 0.2 add_convert_fusion.1
  139.3 6.2 %shard_map.94 = (bf16[256,1536]{1,0:T(8,128)(2,1)}, bf16[256,1536]{1,0:T(8,128)(2,1)}) custom-call(s32[4]{0:T(128)} %pad_add_fusion.order_ref, bf16[8,256,256]{2,1,0:T(8,128)(2,1)} %copy-done.1, bf16[768,6144]{1,0:T(8,128)(2,1)} %w_ref.7, bf16[8,272,256]{2,1,0:T(8,128)(2,1)} %shard_map.92.refs_0_), custom_call_target="tpu_custom_call" | custom-call | tf_op jit(solution)/shard_map/pallas_call | solution.py:573
  145.6 0.9 collective-permute-start.11
  146.5 8.5 %all-to-all-done.3.x_ref = bf16[8,272,256]{2,1,0:T(8,128)(2,1)} async-done(((bf16[8,272,256]{2,1,0:T(8,128)(2,1)}), bf16[8,272,256]{2,1,0:T(8,128)(2,1)}, u32[]{:S(2)}, u32[]{:S(2)}) %all-to-all-start.3) | async-done | bytes 1114144 | tf_op jit(solution)/shard_map/all_to_all | solution.py:600
  155.0 2.5 %shard_map.95 = (bf16[256,768]{1,0:T(8,128)(2,1)}, bf16[256,768]{1,0:T(8,128)(2,1)}, bf16[256,768]{1,0:T(8,128)(2,1)}) custom-call(bf16[8,256,256]{2,1,0:T(8,128)(2,1)S(1)} %copy-done.2, bf16[8,272,256]{2,1,0:T(8,128)(2,1)} %all-to-all-done.3.x_ref), custom_call_target="tpu_custom_call" | custom-call | tf_op jit(solution)/shard_map/pallas_call | solution.py:731
  157.5 12.8 %collective-permute-done.11 = bf16[256,1536]{1,0:T(8,128)(2,1)} collective-permute-done((bf16[256,1536]{1,0:T(8,128)(2,1)S(1)}, bf16[256,1536]{1,0:T(8,128)(2,1)}, u32[]{:S(2)}, u32[]{:S(2)}) %collective-permute-start.11) | collective-permute-done | bytes 786464 | tf_op jit(solution)/shard_map/ppermute | solution.py:592
  170.3 2.5 %add_convert_fusion = bf16[256,1536]{1,0:T(8,128)(2,1)} fusion(bf16[256,1536]{1,0:T(8,128)(2,1)} %collective-permute-done.11, bf16[256,1536]{1,0:T(8,128)(2,1)} %collective-permute-done.10, bf16[256,1536]{1,0:T(8,128)(2,1)S(1)} %copy-done.14), kind=kLoop, calls=%fused_computation | loop fusion | flops 2359296 | bytes 3145728 | tf_op jit(solution)/shard_map/convert_element_type | solution.py:626
  (37 shorter events, 0.1 us)
Async XLA Ops:
  0.6 12.1 %collective-permute-start.1 = (bf16[256,1536]{1,0:T(8,128)(2,1)}, bf16[256,1536]{1,0:T(8,128)(2,1)}, u32[]{:S(2)}, u32[]{:S(2)}) collective-permute-start(bf16[256,1536]{1,0:T(8,128)(2,1)} %a_ref.1), channel_id=1, source_target_pairs={{0,1},{1,0},{2,3},{3,2},{4,5},{5,4},{6,7},{7,6},{8,9},{9,8},{10,11... | collective-permute-start | bytes 2359304 | tf_op jit(solution)/shard_map/ppermute | solution.py:592
  0.7 20.6 %collective-permute-start = (bf16[256,1536]{1,0:T(8,128)(2,1)}, bf16[256,1536]{1,0:T(8,128)(2,1)S(1)}, u32[]{:S(2)}, u32[]{:S(2)}) collective-permute-start(bf16[256,1536]{1,0:T(8,128)(2,1)} %a_ref.1), channel_id=1, source_target_pairs={{0,2},{2,0},{1,3},{3,1},{4,6},{6,4},{5,7},{7,5},{8,10},{10,8},{9,1... | collective-permute-start | bytes 2359304 | tf_op jit(solution)/shard_map/ppermute | solution.py:592
  4.7 28.2 %all-to-all-start = ((bf16[8,272,256]{2,1,0:T(8,128)(2,1)}), bf16[8,272,256]{2,1,0:T(8,128)(2,1)S(1)}, u32[]{:S(2)}, u32[]{:S(2)}) async-start(bf16[8,272,256]{2,1,0:T(8,128)(2,1)} %shard_map.84), calls=%async_computation | async-start | bytes 2228224 | tf_op jit(solution)/shard_map/all_to_all | solution.py:600
  21.4 2.4 %copy-start.13 = (bf16[256,1536]{1,0:T(8,128)(2,1)}, bf16[256,1536]{1,0:T(8,128)(2,1)S(1)}, u32[]{:S(2)}) copy-start(bf16[256,1536]{1,0:T(8,128)(2,1)S(1)} %collective-permute-done.a_ref) | copy-start | bytes 2359300
  21.4 2.4 %collective-permute-start.3 = (bf16[256,1536]{1,0:T(8,128)(2,1)S(1)}, bf16[256,1536]{1,0:T(8,128)(2,1)}, u32[]{:S(2)}, u32[]{:S(2)}) collective-permute-start(bf16[256,1536]{1,0:T(8,128)(2,1)S(1)} %collective-permute-done.a_ref), channel_id=1, source_target_pairs={{0,1},{1,0},{2,3},{3,2},{4,5},{5,4},{6,7},{7,6},{8,9},{9,8},{10,11... | collective-permute-start | bytes 2359304 | tf_op jit(solution)/shard_map/ppermute | solution.py:592
  29.6 12.5 %copy-start.3 = (f32[768,256]{1,0:T(8,128)S(1)}, f32[768,256]{1,0:T(8,128)}, u32[]{:S(2)}) copy-start(f32[768,256]{1,0:T(8,128)} %shard_map.85.after_ref.start) | copy-start | bytes 2359300
  32.9 9.5 %copy-start = (bf16[8,272,256]{2,1,0:T(8,128)(2,1)}, bf16[8,272,256]{2,1,0:T(8,128)(2,1)S(1)}, u32[]{:S(2)}) copy-start(bf16[8,272,256]{2,1,0:T(8,128)(2,1)S(1)} %all-to-all-done.x_ref) | copy-start | bytes 3342340
  32.9 23.9 %all-to-all-start.1 = ((bf16[8,256,256]{2,1,0:T(8,128)(2,1)}), bf16[8,256,256]{2,1,0:T(8,128)(2,1)}, u32[]{:S(2)}, u32[]{:S(2)}) async-start(bf16[8,256,256]{2,1,0:T(8,128)(2,1)} %shard_map.87), calls=%async_computation.1 | async-start | bytes 2097152 | tf_op jit(solution)/shard_map/all_to_all | solution.py:600
  42.5 25.0 %copy-start.11 = (bf16[528,256]{1,0:T(8,128)(2,1)}, bf16[528,256]{1,0:T(8,128)(2,1)S(1)}, u32[]{:S(2)}) copy-start(bf16[528,256]{1,0:T(8,128)(2,1)S(1)} %get-tuple-element.35.own_ref) | copy-start | bytes 811012
  42.5 24.9 %collective-permute-start.2 = (bf16[1312,256]{1,0:T(8,128)(2,1)S(1)}, bf16[1312,256]{1,0:T(8,128)(2,1)S(1)}, u32[]{:S(2)}, u32[]{:S(2)}) collective-permute-start(bf16[1312,256]{1,0:T(8,128)(2,1)S(1)} %get-tuple-element.33), channel_id=1, source_target_pairs={{0,32},{32,64},{64,96},{1,33},{33,65},{65,97},{2,34},{34,66},{66,9... | collective-permute-start | bytes 2015240 | tf_op jit(solution)/shard_map/ppermute | solution.py:596
  46.3 21.1 %collective-permute-start.5 = (bf16[528,256]{1,0:T(8,128)(2,1)S(1)}, bf16[528,256]{1,0:T(8,128)(2,1)S(1)}, u32[]{:S(2)}, u32[]{:S(2)}) collective-permute-start(bf16[528,256]{1,0:T(8,128)(2,1)S(1)} %get-tuple-element.35.own_ref), channel_id=1, source_target_pairs={{0,96},{1,97},{2,98},{3,99},{4,100},{5,101},{6,102},{7,103},{8,104... | collective-permute-start | bytes 811016 | tf_op jit(solution)/shard_map/ppermute | solution.py:596
  47.0 20.4 %collective-permute-start.4 = (bf16[528,256]{1,0:T(8,128)(2,1)S(1)}, bf16[528,256]{1,0:T(8,128)(2,1)S(1)}, u32[]{:S(2)}, u32[]{:S(2)}) collective-permute-start(bf16[528,256]{1,0:T(8,128)(2,1)S(1)} %get-tuple-element.35.own_ref), channel_id=1, source_target_pairs={{0,64},{32,96},{1,65},{33,97},{2,66},{34,98},{3,67},{35,99},{4,68}... | collective-permute-start | bytes 811016 | tf_op jit(solution)/shard_map/ppermute | solution.py:596
  67.4 0.7 copy-start.16
  67.4 0.8 copy-start.17
  67.4 1.0 copy-start.12
  77.6 13.1 %collective-permute-start.6 = (bf16[528,256]{1,0:T(8,128)(2,1)}, bf16[528,256]{1,0:T(8,128)(2,1)S(1)}, u32[]{:S(2)}, u32[]{:S(2)}) collective-permute-start(bf16[528,256]{1,0:T(8,128)(2,1)} %get-tuple-element.45), channel_id=1, source_target_pairs={{64,0},{96,32},{65,1},{97,33},{66,2},{98,34},{67,3},{99,35},{68,4}... | collective-permute-start | bytes 811016 | tf_op jit(solution)/shard_map/ppermute | solution.py:596
  78.9 11.8 %collective-permute-start.7 = (bf16[528,256]{1,0:T(8,128)(2,1)}, bf16[528,256]{1,0:T(8,128)(2,1)S(1)}, u32[]{:S(2)}, u32[]{:S(2)}) collective-permute-start(bf16[528,256]{1,0:T(8,128)(2,1)} %get-tuple-element.46), channel_id=1, source_target_pairs={{96,0},{97,1},{98,2},{99,3},{100,4},{101,5},{102,6},{103,7},{104,8... | collective-permute-start | bytes 811016 | tf_op jit(solution)/shard_map/ppermute | solution.py:596
  90.7 0.7 copy-start.5
  90.7 0.8 copy-start.7
  94.5 6.3 %copy-start.18 = (bf16[1312,256]{1,0:T(8,128)(2,1)S(1)}, bf16[1312,256]{1,0:T(8,128)(2,1)}, u32[]{:S(2)}) copy-start(bf16[1312,256]{1,0:T(8,128)(2,1)} %get-tuple-element.50) | copy-start | bytes 2015236
  94.5 26.1 %copy-start.6 = (bf16[528,256]{1,0:T(8,128)(2,1)S(1)}, bf16[528,256]{1,0:T(8,128)(2,1)}, u32[]{:S(2)}) copy-start(bf16[528,256]{1,0:T(8,128)(2,1)} %copy-done.5) | copy-start | bytes 811012
  94.5 26.1 %copy-start.8 = (bf16[528,256]{1,0:T(8,128)(2,1)S(1)}, bf16[528,256]{1,0:T(8,128)(2,1)}, u32[]{:S(2)}) copy-start(bf16[528,256]{1,0:T(8,128)(2,1)} %copy-done.7) | copy-start | bytes 811012
  94.5 26.1 %copy-start.10 = (f32[512,256]{1,0:T(8,128)S(1)}, f32[512,256]{1,0:T(8,128)}, u32[]{:S(2)}) copy-start(f32[512,256]{1,0:T(8,128)} %get-tuple-element.49.coarse_ref) | copy-start | bytes 1572868
  94.5 30.7 %all-to-all-start.2 = ((bf16[8,256,256]{2,1,0:T(8,128)(2,1)}), bf16[8,256,256]{2,1,0:T(8,128)(2,1)S(1)}, u32[]{:S(2)}, u32[]{:S(2)}) async-start(bf16[8,256,256]{2,1,0:T(8,128)(2,1)} %bitcast.7), calls=%async_computation.2 | async-start | bytes 2097152 | tf_op jit(solution)/shard_map/all_to_all | solution.py:600
  100.8 19.8 %collective-permute-start.8 = (bf16[1312,256]{1,0:T(8,128)(2,1)S(1)}, bf16[1312,256]{1,0:T(8,128)(2,1)S(1)}, u32[]{:S(2)}, u32[]{:S(2)}) collective-permute-start(bf16[1312,256]{1,0:T(8,128)(2,1)S(1)} %copy-done.18), channel_id=1, source_target_pairs={{32,0},{64,32},{96,64},{33,1},{65,33},{97,65},{34,2},{66,34},{98,6... | collective-permute-start | bytes 2015240 | tf_op jit(solution)/shard_map/ppermute | solution.py:596
  120.6 1.6 copy-start.4
  122.2 1.2 copy-start.9
  125.2 1.0 copy-start.1
  131.8 7.4 %copy-start.15 = (bf16[256,1536]{1,0:T(8,128)(2,1)S(1)}, bf16[256,1536]{1,0:T(8,128)(2,1)}, u32[]{:S(2)}) copy-start(bf16[256,1536]{1,0:T(8,128)(2,1)} %get-tuple-element.51) | copy-start | bytes 2359300
  131.8 7.4 %collective-permute-start.9 = (bf16[256,1536]{1,0:T(8,128)(2,1)}, bf16[256,1536]{1,0:T(8,128)(2,1)S(1)}, u32[]{:S(2)}, u32[]{:S(2)}) collective-permute-start(bf16[256,1536]{1,0:T(8,128)(2,1)} %get-tuple-element.52), channel_id=1, source_target_pairs={{0,1},{1,0},{2,3},{3,2},{4,5},{5,4},{6,7},{7,6},{8,9},{9,8},{10,11... | collective-permute-start | bytes 2359304 | tf_op jit(solution)/shard_map/ppermute | solution.py:592
  131.8 23.2 %all-to-all-start.3 = ((bf16[8,272,256]{2,1,0:T(8,128)(2,1)}), bf16[8,272,256]{2,1,0:T(8,128)(2,1)}, u32[]{:S(2)}, u32[]{:S(2)}) async-start(bf16[8,272,256]{2,1,0:T(8,128)(2,1)} %shard_map.92.refs_0_), calls=%async_computation.3 | async-start | bytes 2228224 | tf_op jit(solution)/shard_map/all_to_all | solution.py:600
  139.3 15.7 %copy-start.2 = (bf16[8,256,256]{2,1,0:T(8,128)(2,1)S(1)}, bf16[8,256,256]{2,1,0:T(8,128)(2,1)}, u32[]{:S(2)}) copy-start(bf16[8,256,256]{2,1,0:T(8,128)(2,1)} %copy-done.1) | copy-start | bytes 3145732
  145.6 24.7 %copy-start.14 = (bf16[256,1536]{1,0:T(8,128)(2,1)S(1)}, bf16[256,1536]{1,0:T(8,128)(2,1)}, u32[]{:S(2)}) copy-start(bf16[256,1536]{1,0:T(8,128)(2,1)} %get-tuple-element.54) | copy-start | bytes 2359300
  145.6 11.9 %collective-permute-start.10 = (bf16[256,1536]{1,0:T(8,128)(2,1)}, bf16[256,1536]{1,0:T(8,128)(2,1)}, u32[]{:S(2)}, u32[]{:S(2)}) collective-permute-start(bf16[256,1536]{1,0:T(8,128)(2,1)} %get-tuple-element.55), channel_id=1, source_target_pairs={{0,1},{1,0},{2,3},{3,2},{4,5},{5,4},{6,7},{7,6},{8,9},{9,8},{10,11... | collective-permute-start | bytes 2359304 | tf_op jit(solution)/shard_map/ppermute | solution.py:592
  145.6 24.7 %collective-permute-start.11 = (bf16[256,1536]{1,0:T(8,128)(2,1)S(1)}, bf16[256,1536]{1,0:T(8,128)(2,1)}, u32[]{:S(2)}, u32[]{:S(2)}) collective-permute-start(bf16[256,1536]{1,0:T(8,128)(2,1)S(1)} %add_convert_fusion.1), channel_id=1, source_target_pairs={{0,2},{2,0},{1,3},{3,1},{4,6},{6,4},{5,7},{7,5},{8,10},{10,8},{9,1... | collective-permute-start | bytes 2359304 | tf_op jit(solution)/shard_map/ppermute | solution.py:592

commit v6 on v3

--- a/solution.py
+++ b/solution.py
@@ -391,8 +391,9 @@
 
 
 def finish_kernel(
-    sums_ref, fine_ref, coarse_ref, back1_ref, back2_ref, back3_ref, out_ref, high, low
+    sums_ref, fine_ref, coarse_ref, back1_ref, back2_ref, back3_ref, after_ref, out_ref, high, low
 ):
+    del after_ref
     rows = sums_ref.shape[0]
     tokens = rows // PLANE_DEVS
     coarse = rows // SHORT
@@ -574,15 +575,9 @@
     return start, grad_part((far, both), blocks, out_weight, (start, q_proj))
 
 
-def projected(attn, out_weight, width, blocks, after):
-    def share(last, attn):
-        send, keep = project(attn, blocks, last, out_weight, width, after)
-        return keep.astype(f32) + swap(send, "c").astype(f32)
-
-    part = share(3, attn).astype(bf16)
-    part, attn = lax.optimization_barrier((part, attn))
-    far = swap(part, "xl")
-    return (share(1, attn) + far.astype(f32)).astype(bf16)
+def projected(attn, out_weight, width, blocks, last, after):
+    send, keep = project(attn, blocks, last, out_weight, width, after)
+    return keep.astype(f32) + swap(send, "c").astype(f32), keep
 
 
 def shards(q_proj, k_proj, v_proj, out_weight, out_grad):
@@ -671,18 +666,20 @@
     back2_in = planes_up(back2, -2)
     back3_in = planes_up(back3, -3)
     attn_in = in_plane(attn.reshape(PLANE_DEVS, tokens, 256))
+    width = out_grad.shape[1]
+    part, kept = projected(attn_in, out_weight, width, blocks, 1, ())
     finished = call(
         finish_kernel,
         array(PLANE_DEVS, tokens + TAIL, 256),
         32,
+        in_specs=[whole] * 6 + [in_place],
         scratch_shapes=[
             pltpu.VMEM((coarse + 2 * TAIL, 256), bf16),
             pltpu.VMEM((coarse + 2 * TAIL, 256), bf16),
         ],
-    )(sums, fine, short, back1_in, back2_in, back3_in)
-    mixed_out = projected(
-        attn_in, out_weight, out_grad.shape[1], blocks, (finished,)
-    )
+    )(sums, fine, short, back1_in, back2_in, back3_in, kept)
+    other, _ = projected(attn_in, out_weight, width, blocks, 3, (finished,))
+    mixed_out = (part + swap(other.astype(bf16), "xl").astype(f32)).astype(bf16)
     returned = in_plane(finished)
     grads = call(unpack_kernel, (array(tokens, cols),) * 3, 16)(attn_in, returned)
     return (mixed_out, *grads)

time: 170 us -> 173 us (1.018)
  local copies, waits for them, and re-layouts: 3.57 us -> 7.99 us
  other arithmetic: 3.32 us -> 5.43 us
  Pallas kernels: 59 us -> 57 us
  waiting for transfers between devices: 58.1 us -> 56.1 us
    ppermute x6, waiting for transfers between devices: 20.9 us -> 4.2 us  [planes_up(): lax.ppermute(x, 'z', [(i, i + by) for i in range(PLANES) if 0 <= i + by <...]
    all_to_all x4, waiting for transfers between devices: 18.6 us -> 32 us  [in_plane(): return lax.all_to_all(x, PLANE, 0, 0, tiled=True)]
    unnamed x30 -> x32, local copies, waits for them, and re-layouts: 3.57 us -> 7.99 us
    convert_element_type x2, other arithmetic: 2.73 us -> 4.82 us  [shards(): mixed_out = (part + swap(other.astype(bf16), 'xl').astype(f32)).astype(bf16)]
  transfers between devices with their start and end apart: 16 -> 16, of which waited for: 7 -> 8; matrix products, arithmetic and copies ran while one was open for 0% -> 2% of each run, Pallas kernels for 21% -> 18%
where the time goes in v6:
time: 173 us; the launch traced here: 172 us
  Pallas kernels  57 us (33%)
  waiting for transfers between devices  56.1 us (32%)
  starting transfers between devices  44.5 us (26%)
  local copies, waits for them, and re-layouts  7.99 us (5%)
  other arithmetic  5.43 us (3%)
    all_to_all x4, waiting for transfers between devices, in_plane(): return lax.all_to_all(x, PLANE, 0, 0, tiled=True)  32 us
    all_to_all x4, starting transfers between devices, in_plane(): return lax.all_to_all(x, PLANE, 0, 0, tiled=True)  30.2 us
    ppermute x6, waiting for transfers between devices, swap(): return lax.ppermute(x, axis, [(0, 1), (1, 0)])  19.9 us
    pallas_call x1, Pallas kernels, shards(): call(attention_kernel, (array(rows, 256), array(rows - WINDOW, 256, dtype...  18.1 us
    ppermute x6, starting transfers between devices, planes_up(): lax.ppermute(x, 'z', [(i, i + by) for i in range(PLANES) if 0 <= i + by <...  12.2 us
    pallas_call x2, Pallas kernels, project(): pl.pallas_call(functools.partial(project_kernel, halves), out_shape=(out,...  11.4 us
    pallas_call x2, Pallas kernels, grad_part(): pl.pallas_call(functools.partial(grad_far_kernel if rest else grad_near_k...  11.1 us
    pallas_call x1, Pallas kernels, shards(): call(own_kernel, (array(rows - WINDOW, 256, dtype=f32), array(rows, 256,...  10.4 us
  transfers between devices with their start and end apart: 16, of which 8 were waited for; matrix products, arithmetic and copies ran while one was open for 2% of the time, Pallas kernels for 18%

profile of v6, /device:TPU:36, one launch (start us, length us, event | category | flops | bytes accessed | tf_op | source)
XLA Modules:
  0.0 171.8 jit_solution(7697089117051535909)
XLA Ops:
  0.6 0.1 collective-permute-start.1
  0.7 1.3 collective-permute-start
  2.0 2.7 %shard_map.84 = bf16[8,272,256]{2,1,0:T(8,128)(2,1)} custom-call(bf16[256,768]{1,0:T(8,128)(2,1)} %q_ref.3, bf16[256,768]{1,0:T(8,128)(2,1)} %k_ref.1, bf16[256,768]{1,0:T(8,128)(2,1)} %v_ref.1), custom_call_target="tpu_custom_call" | custom-call | tf_op jit(solution)/shard_map/pallas_call | solution.py:595
  4.7 7.4 %all-to-all-start = ((bf16[8,272,256]{2,1,0:T(8,128)(2,1)}), bf16[8,272,256]{2,1,0:T(8,128)(2,1)S(1)}, u32[]{:S(2)}, u32[]{:S(2)}) async-start(bf16[8,272,256]{2,1,0:T(8,128)(2,1)} %shard_map.84), calls=%async_computation | async-start | bytes 2228224 | tf_op jit(solution)/shard_map/all_to_all | solution.py:560
  12.1 0.6 pad_add_fusion.order_ref
  12.7 0.0 collective-permute-done.1.b_ref
  12.7 5.3 %shard_map.85.after_ref.start = f32[768,256]{1,0:T(8,128)} custom-call(s32[4]{0:T(128)} %pad_add_fusion.order_ref, bf16[256,1536]{1,0:T(8,128)(2,1)} %a_ref.1, bf16[256,1536]{1,0:T(8,128)(2,1)} %collective-permute-done.1.b_ref, bf16[768,6144]{1,0:T(8,128)(2,1)} %w_ref.7), custom_call_target="tpu_custom_call" | custom-call | tf_op jit(solution)/shard_map/pallas_call | solution.py:488
  18.0 3.3 %collective-permute-done.a_ref = bf16[256,1536]{1,0:T(8,128)(2,1)S(1)} collective-permute-done((bf16[256,1536]{1,0:T(8,128)(2,1)}, bf16[256,1536]{1,0:T(8,128)(2,1)S(1)}, u32[]{:S(2)}, u32[]{:S(2)}) %collective-permute-start) | collective-permute-done | bytes 786464 | tf_op jit(solution)/shard_map/ppermute | solution.py:552
  21.4 0.0 collective-permute-start.5
  21.4 2.4 %collective-permute-done.5.b_ref = bf16[256,1536]{1,0:T(8,128)(2,1)} collective-permute-done((bf16[256,1536]{1,0:T(8,128)(2,1)S(1)}, bf16[256,1536]{1,0:T(8,128)(2,1)}, u32[]{:S(2)}, u32[]{:S(2)}) %collective-permute-start.5) | collective-permute-done | bytes 786464 | tf_op jit(solution)/shard_map/ppermute | solution.py:552
  23.8 5.9 %shard_map.87 = bf16[8,256,256]{2,1,0:T(8,128)(2,1)} custom-call(s32[4]{0:T(128)} %pad_add_fusion.order_ref, bf16[256,1536]{1,0:T(8,128)(2,1)} %copy-done.11, bf16[256,1536]{1,0:T(8,128)(2,1)} %collective-permute-done.5.b_ref, bf16[768,6144]{1,0:T(8,128)(2,1)} %w_ref.7, f32[768,256]{1,0:T(8,128)} %shard_map.85.after_ref.start, bf16[256,768]{1,0:T(8,128)(2,1)} %q_ref.3), custom_call_target="tpu_custom_call" | custom-call | tf_op jit(solution)/shard_map/pallas_call | solution.py:488
  29.6 3.3 %all-to-all-done.x_ref = bf16[8,272,256]{2,1,0:T(8,128)(2,1)S(1)} async-done(((bf16[8,272,256]{2,1,0:T(8,128)(2,1)}), bf16[8,272,256]{2,1,0:T(8,128)(2,1)S(1)}, u32[]{:S(2)}, u32[]{:S(2)}) %all-to-all-start) | async-done | bytes 1114144 | tf_op jit(solution)/shard_map/all_to_all | solution.py:560
  32.9 9.2 %all-to-all-start.1 = ((bf16[8,256,256]{2,1,0:T(8,128)(2,1)}), bf16[8,256,256]{2,1,0:T(8,128)(2,1)}, u32[]{:S(2)}, u32[]{:S(2)}) async-start(bf16[8,256,256]{2,1,0:T(8,128)(2,1)} %shard_map.87), calls=%async_computation.1 | async-start | bytes 2097152 | tf_op jit(solution)/shard_map/all_to_all | solution.py:560
  42.1 0.3 shard_map.86
  42.5 0.0 copy-start.10
  42.5 3.8 %collective-permute-start.2 = (bf16[1312,256]{1,0:T(8,128)(2,1)S(1)}, bf16[1312,256]{1,0:T(8,128)(2,1)S(1)}, u32[]{:S(2)}, u32[]{:S(2)}) collective-permute-start(bf16[1312,256]{1,0:T(8,128)(2,1)S(1)} %get-tuple-element.25), channel_id=1, source_target_pairs={{0,32},{32,64},{64,96},{1,33},{33,65},{65,97},{2,34},{34,66},{66,9... | collective-permute-start | bytes 2015240 | tf_op jit(solution)/shard_map/ppermute | solution.py:556
  46.3 0.7 collective-permute-start.4
  47.0 3.0 %collective-permute-start.3 = (bf16[528,256]{1,0:T(8,128)(2,1)S(1)}, bf16[528,256]{1,0:T(8,128)(2,1)S(1)}, u32[]{:S(2)}, u32[]{:S(2)}) collective-permute-start(bf16[528,256]{1,0:T(8,128)(2,1)S(1)} %get-tuple-element.24.own_ref), channel_id=1, source_target_pairs={{0,64},{32,96},{1,65},{33,97},{2,66},{34,98},{3,67},{35,99},{4,68}... | collective-permute-start | bytes 811016 | tf_op jit(solution)/shard_map/ppermute | solution.py:556
  50.0 6.9 %all-to-all-done.1 = bf16[8,256,256]{2,1,0:T(8,128)(2,1)} async-done(((bf16[8,256,256]{2,1,0:T(8,128)(2,1)}), bf16[8,256,256]{2,1,0:T(8,128)(2,1)}, u32[]{:S(2)}, u32[]{:S(2)}) %all-to-all-start.1) | async-done | bytes 1048608 | tf_op jit(solution)/shard_map/all_to_all | solution.py:560
  56.9 10.4 %shard_map.88 = (f32[1024,256]{1,0:T(8,128)}, f32[2048,256]{1,0:T(8,128)}) custom-call(bf16[8,272,256]{2,1,0:T(8,128)(2,1)} %copy-done, bf16[2048,256]{1,0:T(8,128)(2,1)} %bitcast.5.pair_ref), custom_call_target="tpu_custom_call" | custom-call | tf_op jit(solution)/shard_map/pallas_call | solution.py:618
  67.3 0.0 copy-start.15
  67.3 0.0 copy-start.13
  67.3 0.7 copy-done.14
  68.0 0.1 copy-done.15
  68.0 0.2 copy-done.13
  68.3 18.1 %shard_map.89 = (bf16[2048,256]{1,0:T(8,128)(2,1)}, f32[1024,256]{1,0:T(8,128)}, f32[512,256]{1,0:T(8,128)}, bf16[1312,256]{1,0:T(8,128)(2,1)}, bf16[528,256]{1,0:T(8,128)(2,1)}, /*index=5*/bf16[528,256]{1,0:T(8,128)(2,1)}) custom-call(s32[1]{0:T(128)} %bitcast.4.z_ref, bf16[8,272,256]{2,1,0:T(8,128)(2,1)} %copy-done, bf16[528,256]{1,0:T(8,128)(2,1)} %copy-done.10, ...), custom_call_target="tpu_custom_call" | custom-call | tf_op jit(solution)/shard_map/pallas_call | solution.py:628
  86.4 6.2 %all-to-all-start.2 = ((bf16[8,256,256]{2,1,0:T(8,128)(2,1)}), bf16[8,256,256]{2,1,0:T(8,128)(2,1)S(1)}, u32[]{:S(2)}, u32[]{:S(2)}) async-start(bf16[8,256,256]{2,1,0:T(8,128)(2,1)} %bitcast.7), calls=%async_computation.2 | async-start | bytes 2097152 | tf_op jit(solution)/shard_map/all_to_all | solution.py:560
  92.6 2.0 %collective-permute-start.7 = (bf16[1312,256]{1,0:T(8,128)(2,1)}, bf16[1312,256]{1,0:T(8,128)(2,1)S(1)}, u32[]{:S(2)}, u32[]{:S(2)}) collective-permute-start(bf16[1312,256]{1,0:T(8,128)(2,1)} %get-tuple-element.34), channel_id=1, source_target_pairs={{32,0},{64,32},{96,64},{33,1},{65,33},{97,65},{34,2},{66,34},{98,6... | collective-permute-start | bytes 2015240 | tf_op jit(solution)/shard_map/ppermute | solution.py:556
  94.6 1.3 collective-permute-start.8
  95.9 1.4 collective-permute-start.9
  97.3 9.2 %all-to-all-done.2.attn_ref.pair_ref = bf16[8,256,256]{2,1,0:T(8,128)(2,1)S(1)} async-done(((bf16[8,256,256]{2,1,0:T(8,128)(2,1)}), bf16[8,256,256]{2,1,0:T(8,128)(2,1)S(1)}, u32[]{:S(2)}, u32[]{:S(2)}) %all-to-all-start.2) | async-done | bytes 1048608 | tf_op jit(solution)/shard_map/all_to_all | solution.py:560
  106.5 1.0 copy-done.1
  107.5 5.8 %shard_map.90 = (bf16[256,1536]{1,0:T(8,128)(2,1)}, bf16[256,1536]{1,0:T(8,128)(2,1)}) custom-call(s32[4]{0:T(128)} %pad_add_fusion.order_ref, bf16[8,256,256]{2,1,0:T(8,128)(2,1)} %copy-done.1, bf16[768,6144]{1,0:T(8,128)(2,1)} %w_ref.7), custom_call_target="tpu_custom_call" | custom-call | tf_op jit(solution)/shard_map/pallas_call | solution.py:533
  113.3 4.2 %collective-permute-done.8.back2_ref = bf16[528,256]{1,0:T(8,128)(2,1)S(1)} collective-permute-done((bf16[528,256]{1,0:T(8,128)(2,1)}, bf16[528,256]{1,0:T(8,128)(2,1)S(1)}, u32[]{:S(2)}, u32[]{:S(2)}) %collective-permute-start.8) | collective-permute-done | bytes 270368 | tf_op jit(solution)/shard_map/ppermute | solution.py:556
  117.5 1.1 copy-done.5
  118.6 1.6 copy-done.7
  120.2 1.2 copy-done.8
  121.4 1.0 copy-done.9
  122.5 1.7 shard_map.91.refs_0_
  124.2 1.0 copy-done.3
  125.2 5.6 %shard_map.92 = (bf16[256,1536]{1,0:T(8,128)(2,1)}, bf16[256,1536]{1,0:T(8,128)(2,1)}) custom-call(s32[4]{0:T(128)} %pad_add_fusion.order_ref, bf16[8,256,256]{2,1,0:T(8,128)(2,1)} %copy-done.1, bf16[768,6144]{1,0:T(8,128)(2,1)} %w_ref.7, bf16[8,272,256]{2,1,0:T(8,128)(2,1)} %copy-done.3), custom_call_target="tpu_custom_call" | custom-call | tf_op jit(solution)/shard_map/pallas_call | solution.py:533
  130.8 7.4 %all-to-all-start.3 = ((bf16[8,272,256]{2,1,0:T(8,128)(2,1)}), bf16[8,272,256]{2,1,0:T(8,128)(2,1)S(1)}, u32[]{:S(2)}, u32[]{:S(2)}) async-start(bf16[8,272,256]{2,1,0:T(8,128)(2,1)} %copy-done.3), calls=%async_computation.3 | async-start | bytes 2228224 | tf_op jit(solution)/shard_map/all_to_all | solution.py:560
  138.2 2.3 %add_convert_fusion.1 = bf16[256,1536]{1,0:T(8,128)(2,1)} fusion(bf16[256,1536]{1,0:T(8,128)(2,1)} %collective-permute-done.10, bf16[256,1536]{1,0:T(8,128)(2,1)S(1)} %copy-done.12), kind=kLoop, calls=%fused_computation.1 | loop fusion | flops 1572864 | bytes 2359296 | tf_op jit(solution)/shard_map/convert_element_type | solution.py:682
  140.4 0.8 collective-permute-start.11
  141.3 12.6 %all-to-all-done.3.x_ref = bf16[8,272,256]{2,1,0:T(8,128)(2,1)S(1)} async-done(((bf16[8,272,256]{2,1,0:T(8,128)(2,1)}), bf16[8,272,256]{2,1,0:T(8,128)(2,1)S(1)}, u32[]{:S(2)}, u32[]{:S(2)}) %all-to-all-start.3) | async-done | bytes 1114144 | tf_op jit(solution)/shard_map/all_to_all | solution.py:560
  153.9 1.2 shard_map.93
  155.1 14.2 %collective-permute-done.11 = bf16[256,1536]{1,0:T(8,128)(2,1)} collective-permute-done((bf16[256,1536]{1,0:T(8,128)(2,1)}, bf16[256,1536]{1,0:T(8,128)(2,1)}, u32[]{:S(2)}, u32[]{:S(2)}) %collective-permute-start.11) | collective-permute-done | bytes 786464 | tf_op jit(solution)/shard_map/ppermute | solution.py:552
  169.3 2.5 %add_convert_fusion = bf16[256,1536]{1,0:T(8,128)(2,1)} fusion(bf16[256,1536]{1,0:T(8,128)(2,1)} %collective-permute-done.11, bf16[256,1536]{1,0:T(8,128)(2,1)} %collective-permute-done.6, bf16[256,1536]{1,0:T(8,128)(2,1)S(1)} %copy-done.6), kind=kLoop, calls=%fused_computation | loop fusion | flops 2359296 | bytes 3145728 | tf_op jit(solution)/shard_map/convert_element_type | solution.py:682
  (29 shorter events, 0.1 us)
Async XLA Ops:
  0.6 12.1 %collective-permute-start.1 = (bf16[256,1536]{1,0:T(8,128)(2,1)}, bf16[256,1536]{1,0:T(8,128)(2,1)}, u32[]{:S(2)}, u32[]{:S(2)}) collective-permute-start(bf16[256,1536]{1,0:T(8,128)(2,1)} %a_ref.1), channel_id=1, source_target_pairs={{0,1},{1,0},{2,3},{3,2},{4,5},{5,4},{6,7},{7,6},{8,9},{9,8},{10,11... | collective-permute-start | bytes 2359304 | tf_op jit(solution)/shard_map/ppermute | solution.py:552
  0.7 20.6 %collective-permute-start = (bf16[256,1536]{1,0:T(8,128)(2,1)}, bf16[256,1536]{1,0:T(8,128)(2,1)S(1)}, u32[]{:S(2)}, u32[]{:S(2)}) collective-permute-start(bf16[256,1536]{1,0:T(8,128)(2,1)} %a_ref.1), channel_id=1, source_target_pairs={{0,2},{2,0},{1,3},{3,1},{4,6},{6,4},{5,7},{7,5},{8,10},{10,8},{9,1... | collective-permute-start | bytes 2359304 | tf_op jit(solution)/shard_map/ppermute | solution.py:552
  4.7 28.2 %all-to-all-start = ((bf16[8,272,256]{2,1,0:T(8,128)(2,1)}), bf16[8,272,256]{2,1,0:T(8,128)(2,1)S(1)}, u32[]{:S(2)}, u32[]{:S(2)}) async-start(bf16[8,272,256]{2,1,0:T(8,128)(2,1)} %shard_map.84), calls=%async_computation | async-start | bytes 2228224 | tf_op jit(solution)/shard_map/all_to_all | solution.py:560
  21.4 2.4 %copy-start.11 = (bf16[256,1536]{1,0:T(8,128)(2,1)}, bf16[256,1536]{1,0:T(8,128)(2,1)S(1)}, u32[]{:S(2)}) copy-start(bf16[256,1536]{1,0:T(8,128)(2,1)S(1)} %collective-permute-done.a_ref) | copy-start | bytes 2359300
  21.4 2.4 %collective-permute-start.5 = (bf16[256,1536]{1,0:T(8,128)(2,1)S(1)}, bf16[256,1536]{1,0:T(8,128)(2,1)}, u32[]{:S(2)}, u32[]{:S(2)}) collective-permute-start(bf16[256,1536]{1,0:T(8,128)(2,1)S(1)} %collective-permute-done.a_ref), channel_id=1, source_target_pairs={{0,1},{1,0},{2,3},{3,2},{4,5},{5,4},{6,7},{7,6},{8,9},{9,8},{10,11... | collective-permute-start | bytes 2359304 | tf_op jit(solution)/shard_map/ppermute | solution.py:552
  29.6 12.5 %copy-start.4 = (f32[768,256]{1,0:T(8,128)S(1)}, f32[768,256]{1,0:T(8,128)}, u32[]{:S(2)}) copy-start(f32[768,256]{1,0:T(8,128)} %shard_map.85.after_ref.start) | copy-start | bytes 2359300
  32.9 9.5 %copy-start = (bf16[8,272,256]{2,1,0:T(8,128)(2,1)}, bf16[8,272,256]{2,1,0:T(8,128)(2,1)S(1)}, u32[]{:S(2)}) copy-start(bf16[8,272,256]{2,1,0:T(8,128)(2,1)S(1)} %all-to-all-done.x_ref) | copy-start | bytes 3342340
  32.9 23.9 %all-to-all-start.1 = ((bf16[8,256,256]{2,1,0:T(8,128)(2,1)}), bf16[8,256,256]{2,1,0:T(8,128)(2,1)}, u32[]{:S(2)}, u32[]{:S(2)}) async-start(bf16[8,256,256]{2,1,0:T(8,128)(2,1)} %shard_map.87), calls=%async_computation.1 | async-start | bytes 2097152 | tf_op jit(solution)/shard_map/all_to_all | solution.py:560
  42.5 24.8 %copy-start.10 = (bf16[528,256]{1,0:T(8,128)(2,1)}, bf16[528,256]{1,0:T(8,128)(2,1)S(1)}, u32[]{:S(2)}) copy-start(bf16[528,256]{1,0:T(8,128)(2,1)S(1)} %get-tuple-element.24.own_ref) | copy-start | bytes 811012
  42.5 24.8 %collective-permute-start.2 = (bf16[1312,256]{1,0:T(8,128)(2,1)S(1)}, bf16[1312,256]{1,0:T(8,128)(2,1)S(1)}, u32[]{:S(2)}, u32[]{:S(2)}) collective-permute-start(bf16[1312,256]{1,0:T(8,128)(2,1)S(1)} %get-tuple-element.25), channel_id=1, source_target_pairs={{0,32},{32,64},{64,96},{1,33},{33,65},{65,97},{2,34},{34,66},{66,9... | collective-permute-start | bytes 2015240 | tf_op jit(solution)/shard_map/ppermute | solution.py:556
  46.3 20.9 %collective-permute-start.4 = (bf16[528,256]{1,0:T(8,128)(2,1)S(1)}, bf16[528,256]{1,0:T(8,128)(2,1)S(1)}, u32[]{:S(2)}, u32[]{:S(2)}) collective-permute-start(bf16[528,256]{1,0:T(8,128)(2,1)S(1)} %get-tuple-element.24.own_ref), channel_id=1, source_target_pairs={{0,96},{1,97},{2,98},{3,99},{4,100},{5,101},{6,102},{7,103},{8,104... | collective-permute-start | bytes 811016 | tf_op jit(solution)/shard_map/ppermute | solution.py:556
  47.0 20.3 %collective-permute-start.3 = (bf16[528,256]{1,0:T(8,128)(2,1)S(1)}, bf16[528,256]{1,0:T(8,128)(2,1)S(1)}, u32[]{:S(2)}, u32[]{:S(2)}) collective-permute-start(bf16[528,256]{1,0:T(8,128)(2,1)S(1)} %get-tuple-element.24.own_ref), channel_id=1, source_target_pairs={{0,64},{32,96},{1,65},{33,97},{2,66},{34,98},{3,67},{35,99},{4,68}... | collective-permute-start | bytes 811016 | tf_op jit(solution)/shard_map/ppermute | solution.py:556
  67.3 0.7 copy-start.14
  67.3 0.8 copy-start.15
  67.3 1.0 copy-start.13
  86.4 20.1 %all-to-all-start.2 = ((bf16[8,256,256]{2,1,0:T(8,128)(2,1)}), bf16[8,256,256]{2,1,0:T(8,128)(2,1)S(1)}, u32[]{:S(2)}, u32[]{:S(2)}) async-start(bf16[8,256,256]{2,1,0:T(8,128)(2,1)} %bitcast.7), calls=%async_computation.2 | async-start | bytes 2097152 | tf_op jit(solution)/shard_map/all_to_all | solution.py:560
  92.6 24.9 %collective-permute-start.7 = (bf16[1312,256]{1,0:T(8,128)(2,1)}, bf16[1312,256]{1,0:T(8,128)(2,1)S(1)}, u32[]{:S(2)}, u32[]{:S(2)}) collective-permute-start(bf16[1312,256]{1,0:T(8,128)(2,1)} %get-tuple-element.34), channel_id=1, source_target_pairs={{32,0},{64,32},{96,64},{33,1},{65,33},{97,65},{34,2},{66,34},{98,6... | collective-permute-start | bytes 2015240 | tf_op jit(solution)/shard_map/ppermute | solution.py:556
  94.6 22.9 %collective-permute-start.8 = (bf16[528,256]{1,0:T(8,128)(2,1)}, bf16[528,256]{1,0:T(8,128)(2,1)S(1)}, u32[]{:S(2)}, u32[]{:S(2)}) collective-permute-start(bf16[528,256]{1,0:T(8,128)(2,1)} %get-tuple-element.35), channel_id=1, source_target_pairs={{64,0},{96,32},{65,1},{97,33},{66,2},{98,34},{67,3},{99,35},{68,4}... | collective-permute-start | bytes 811016 | tf_op jit(solution)/shard_map/ppermute | solution.py:556
  95.9 21.6 %collective-permute-start.9 = (bf16[528,256]{1,0:T(8,128)(2,1)}, bf16[528,256]{1,0:T(8,128)(2,1)}, u32[]{:S(2)}, u32[]{:S(2)}) collective-permute-start(bf16[528,256]{1,0:T(8,128)(2,1)} %get-tuple-element.36), channel_id=1, source_target_pairs={{96,0},{97,1},{98,2},{99,3},{100,4},{101,5},{102,6},{103,7},{104,8... | collective-permute-start | bytes 811016 | tf_op jit(solution)/shard_map/ppermute | solution.py:556
  106.5 1.0 copy-start.1
  117.5 1.1 copy-start.5
  118.6 1.6 copy-start.7
  120.2 1.2 copy-start.8
  121.4 1.0 copy-start.9
  124.2 1.0 copy-start.3
  130.8 7.4 %copy-start.12 = (bf16[256,1536]{1,0:T(8,128)(2,1)S(1)}, bf16[256,1536]{1,0:T(8,128)(2,1)}, u32[]{:S(2)}) copy-start(bf16[256,1536]{1,0:T(8,128)(2,1)} %get-tuple-element.37) | copy-start | bytes 2359300
  130.8 7.4 %collective-permute-start.10 = (bf16[256,1536]{1,0:T(8,128)(2,1)}, bf16[256,1536]{1,0:T(8,128)(2,1)}, u32[]{:S(2)}, u32[]{:S(2)}) collective-permute-start(bf16[256,1536]{1,0:T(8,128)(2,1)} %get-tuple-element.38), channel_id=1, source_target_pairs={{0,1},{1,0},{2,3},{3,2},{4,5},{5,4},{6,7},{7,6},{8,9},{9,8},{10,11... | collective-permute-start | bytes 2359304 | tf_op jit(solution)/shard_map/ppermute | solution.py:552
  130.8 23.1 %all-to-all-start.3 = ((bf16[8,272,256]{2,1,0:T(8,128)(2,1)}), bf16[8,272,256]{2,1,0:T(8,128)(2,1)S(1)}, u32[]{:S(2)}, u32[]{:S(2)}) async-start(bf16[8,272,256]{2,1,0:T(8,128)(2,1)} %copy-done.3), calls=%async_computation.3 | async-start | bytes 2228224 | tf_op jit(solution)/shard_map/all_to_all | solution.py:560
  138.1 15.8 %copy-start.2 = (bf16[8,256,256]{2,1,0:T(8,128)(2,1)S(1)}, bf16[8,256,256]{2,1,0:T(8,128)(2,1)}, u32[]{:S(2)}) copy-start(bf16[8,256,256]{2,1,0:T(8,128)(2,1)} %copy-done.1) | copy-start | bytes 3145732
  138.1 17.0 %collective-permute-start.6 = (bf16[256,1536]{1,0:T(8,128)(2,1)}, bf16[256,1536]{1,0:T(8,128)(2,1)}, u32[]{:S(2)}, u32[]{:S(2)}) collective-permute-start(bf16[256,1536]{1,0:T(8,128)(2,1)} %get-tuple-element.30), channel_id=1, source_target_pairs={{0,1},{1,0},{2,3},{3,2},{4,5},{5,4},{6,7},{7,6},{8,9},{9,8},{10,11... | collective-permute-start | bytes 2359304 | tf_op jit(solution)/shard_map/ppermute | solution.py:552
  140.4 28.8 %copy-start.6 = (bf16[256,1536]{1,0:T(8,128)(2,1)S(1)}, bf16[256,1536]{1,0:T(8,128)(2,1)}, u32[]{:S(2)}) copy-start(bf16[256,1536]{1,0:T(8,128)(2,1)} %get-tuple-element.29.after_ref) | copy-start | bytes 2359300
  140.4 28.8 %collective-permute-start.11 = (bf16[256,1536]{1,0:T(8,128)(2,1)}, bf16[256,1536]{1,0:T(8,128)(2,1)}, u32[]{:S(2)}, u32[]{:S(2)}) collective-permute-start(bf16[256,1536]{1,0:T(8,128)(2,1)} %add_convert_fusion.1), channel_id=1, source_target_pairs={{0,2},{2,0},{1,3},{3,1},{4,6},{6,4},{5,7},{7,5},{8,10},{10,8},{9,1... | collective-permute-start | bytes 2359304 | tf_op jit(solution)/shard_map/ppermute | solution.py:552

commit v7 on v6

--- a/solution.py
+++ b/solution.py
@@ -544,7 +544,7 @@
             out_specs=[pl.BlockSpec((rows, width), lambda i, o: (0, 0))] * 2,
             scratch_shapes=[pltpu.VMEM((rows, depth), bf16)],
         ),
-        compiler_params=pltpu.CompilerParams(vmem_limit_bytes=62 * 1024 * 1024),
+        compiler_params=pltpu.CompilerParams(vmem_limit_bytes=64 * 1024 * 1024),
     )(order, attn, weight, *after)
 
 
@@ -671,7 +671,7 @@
     finished = call(
         finish_kernel,
         array(PLANE_DEVS, tokens + TAIL, 256),
-        32,
+        64,
         in_specs=[whole] * 6 + [in_place],
         scratch_shapes=[
             pltpu.VMEM((coarse + 2 * TAIL, 256), bf16),

time: 173 us -> 168 us (0.971)
  local copies, waits for them, and re-layouts: 7.99 us -> 1 us
  Pallas kernels: 57 us -> 60.8 us
  other arithmetic: 5.43 us -> 2.86 us
    unnamed x32 -> x18, local copies, waits for them, and re-layouts: 7.99 us -> 1 us
    convert_element_type x2, other arithmetic: 4.82 us -> 2.27 us  [shards(): mixed_out = (part + swap(other.astype(bf16), 'xl').astype(f32)).astype(bf16)]
    pallas_call x1, Pallas kernels: 1.69 us -> 4.11 us  [shards(): call(finish_kernel, array(PLANE_DEVS, tokens + TAIL, 256), 64, in_specs=[...]
  transfers between devices with their start and end apart: 16 -> 16, of which waited for: 8 -> 8; matrix products, arithmetic and copies ran while one was open for 2% -> 1% of each run, Pallas kernels for 18% -> 20%
where the time goes in v7:
time: 168 us; the launch traced here: 167 us
  Pallas kernels  60.8 us (36%)
  waiting for transfers between devices  56.8 us (34%)
  starting transfers between devices  45.2 us (27%)
  other arithmetic  2.86 us (2%)
    all_to_all x4, waiting for transfers between devices, in_plane(): return lax.all_to_all(x, PLANE, 0, 0, tiled=True)  33 us
    all_to_all x4, starting transfers between devices, in_plane(): return lax.all_to_all(x, PLANE, 0, 0, tiled=True)  30.8 us
    ppermute x6, waiting for transfers between devices, swap(): return lax.ppermute(x, axis, [(0, 1), (1, 0)])  18.6 us
    pallas_call x1, Pallas kernels, shards(): call(attention_kernel, (array(rows, 256), array(rows - WINDOW, 256, dtype...  18.2 us
    ppermute x6, starting transfers between devices, planes_up(): lax.ppermute(x, 'z', [(i, i + by) for i in range(PLANES) if 0 <= i + by <...  12.2 us
    pallas_call x2, Pallas kernels, project(): pl.pallas_call(functools.partial(project_kernel, halves), out_shape=(out,...  11.4 us
    pallas_call x2, Pallas kernels, grad_part(): pl.pallas_call(functools.partial(grad_far_kernel if rest else grad_near_k...  11.2 us
    pallas_call x1, Pallas kernels, shards(): call(own_kernel, (array(rows - WINDOW, 256, dtype=f32), array(rows, 256,...  10.5 us
  transfers between devices with their start and end apart: 16, of which 8 were waited for; matrix products, arithmetic and copies ran while one was open for 1% of the time, Pallas kernels for 20%

profile of v7, /device:TPU:36, one launch (start us, length us, event | category | flops | bytes accessed | tf_op | source)
XLA Modules:
  0.0 167.5 jit_solution(8129165253695999941)
XLA Ops:
  0.6 0.1 collective-permute-start.1
  0.7 1.3 collective-permute-start
  2.0 2.6 %shard_map.84 = bf16[8,272,256]{2,1,0:T(8,128)(2,1)} custom-call(bf16[256,768]{1,0:T(8,128)(2,1)} %q_ref.3, bf16[256,768]{1,0:T(8,128)(2,1)} %k_ref.1, bf16[256,768]{1,0:T(8,128)(2,1)} %v_ref.1), custom_call_target="tpu_custom_call" | custom-call | tf_op jit(solution)/shard_map/pallas_call | solution.py:595
  4.7 7.4 %all-to-all-start = ((bf16[8,272,256]{2,1,0:T(8,128)(2,1)}), bf16[8,272,256]{2,1,0:T(8,128)(2,1)S(1)}, u32[]{:S(2)}, u32[]{:S(2)}) async-start(bf16[8,272,256]{2,1,0:T(8,128)(2,1)} %shard_map.84), calls=%async_computation | async-start | bytes 2228224 | tf_op jit(solution)/shard_map/all_to_all | solution.py:560
  12.1 0.6 pad_add_fusion.order_ref
  12.7 5.3 %shard_map.85.after_ref.start = f32[768,256]{1,0:T(8,128)} custom-call(s32[4]{0:T(128)} %pad_add_fusion.order_ref, bf16[256,1536]{1,0:T(8,128)(2,1)} %a_ref.1, bf16[256,1536]{1,0:T(8,128)(2,1)} %collective-permute-done.1.b_ref, bf16[768,6144]{1,0:T(8,128)(2,1)} %w_ref.7), custom_call_target="tpu_custom_call" | custom-call | tf_op jit(solution)/shard_map/pallas_call | solution.py:488
  18.0 3.4 %collective-permute-done.a_ref = bf16[256,1536]{1,0:T(8,128)(2,1)S(1)} collective-permute-done((bf16[256,1536]{1,0:T(8,128)(2,1)}, bf16[256,1536]{1,0:T(8,128)(2,1)S(1)}, u32[]{:S(2)}, u32[]{:S(2)}) %collective-permute-start) | collective-permute-done | bytes 786464 | tf_op jit(solution)/shard_map/ppermute | solution.py:552
  21.4 0.0 collective-permute-start.5
  21.4 2.4 %collective-permute-done.5.b_ref = bf16[256,1536]{1,0:T(8,128)(2,1)} collective-permute-done((bf16[256,1536]{1,0:T(8,128)(2,1)S(1)}, bf16[256,1536]{1,0:T(8,128)(2,1)}, u32[]{:S(2)}, u32[]{:S(2)}) %collective-permute-start.5) | collective-permute-done | bytes 786464 | tf_op jit(solution)/shard_map/ppermute | solution.py:552
  23.8 5.9 %shard_map.87 = bf16[8,256,256]{2,1,0:T(8,128)(2,1)} custom-call(s32[4]{0:T(128)} %pad_add_fusion.order_ref, bf16[256,1536]{1,0:T(8,128)(2,1)} %copy-done.4, bf16[256,1536]{1,0:T(8,128)(2,1)} %collective-permute-done.5.b_ref, bf16[768,6144]{1,0:T(8,128)(2,1)} %w_ref.7, f32[768,256]{1,0:T(8,128)} %shard_map.85.after_ref.start, bf16[256,768]{1,0:T(8,128)(2,1)} %q_ref.3), custom_call_target="tpu_custom_call" | custom-call | tf_op jit(solution)/shard_map/pallas_call | solution.py:488
  29.7 3.2 %all-to-all-done.x_ref = bf16[8,272,256]{2,1,0:T(8,128)(2,1)S(1)} async-done(((bf16[8,272,256]{2,1,0:T(8,128)(2,1)}), bf16[8,272,256]{2,1,0:T(8,128)(2,1)S(1)}, u32[]{:S(2)}, u32[]{:S(2)}) %all-to-all-start) | async-done | bytes 1114144 | tf_op jit(solution)/shard_map/all_to_all | solution.py:560
  32.9 9.2 %all-to-all-start.1 = ((bf16[8,256,256]{2,1,0:T(8,128)(2,1)}), bf16[8,256,256]{2,1,0:T(8,128)(2,1)}, u32[]{:S(2)}, u32[]{:S(2)}) async-start(bf16[8,256,256]{2,1,0:T(8,128)(2,1)} %shard_map.87), calls=%async_computation.1 | async-start | bytes 2097152 | tf_op jit(solution)/shard_map/all_to_all | solution.py:560
  42.1 0.3 shard_map.86
  42.5 0.0 copy-start.2
  42.5 3.8 %collective-permute-start.2 = (bf16[1312,256]{1,0:T(8,128)(2,1)S(1)}, bf16[1312,256]{1,0:T(8,128)(2,1)S(1)}, u32[]{:S(2)}, u32[]{:S(2)}) collective-permute-start(bf16[1312,256]{1,0:T(8,128)(2,1)S(1)} %get-tuple-element.25), channel_id=1, source_target_pairs={{0,32},{32,64},{64,96},{1,33},{33,65},{65,97},{2,34},{34,66},{66,9... | collective-permute-start | bytes 2015240 | tf_op jit(solution)/shard_map/ppermute | solution.py:556
  46.3 0.7 collective-permute-start.4
  47.0 3.0 %collective-permute-start.3 = (bf16[528,256]{1,0:T(8,128)(2,1)S(1)}, bf16[528,256]{1,0:T(8,128)(2,1)S(1)}, u32[]{:S(2)}, u32[]{:S(2)}) collective-permute-start(bf16[528,256]{1,0:T(8,128)(2,1)S(1)} %get-tuple-element.24.own_ref), channel_id=1, source_target_pairs={{0,64},{32,96},{1,65},{33,97},{2,66},{34,98},{3,67},{35,99},{4,68}... | collective-permute-start | bytes 811016 | tf_op jit(solution)/shard_map/ppermute | solution.py:556
  50.0 6.9 %all-to-all-done.1 = bf16[8,256,256]{2,1,0:T(8,128)(2,1)} async-done(((bf16[8,256,256]{2,1,0:T(8,128)(2,1)}), bf16[8,256,256]{2,1,0:T(8,128)(2,1)}, u32[]{:S(2)}, u32[]{:S(2)}) %all-to-all-start.1) | async-done | bytes 1048608 | tf_op jit(solution)/shard_map/all_to_all | solution.py:560
  56.9 10.5 %shard_map.88 = (f32[1024,256]{1,0:T(8,128)}, f32[2048,256]{1,0:T(8,128)}) custom-call(bf16[8,272,256]{2,1,0:T(8,128)(2,1)} %copy-done, bf16[2048,256]{1,0:T(8,128)(2,1)} %bitcast.5.pair_ref), custom_call_target="tpu_custom_call" | custom-call | tf_op jit(solution)/shard_map/pallas_call | solution.py:618
  67.4 0.0 collective-permute-done.3.far2_ref
  67.4 0.0 copy-start.8
  67.4 0.0 collective-permute-done.2.near_ref
  67.4 0.0 copy-start.6
  67.4 0.7 copy-done.7
  68.1 0.1 copy-done.8
  68.2 0.2 copy-done.6
  68.4 18.2 %shard_map.89 = (bf16[2048,256]{1,0:T(8,128)(2,1)}, f32[1024,256]{1,0:T(8,128)}, f32[512,256]{1,0:T(8,128)}, bf16[1312,256]{1,0:T(8,128)(2,1)}, bf16[528,256]{1,0:T(8,128)(2,1)}, /*index=5*/bf16[528,256]{1,0:T(8,128)(2,1)}) custom-call(s32[1]{0:T(128)} %bitcast.4.z_ref, bf16[8,272,256]{2,1,0:T(8,128)(2,1)} %copy-done, bf16[528,256]{1,0:T(8,128)(2,1)} %copy-done.2, ...), custom_call_target="tpu_custom_call" | custom-call | tf_op jit(solution)/shard_map/pallas_call | solution.py:628
  86.6 6.8 %all-to-all-start.2 = ((bf16[8,256,256]{2,1,0:T(8,128)(2,1)}), bf16[8,256,256]{2,1,0:T(8,128)(2,1)}, u32[]{:S(2)}, u32[]{:S(2)}) async-start(bf16[8,256,256]{2,1,0:T(8,128)(2,1)} %bitcast.7), calls=%async_computation.2 | async-start | bytes 2097152 | tf_op jit(solution)/shard_map/all_to_all | solution.py:560
  93.4 2.0 %collective-permute-start.7 = (bf16[1312,256]{1,0:T(8,128)(2,1)}, bf16[1312,256]{1,0:T(8,128)(2,1)}, u32[]{:S(2)}, u32[]{:S(2)}) collective-permute-start(bf16[1312,256]{1,0:T(8,128)(2,1)} %get-tuple-element.34), channel_id=1, source_target_pairs={{32,0},{64,32},{96,64},{33,1},{65,33},{97,65},{34,2},{66,34},{98,6... | collective-permute-start | bytes 2015240 | tf_op jit(solution)/shard_map/ppermute | solution.py:556
  95.4 1.3 collective-permute-start.8
  96.7 1.4 collective-permute-start.9
  98.1 9.1 %all-to-all-done.2.attn_ref.pair_ref = bf16[8,256,256]{2,1,0:T(8,128)(2,1)} async-done(((bf16[8,256,256]{2,1,0:T(8,128)(2,1)}), bf16[8,256,256]{2,1,0:T(8,128)(2,1)}, u32[]{:S(2)}, u32[]{:S(2)}) %all-to-all-start.2) | async-done | bytes 1048608 | tf_op jit(solution)/shard_map/all_to_all | solution.py:560
  107.2 5.8 %shard_map.90 = (bf16[256,1536]{1,0:T(8,128)(2,1)}, bf16[256,1536]{1,0:T(8,128)(2,1)}) custom-call(s32[4]{0:T(128)} %pad_add_fusion.order_ref, bf16[8,256,256]{2,1,0:T(8,128)(2,1)} %all-to-all-done.2.attn_ref.pair_ref, bf16[768,6144]{1,0:T(8,128)(2,1)} %w_ref.7), custom_call_target="tpu_custom_call" | custom-call | tf_op jit(solution)/shard_map/pallas_call | solution.py:533
  113.0 5.2 %collective-permute-done.8.back2_ref = bf16[528,256]{1,0:T(8,128)(2,1)} collective-permute-done((bf16[528,256]{1,0:T(8,128)(2,1)}, bf16[528,256]{1,0:T(8,128)(2,1)}, u32[]{:S(2)}, u32[]{:S(2)}) %collective-permute-start.8) | collective-permute-done | bytes 270368 | tf_op jit(solution)/shard_map/ppermute | solution.py:556
  118.2 0.0 collective-permute-done.9.back3_ref
  118.2 0.0 collective-permute-done.7.back1_ref
  118.2 4.1 %shard_map.91.refs_0_ = bf16[8,272,256]{2,1,0:T(8,128)(2,1)} custom-call(f32[2048,256]{1,0:T(8,128)} %get-tuple-element.31.sums_ref, f32[1024,256]{1,0:T(8,128)} %get-tuple-element.32.fine_ref, f32[512,256]{1,0:T(8,128)} %get-tuple-element.33.coarse_ref, bf16[1312,256]{1,0:T(8,128)(2,1)} %collective-permute-done.7.back1_ref, ...), custom_call_target="tpu_custom_call" | custom-call | tf_op jit(solution)/shard_map/pallas_call | solution.py:671
  122.3 5.6 %shard_map.92 = (bf16[256,1536]{1,0:T(8,128)(2,1)}, bf16[256,1536]{1,0:T(8,128)(2,1)}) custom-call(s32[4]{0:T(128)} %pad_add_fusion.order_ref, bf16[8,256,256]{2,1,0:T(8,128)(2,1)} %all-to-all-done.2.attn_ref.pair_ref, bf16[768,6144]{1,0:T(8,128)(2,1)} %w_ref.7, bf16[8,272,256]{2,1,0:T(8,128)(2,1)} %shard_map.91.refs_0_), custom_call_target="tpu_custom_call" | custom-call | tf_op jit(solution)/shard_map/pallas_call | solution.py:533
  127.9 0.0 collective-permute-start.10
  127.9 7.4 %all-to-all-start.3 = ((bf16[8,272,256]{2,1,0:T(8,128)(2,1)}), bf16[8,272,256]{2,1,0:T(8,128)(2,1)S(1)}, u32[]{:S(2)}, u32[]{:S(2)}) async-start(bf16[8,272,256]{2,1,0:T(8,128)(2,1)} %shard_map.91.refs_0_), calls=%async_computation.3 | async-start | bytes 2228224 | tf_op jit(solution)/shard_map/all_to_all | solution.py:560
  135.3 0.0 collective-permute-start.6
  135.3 0.0 collective-permute-done.10
  135.3 1.1 add_convert_fusion.1
  136.4 0.8 collective-permute-start.11
  137.2 13.8 %all-to-all-done.3.x_ref = bf16[8,272,256]{2,1,0:T(8,128)(2,1)S(1)} async-done(((bf16[8,272,256]{2,1,0:T(8,128)(2,1)}), bf16[8,272,256]{2,1,0:T(8,128)(2,1)S(1)}, u32[]{:S(2)}, u32[]{:S(2)}) %all-to-all-start.3) | async-done | bytes 1114144 | tf_op jit(solution)/shard_map/all_to_all | solution.py:560
  151.0 2.4 %shard_map.93 = (bf16[256,768]{1,0:T(8,128)(2,1)}, bf16[256,768]{1,0:T(8,128)(2,1)}, bf16[256,768]{1,0:T(8,128)(2,1)}) custom-call(bf16[8,256,256]{2,1,0:T(8,128)(2,1)} %all-to-all-done.2.attn_ref.pair_ref, bf16[8,272,256]{2,1,0:T(8,128)(2,1)S(1)} %all-to-all-done.3.x_ref), custom_call_target="tpu_custom_call" | custom-call | tf_op jit(solution)/shard_map/pallas_call | solution.py:684
  153.5 12.8 %collective-permute-done.11 = bf16[256,1536]{1,0:T(8,128)(2,1)S(1)} collective-permute-done((bf16[256,1536]{1,0:T(8,128)(2,1)}, bf16[256,1536]{1,0:T(8,128)(2,1)S(1)}, u32[]{:S(2)}, u32[]{:S(2)}) %collective-permute-start.11) | collective-permute-done | bytes 786464 | tf_op jit(solution)/shard_map/ppermute | solution.py:552
  166.3 1.2 add_convert_fusion
  (15 shorter events, 0.0 us)
Async XLA Ops:
  0.6 12.1 %collective-permute-start.1 = (bf16[256,1536]{1,0:T(8,128)(2,1)}, bf16[256,1536]{1,0:T(8,128)(2,1)}, u32[]{:S(2)}, u32[]{:S(2)}) collective-permute-start(bf16[256,1536]{1,0:T(8,128)(2,1)} %a_ref.1), channel_id=1, source_target_pairs={{0,1},{1,0},{2,3},{3,2},{4,5},{5,4},{6,7},{7,6},{8,9},{9,8},{10,11... | collective-permute-start | bytes 2359304 | tf_op jit(solution)/shard_map/ppermute | solution.py:552
  0.7 20.6 %collective-permute-start = (bf16[256,1536]{1,0:T(8,128)(2,1)}, bf16[256,1536]{1,0:T(8,128)(2,1)S(1)}, u32[]{:S(2)}, u32[]{:S(2)}) collective-permute-start(bf16[256,1536]{1,0:T(8,128)(2,1)} %a_ref.1), channel_id=1, source_target_pairs={{0,2},{2,0},{1,3},{3,1},{4,6},{6,4},{5,7},{7,5},{8,10},{10,8},{9,1... | collective-permute-start | bytes 2359304 | tf_op jit(solution)/shard_map/ppermute | solution.py:552
  4.7 28.3 %all-to-all-start = ((bf16[8,272,256]{2,1,0:T(8,128)(2,1)}), bf16[8,272,256]{2,1,0:T(8,128)(2,1)S(1)}, u32[]{:S(2)}, u32[]{:S(2)}) async-start(bf16[8,272,256]{2,1,0:T(8,128)(2,1)} %shard_map.84), calls=%async_computation | async-start | bytes 2228224 | tf_op jit(solution)/shard_map/all_to_all | solution.py:560
  21.4 2.4 %copy-start.4 = (bf16[256,1536]{1,0:T(8,128)(2,1)}, bf16[256,1536]{1,0:T(8,128)(2,1)S(1)}, u32[]{:S(2)}) copy-start(bf16[256,1536]{1,0:T(8,128)(2,1)S(1)} %collective-permute-done.a_ref) | copy-start | bytes 2359300
  21.4 2.4 %collective-permute-start.5 = (bf16[256,1536]{1,0:T(8,128)(2,1)S(1)}, bf16[256,1536]{1,0:T(8,128)(2,1)}, u32[]{:S(2)}, u32[]{:S(2)}) collective-permute-start(bf16[256,1536]{1,0:T(8,128)(2,1)S(1)} %collective-permute-done.a_ref), channel_id=1, source_target_pairs={{0,1},{1,0},{2,3},{3,2},{4,5},{5,4},{6,7},{7,6},{8,9},{9,8},{10,11... | collective-permute-start | bytes 2359304 | tf_op jit(solution)/shard_map/ppermute | solution.py:552
  29.7 12.4 %copy-start.1 = (f32[768,256]{1,0:T(8,128)S(1)}, f32[768,256]{1,0:T(8,128)}, u32[]{:S(2)}) copy-start(f32[768,256]{1,0:T(8,128)} %shard_map.85.after_ref.start) | copy-start | bytes 2359300
  32.9 9.5 %copy-start = (bf16[8,272,256]{2,1,0:T(8,128)(2,1)}, bf16[8,272,256]{2,1,0:T(8,128)(2,1)S(1)}, u32[]{:S(2)}) copy-start(bf16[8,272,256]{2,1,0:T(8,128)(2,1)S(1)} %all-to-all-done.x_ref) | copy-start | bytes 3342340
  32.9 23.9 %all-to-all-start.1 = ((bf16[8,256,256]{2,1,0:T(8,128)(2,1)}), bf16[8,256,256]{2,1,0:T(8,128)(2,1)}, u32[]{:S(2)}, u32[]{:S(2)}) async-start(bf16[8,256,256]{2,1,0:T(8,128)(2,1)} %shard_map.87), calls=%async_computation.1 | async-start | bytes 2097152 | tf_op jit(solution)/shard_map/all_to_all | solution.py:560
  42.5 24.9 %copy-start.2 = (bf16[528,256]{1,0:T(8,128)(2,1)}, bf16[528,256]{1,0:T(8,128)(2,1)S(1)}, u32[]{:S(2)}) copy-start(bf16[528,256]{1,0:T(8,128)(2,1)S(1)} %get-tuple-element.24.own_ref) | copy-start | bytes 811012
  42.5 24.9 %collective-permute-start.2 = (bf16[1312,256]{1,0:T(8,128)(2,1)S(1)}, bf16[1312,256]{1,0:T(8,128)(2,1)S(1)}, u32[]{:S(2)}, u32[]{:S(2)}) collective-permute-start(bf16[1312,256]{1,0:T(8,128)(2,1)S(1)} %get-tuple-element.25), channel_id=1, source_target_pairs={{0,32},{32,64},{64,96},{1,33},{33,65},{65,97},{2,34},{34,66},{66,9... | collective-permute-start | bytes 2015240 | tf_op jit(solution)/shard_map/ppermute | solution.py:556
  46.3 21.0 %collective-permute-start.4 = (bf16[528,256]{1,0:T(8,128)(2,1)S(1)}, bf16[528,256]{1,0:T(8,128)(2,1)S(1)}, u32[]{:S(2)}, u32[]{:S(2)}) collective-permute-start(bf16[528,256]{1,0:T(8,128)(2,1)S(1)} %get-tuple-element.24.own_ref), channel_id=1, source_target_pairs={{0,96},{1,97},{2,98},{3,99},{4,100},{5,101},{6,102},{7,103},{8,104... | collective-permute-start | bytes 811016 | tf_op jit(solution)/shard_map/ppermute | solution.py:556
  47.0 20.4 %collective-permute-start.3 = (bf16[528,256]{1,0:T(8,128)(2,1)S(1)}, bf16[528,256]{1,0:T(8,128)(2,1)S(1)}, u32[]{:S(2)}, u32[]{:S(2)}) collective-permute-start(bf16[528,256]{1,0:T(8,128)(2,1)S(1)} %get-tuple-element.24.own_ref), channel_id=1, source_target_pairs={{0,64},{32,96},{1,65},{33,97},{2,66},{34,98},{3,67},{35,99},{4,68}... | collective-permute-start | bytes 811016 | tf_op jit(solution)/shard_map/ppermute | solution.py:556
  67.4 0.7 copy-start.7
  67.4 0.8 copy-start.8
  67.4 1.0 copy-start.6
  86.6 20.6 %all-to-all-start.2 = ((bf16[8,256,256]{2,1,0:T(8,128)(2,1)}), bf16[8,256,256]{2,1,0:T(8,128)(2,1)}, u32[]{:S(2)}, u32[]{:S(2)}) async-start(bf16[8,256,256]{2,1,0:T(8,128)(2,1)} %bitcast.7), calls=%async_computation.2 | async-start | bytes 2097152 | tf_op jit(solution)/shard_map/all_to_all | solution.py:560
  93.4 24.8 %collective-permute-start.7 = (bf16[1312,256]{1,0:T(8,128)(2,1)}, bf16[1312,256]{1,0:T(8,128)(2,1)}, u32[]{:S(2)}, u32[]{:S(2)}) collective-permute-start(bf16[1312,256]{1,0:T(8,128)(2,1)} %get-tuple-element.34), channel_id=1, source_target_pairs={{32,0},{64,32},{96,64},{33,1},{65,33},{97,65},{34,2},{66,34},{98,6... | collective-permute-start | bytes 2015240 | tf_op jit(solution)/shard_map/ppermute | solution.py:556
  95.4 22.7 %collective-permute-start.8 = (bf16[528,256]{1,0:T(8,128)(2,1)}, bf16[528,256]{1,0:T(8,128)(2,1)}, u32[]{:S(2)}, u32[]{:S(2)}) collective-permute-start(bf16[528,256]{1,0:T(8,128)(2,1)} %get-tuple-element.35), channel_id=1, source_target_pairs={{64,0},{96,32},{65,1},{97,33},{66,2},{98,34},{67,3},{99,35},{68,4}... | collective-permute-start | bytes 811016 | tf_op jit(solution)/shard_map/ppermute | solution.py:556
  96.7 21.4 %collective-permute-start.9 = (bf16[528,256]{1,0:T(8,128)(2,1)}, bf16[528,256]{1,0:T(8,128)(2,1)}, u32[]{:S(2)}, u32[]{:S(2)}) collective-permute-start(bf16[528,256]{1,0:T(8,128)(2,1)} %get-tuple-element.36), channel_id=1, source_target_pairs={{96,0},{97,1},{98,2},{99,3},{100,4},{101,5},{102,6},{103,7},{104,8... | collective-permute-start | bytes 811016 | tf_op jit(solution)/shard_map/ppermute | solution.py:556
  127.9 7.4 %copy-start.5 = (bf16[256,1536]{1,0:T(8,128)(2,1)S(1)}, bf16[256,1536]{1,0:T(8,128)(2,1)}, u32[]{:S(2)}) copy-start(bf16[256,1536]{1,0:T(8,128)(2,1)} %get-tuple-element.37) | copy-start | bytes 2359300
  127.9 7.4 %collective-permute-start.10 = (bf16[256,1536]{1,0:T(8,128)(2,1)}, bf16[256,1536]{1,0:T(8,128)(2,1)S(1)}, u32[]{:S(2)}, u32[]{:S(2)}) collective-permute-start(bf16[256,1536]{1,0:T(8,128)(2,1)} %get-tuple-element.38), channel_id=1, source_target_pairs={{0,1},{1,0},{2,3},{3,2},{4,5},{5,4},{6,7},{7,6},{8,9},{9,8},{10,11... | collective-permute-start | bytes 2359304 | tf_op jit(solution)/shard_map/ppermute | solution.py:552
  127.9 23.1 %all-to-all-start.3 = ((bf16[8,272,256]{2,1,0:T(8,128)(2,1)}), bf16[8,272,256]{2,1,0:T(8,128)(2,1)S(1)}, u32[]{:S(2)}, u32[]{:S(2)}) async-start(bf16[8,272,256]{2,1,0:T(8,128)(2,1)} %shard_map.91.refs_0_), calls=%async_computation.3 | async-start | bytes 2228224 | tf_op jit(solution)/shard_map/all_to_all | solution.py:560
  135.3 18.2 %collective-permute-start.6 = (bf16[256,1536]{1,0:T(8,128)(2,1)}, bf16[256,1536]{1,0:T(8,128)(2,1)S(1)}, u32[]{:S(2)}, u32[]{:S(2)}) collective-permute-start(bf16[256,1536]{1,0:T(8,128)(2,1)} %get-tuple-element.30), channel_id=1, source_target_pairs={{0,1},{1,0},{2,3},{3,2},{4,5},{5,4},{6,7},{7,6},{8,9},{9,8},{10,11... | collective-permute-start | bytes 2359304 | tf_op jit(solution)/shard_map/ppermute | solution.py:552
  136.4 29.9 %copy-start.3 = (bf16[256,1536]{1,0:T(8,128)(2,1)S(1)}, bf16[256,1536]{1,0:T(8,128)(2,1)}, u32[]{:S(2)}) copy-start(bf16[256,1536]{1,0:T(8,128)(2,1)} %get-tuple-element.29.after_ref) | copy-start | bytes 2359300
  136.4 29.9 %collective-permute-start.11 = (bf16[256,1536]{1,0:T(8,128)(2,1)}, bf16[256,1536]{1,0:T(8,128)(2,1)S(1)}, u32[]{:S(2)}, u32[]{:S(2)}) collective-permute-start(bf16[256,1536]{1,0:T(8,128)(2,1)} %add_convert_fusion.1), channel_id=1, source_target_pairs={{0,2},{2,0},{1,3},{3,1},{4,6},{6,4},{5,7},{7,5},{8,10},{10,8},{9,1... | collective-permute-start | bytes 2359304 | tf_op jit(solution)/shard_map/ppermute | solution.py:552

commit v8 on v7

--- a/solution.py
+++ b/solution.py
@@ -497,7 +497,7 @@
             out_specs=whole(packed if rest else (depth, rows)),
             scratch_shapes=[pltpu.VMEM((depth, rows), f32)] if rest else [],
         ),
-        compiler_params=pltpu.CompilerParams(vmem_limit_bytes=62 * 1024 * 1024),
+        compiler_params=pltpu.CompilerParams(vmem_limit_bytes=64 * 1024 * 1024),
     )(order, *pieces, weight, *rest)
 
 
@@ -618,7 +618,7 @@
     part, sums = call(
         own_kernel,
         (array(rows - WINDOW, 256, dtype=f32), array(rows, 256, dtype=f32)),
-        56,
+        64,
         in_specs=[whole] * 2,
         out_specs=[whole] * 2,
         scratch_shapes=[pltpu.VMEM((rows, HEAD_DIM), bf16)] * 2
@@ -635,7 +635,7 @@
             array(coarse + TAIL, 256),
             array(coarse + TAIL, 256),
         ),
-        62,
+        64,
         in_specs=[pl.BlockSpec(memory_space=pltpu.SMEM)] + [whole] * 7,
         out_specs=[whole] * 6,
         scratch_shapes=[

time: 168 us -> 168 us (level)
  waiting for transfers between devices: 56.8 us -> 54.7 us
  Pallas kernels: 60.8 us -> 62.8 us
    all_to_all x4, waiting for transfers between devices: 33 us -> 28.7 us  [in_plane(): return lax.all_to_all(x, PLANE, 0, 0, tiled=True)]
    pallas_call x1, Pallas kernels: 0.35 us -> 2.44 us  [shards(): call(pool_kernel, (array(near_rows, 256), array(coarse + TAIL, 256)), 16,...]
    ppermute x6, waiting for transfers between devices: 5.18 us -> 7.12 us  [planes_up(): lax.ppermute(x, 'z', [(i, i + by) for i in range(PLANES) if 0 <= i + by <...]
  transfers between devices with their start and end apart: 16 -> 16, of which waited for: 8 -> 9; matrix products, arithmetic and copies ran while one was open for 1% -> 1% of each run, Pallas kernels for 20% -> 21%
where the time goes in v8:
time: 168 us; the launch traced here: 167 us
  Pallas kernels  62.8 us (37%)
  waiting for transfers between devices  54.7 us (33%)
  starting transfers between devices  46.3 us (28%)
  other arithmetic  2.86 us (2%)
    all_to_all x4, starting transfers between devices, in_plane(): return lax.all_to_all(x, PLANE, 0, 0, tiled=True)  31.2 us
    all_to_all x4, waiting for transfers between devices, in_plane(): return lax.all_to_all(x, PLANE, 0, 0, tiled=True)  28.7 us
    ppermute x6, waiting for transfers between devices, swap(): return lax.ppermute(x, axis, [(0, 1), (1, 0)])  18.9 us
    pallas_call x1, Pallas kernels, shards(): call(attention_kernel, (array(rows, 256), array(rows - WINDOW, 256, dtype...  18.2 us
    ppermute x6, starting transfers between devices, planes_up(): lax.ppermute(x, 'z', [(i, i + by) for i in range(PLANES) if 0 <= i + by <...  12.9 us
    pallas_call x2, Pallas kernels, project(): pl.pallas_call(functools.partial(project_kernel, halves), out_shape=(out,...  11.3 us
    pallas_call x2, Pallas kernels, grad_part(): pl.pallas_call(functools.partial(grad_far_kernel if rest else grad_near_k...  11.2 us
    pallas_call x1, Pallas kernels, shards(): call(own_kernel, (array(rows - WINDOW, 256, dtype=f32), array(rows, 256,...  10.5 us
  transfers between devices with their start and end apart: 16, of which 9 were waited for; matrix products, arithmetic and copies ran while one was open for 1% of the time, Pallas kernels for 21%

profile of v8, /device:TPU:36, one launch (start us, length us, event | category | flops | bytes accessed | tf_op | source)
XLA Modules:
  0.0 167.4 jit_solution(11914860969227990303)
XLA Ops:
  0.6 0.1 collective-permute-start.1
  0.7 1.3 collective-permute-start
  2.0 2.7 %shard_map.84 = bf16[8,272,256]{2,1,0:T(8,128)(2,1)} custom-call(bf16[256,768]{1,0:T(8,128)(2,1)} %q_ref.3, bf16[256,768]{1,0:T(8,128)(2,1)} %k_ref.1, bf16[256,768]{1,0:T(8,128)(2,1)} %v_ref.1), custom_call_target="tpu_custom_call" | custom-call | tf_op jit(solution)/shard_map/pallas_call | solution.py:595
  4.7 7.4 %all-to-all-start = ((bf16[8,272,256]{2,1,0:T(8,128)(2,1)}), bf16[8,272,256]{2,1,0:T(8,128)(2,1)}, u32[]{:S(2)}, u32[]{:S(2)}) async-start(bf16[8,272,256]{2,1,0:T(8,128)(2,1)} %shard_map.84), calls=%async_computation | async-start | bytes 2228224 | tf_op jit(solution)/shard_map/all_to_all | solution.py:560
  12.1 0.6 pad_add_fusion.order_ref
  12.7 0.0 collective-permute-done.1.b_ref
  12.7 5.3 %shard_map.85.after_ref.start = f32[768,256]{1,0:T(8,128)} custom-call(s32[4]{0:T(128)} %pad_add_fusion.order_ref, bf16[256,1536]{1,0:T(8,128)(2,1)} %a_ref.1, bf16[256,1536]{1,0:T(8,128)(2,1)} %collective-permute-done.1.b_ref, bf16[768,6144]{1,0:T(8,128)(2,1)} %w_ref.7), custom_call_target="tpu_custom_call" | custom-call | tf_op jit(solution)/shard_map/pallas_call | solution.py:488
  18.0 3.5 %collective-permute-done.a_ref = bf16[256,1536]{1,0:T(8,128)(2,1)} collective-permute-done((bf16[256,1536]{1,0:T(8,128)(2,1)}, bf16[256,1536]{1,0:T(8,128)(2,1)}, u32[]{:S(2)}, u32[]{:S(2)}) %collective-permute-start) | collective-permute-done | bytes 786464 | tf_op jit(solution)/shard_map/ppermute | solution.py:552
  21.5 0.0 collective-permute-start.5
  21.5 2.6 %collective-permute-done.5.b_ref = bf16[256,1536]{1,0:T(8,128)(2,1)} collective-permute-done((bf16[256,1536]{1,0:T(8,128)(2,1)}, bf16[256,1536]{1,0:T(8,128)(2,1)}, u32[]{:S(2)}, u32[]{:S(2)}) %collective-permute-start.5) | collective-permute-done | bytes 786464 | tf_op jit(solution)/shard_map/ppermute | solution.py:552
  24.1 5.9 %shard_map.87 = bf16[8,256,256]{2,1,0:T(8,128)(2,1)} custom-call(s32[4]{0:T(128)} %pad_add_fusion.order_ref, bf16[256,1536]{1,0:T(8,128)(2,1)} %collective-permute-done.a_ref, bf16[256,1536]{1,0:T(8,128)(2,1)} %collective-permute-done.5.b_ref, bf16[768,6144]{1,0:T(8,128)(2,1)} %w_ref.7, f32[768,256]{1,0:T(8,128)} %shard_map.85.after_ref.start, ...), custom_call_target="tpu_custom_call" | custom-call | tf_op jit(solution)/shard_map/pallas_call | solution.py:488
  30.0 3.0 %all-to-all-done.x_ref = bf16[8,272,256]{2,1,0:T(8,128)(2,1)} async-done(((bf16[8,272,256]{2,1,0:T(8,128)(2,1)}), bf16[8,272,256]{2,1,0:T(8,128)(2,1)}, u32[]{:S(2)}, u32[]{:S(2)}) %all-to-all-start) | async-done | bytes 1114144 | tf_op jit(solution)/shard_map/all_to_all | solution.py:560
  33.0 9.2 %all-to-all-start.1 = ((bf16[8,256,256]{2,1,0:T(8,128)(2,1)}), bf16[8,256,256]{2,1,0:T(8,128)(2,1)}, u32[]{:S(2)}, u32[]{:S(2)}) async-start(bf16[8,256,256]{2,1,0:T(8,128)(2,1)} %shard_map.87), calls=%async_computation.1 | async-start | bytes 2097152 | tf_op jit(solution)/shard_map/all_to_all | solution.py:560
  42.2 0.0 copy-done
  42.2 2.4 %shard_map.86 = (bf16[1312,256]{1,0:T(8,128)(2,1)}, bf16[528,256]{1,0:T(8,128)(2,1)}) custom-call(bf16[8,272,256]{2,1,0:T(8,128)(2,1)} %all-to-all-done.x_ref, f32[768,256]{1,0:T(8,128)S(1)} %copy-done), custom_call_target="tpu_custom_call" | custom-call | tf_op jit(solution)/shard_map/pallas_call | solution.py:607
  44.7 3.8 %collective-permute-start.2 = (bf16[1312,256]{1,0:T(8,128)(2,1)}, bf16[1312,256]{1,0:T(8,128)(2,1)}, u32[]{:S(2)}, u32[]{:S(2)}) collective-permute-start(bf16[1312,256]{1,0:T(8,128)(2,1)} %get-tuple-element.25), channel_id=1, source_target_pairs={{0,32},{32,64},{64,96},{1,33},{33,65},{65,97},{2,34},{34,66},{66,9... | collective-permute-start | bytes 2015240 | tf_op jit(solution)/shard_map/ppermute | solution.py:556
  48.5 1.4 collective-permute-start.4
  49.9 3.0 %collective-permute-start.3 = (bf16[528,256]{1,0:T(8,128)(2,1)}, bf16[528,256]{1,0:T(8,128)(2,1)}, u32[]{:S(2)}, u32[]{:S(2)}) collective-permute-start(bf16[528,256]{1,0:T(8,128)(2,1)} %get-tuple-element.24.own_ref), channel_id=1, source_target_pairs={{0,64},{32,96},{1,65},{33,97},{2,66},{34,98},{3,67},{35,99},{4,68}... | collective-permute-start | bytes 811016 | tf_op jit(solution)/shard_map/ppermute | solution.py:556
  52.8 4.1 %all-to-all-done.1 = bf16[8,256,256]{2,1,0:T(8,128)(2,1)} async-done(((bf16[8,256,256]{2,1,0:T(8,128)(2,1)}), bf16[8,256,256]{2,1,0:T(8,128)(2,1)}, u32[]{:S(2)}, u32[]{:S(2)}) %all-to-all-start.1) | async-done | bytes 1048608 | tf_op jit(solution)/shard_map/all_to_all | solution.py:560
  57.0 10.5 %shard_map.88 = (f32[1024,256]{1,0:T(8,128)}, f32[2048,256]{1,0:T(8,128)}) custom-call(bf16[8,272,256]{2,1,0:T(8,128)(2,1)} %all-to-all-done.x_ref, bf16[2048,256]{1,0:T(8,128)(2,1)} %bitcast.5.pair_ref), custom_call_target="tpu_custom_call" | custom-call | tf_op jit(solution)/shard_map/pallas_call | solution.py:618
  67.5 0.0 collective-permute-done.4.far3_ref
  67.5 0.0 collective-permute-done.3.far2_ref
  67.5 1.0 collective-permute-done.2.near_ref
  68.5 18.2 %shard_map.89 = (bf16[2048,256]{1,0:T(8,128)(2,1)}, f32[1024,256]{1,0:T(8,128)}, f32[512,256]{1,0:T(8,128)}, bf16[1312,256]{1,0:T(8,128)(2,1)}, bf16[528,256]{1,0:T(8,128)(2,1)}, /*index=5*/bf16[528,256]{1,0:T(8,128)(2,1)}) custom-call(s32[1]{0:T(128)} %bitcast.4.z_ref, bf16[8,272,256]{2,1,0:T(8,128)(2,1)} %all-to-all-done.x_ref, ...), custom_call_target="tpu_custom_call" | custom-call | tf_op jit(solution)/shard_map/pallas_call | solution.py:628
  86.6 7.2 %all-to-all-start.2 = ((bf16[8,256,256]{2,1,0:T(8,128)(2,1)}), bf16[8,256,256]{2,1,0:T(8,128)(2,1)}, u32[]{:S(2)}, u32[]{:S(2)}) async-start(bf16[8,256,256]{2,1,0:T(8,128)(2,1)} %bitcast.7), calls=%async_computation.2 | async-start | bytes 2097152 | tf_op jit(solution)/shard_map/all_to_all | solution.py:560
  93.9 2.0 %collective-permute-start.7 = (bf16[1312,256]{1,0:T(8,128)(2,1)}, bf16[1312,256]{1,0:T(8,128)(2,1)}, u32[]{:S(2)}, u32[]{:S(2)}) collective-permute-start(bf16[1312,256]{1,0:T(8,128)(2,1)} %get-tuple-element.34), channel_id=1, source_target_pairs={{32,0},{64,32},{96,64},{33,1},{65,33},{97,65},{34,2},{66,34},{98,6... | collective-permute-start | bytes 2015240 | tf_op jit(solution)/shard_map/ppermute | solution.py:556
  95.9 1.3 collective-permute-start.8
  97.2 1.4 collective-permute-start.9
  98.6 7.7 %all-to-all-done.2.attn_ref.pair_ref = bf16[8,256,256]{2,1,0:T(8,128)(2,1)} async-done(((bf16[8,256,256]{2,1,0:T(8,128)(2,1)}), bf16[8,256,256]{2,1,0:T(8,128)(2,1)}, u32[]{:S(2)}, u32[]{:S(2)}) %all-to-all-start.2) | async-done | bytes 1048608 | tf_op jit(solution)/shard_map/all_to_all | solution.py:560
  106.3 5.8 %shard_map.90 = (bf16[256,1536]{1,0:T(8,128)(2,1)}, bf16[256,1536]{1,0:T(8,128)(2,1)}) custom-call(s32[4]{0:T(128)} %pad_add_fusion.order_ref, bf16[8,256,256]{2,1,0:T(8,128)(2,1)} %all-to-all-done.2.attn_ref.pair_ref, bf16[768,6144]{1,0:T(8,128)(2,1)} %w_ref.7), custom_call_target="tpu_custom_call" | custom-call | tf_op jit(solution)/shard_map/pallas_call | solution.py:533
  112.1 6.1 %collective-permute-done.8.back2_ref = bf16[528,256]{1,0:T(8,128)(2,1)} collective-permute-done((bf16[528,256]{1,0:T(8,128)(2,1)}, bf16[528,256]{1,0:T(8,128)(2,1)}, u32[]{:S(2)}, u32[]{:S(2)}) %collective-permute-start.8) | collective-permute-done | bytes 270368 | tf_op jit(solution)/shard_map/ppermute | solution.py:556
  118.2 0.0 collective-permute-done.9.back3_ref
  118.2 0.0 collective-permute-done.7.back1_ref
  118.2 4.1 %shard_map.91.refs_0_ = bf16[8,272,256]{2,1,0:T(8,128)(2,1)} custom-call(f32[2048,256]{1,0:T(8,128)} %get-tuple-element.31.sums_ref, f32[1024,256]{1,0:T(8,128)} %get-tuple-element.32.fine_ref, f32[512,256]{1,0:T(8,128)} %get-tuple-element.33.coarse_ref, bf16[1312,256]{1,0:T(8,128)(2,1)} %collective-permute-done.7.back1_ref, ...), custom_call_target="tpu_custom_call" | custom-call | tf_op jit(solution)/shard_map/pallas_call | solution.py:671
  122.3 5.5 %shard_map.92 = (bf16[256,1536]{1,0:T(8,128)(2,1)}, bf16[256,1536]{1,0:T(8,128)(2,1)}) custom-call(s32[4]{0:T(128)} %pad_add_fusion.order_ref, bf16[8,256,256]{2,1,0:T(8,128)(2,1)} %all-to-all-done.2.attn_ref.pair_ref, bf16[768,6144]{1,0:T(8,128)(2,1)} %w_ref.7, bf16[8,272,256]{2,1,0:T(8,128)(2,1)} %shard_map.91.refs_0_), custom_call_target="tpu_custom_call" | custom-call | tf_op jit(solution)/shard_map/pallas_call | solution.py:533
  127.8 0.0 collective-permute-start.10
  127.9 7.4 %all-to-all-start.3 = ((bf16[8,272,256]{2,1,0:T(8,128)(2,1)}), bf16[8,272,256]{2,1,0:T(8,128)(2,1)S(1)}, u32[]{:S(2)}, u32[]{:S(2)}) async-start(bf16[8,272,256]{2,1,0:T(8,128)(2,1)} %shard_map.91.refs_0_), calls=%async_computation.3 | async-start | bytes 2228224 | tf_op jit(solution)/shard_map/all_to_all | solution.py:560
  135.2 0.0 collective-permute-start.6
  135.2 0.0 collective-permute-done.10
  135.2 0.0 copy-done.2
  135.2 1.1 add_convert_fusion.1
  136.3 0.8 collective-permute-start.11
  137.2 13.8 %all-to-all-done.3.x_ref = bf16[8,272,256]{2,1,0:T(8,128)(2,1)S(1)} async-done(((bf16[8,272,256]{2,1,0:T(8,128)(2,1)}), bf16[8,272,256]{2,1,0:T(8,128)(2,1)S(1)}, u32[]{:S(2)}, u32[]{:S(2)}) %all-to-all-start.3) | async-done | bytes 1114144 | tf_op jit(solution)/shard_map/all_to_all | solution.py:560
  151.0 2.4 %shard_map.93 = (bf16[256,768]{1,0:T(8,128)(2,1)}, bf16[256,768]{1,0:T(8,128)(2,1)}, bf16[256,768]{1,0:T(8,128)(2,1)}) custom-call(bf16[8,256,256]{2,1,0:T(8,128)(2,1)} %all-to-all-done.2.attn_ref.pair_ref, bf16[8,272,256]{2,1,0:T(8,128)(2,1)S(1)} %all-to-all-done.3.x_ref), custom_call_target="tpu_custom_call" | custom-call | tf_op jit(solution)/shard_map/pallas_call | solution.py:684
  153.4 0.0 collective-permute-done.6
  153.4 12.8 %collective-permute-done.11 = bf16[256,1536]{1,0:T(8,128)(2,1)S(1)} collective-permute-done((bf16[256,1536]{1,0:T(8,128)(2,1)}, bf16[256,1536]{1,0:T(8,128)(2,1)S(1)}, u32[]{:S(2)}, u32[]{:S(2)}) %collective-permute-start.11) | collective-permute-done | bytes 786464 | tf_op jit(solution)/shard_map/ppermute | solution.py:552
  166.2 0.0 copy-done.1
  166.2 1.2 add_convert_fusion
  (3 shorter events, 0.0 us)
Async XLA Ops:
  0.6 12.1 %collective-permute-start.1 = (bf16[256,1536]{1,0:T(8,128)(2,1)}, bf16[256,1536]{1,0:T(8,128)(2,1)}, u32[]{:S(2)}, u32[]{:S(2)}) collective-permute-start(bf16[256,1536]{1,0:T(8,128)(2,1)} %a_ref.1), channel_id=1, source_target_pairs={{0,1},{1,0},{2,3},{3,2},{4,5},{5,4},{6,7},{7,6},{8,9},{9,8},{10,11... | collective-permute-start | bytes 2359304 | tf_op jit(solution)/shard_map/ppermute | solution.py:552
  0.7 20.7 %collective-permute-start = (bf16[256,1536]{1,0:T(8,128)(2,1)}, bf16[256,1536]{1,0:T(8,128)(2,1)}, u32[]{:S(2)}, u32[]{:S(2)}) collective-permute-start(bf16[256,1536]{1,0:T(8,128)(2,1)} %a_ref.1), channel_id=1, source_target_pairs={{0,2},{2,0},{1,3},{3,1},{4,6},{6,4},{5,7},{7,5},{8,10},{10,8},{9,1... | collective-permute-start | bytes 2359304 | tf_op jit(solution)/shard_map/ppermute | solution.py:552
  4.7 28.3 %all-to-all-start = ((bf16[8,272,256]{2,1,0:T(8,128)(2,1)}), bf16[8,272,256]{2,1,0:T(8,128)(2,1)}, u32[]{:S(2)}, u32[]{:S(2)}) async-start(bf16[8,272,256]{2,1,0:T(8,128)(2,1)} %shard_map.84), calls=%async_computation | async-start | bytes 2228224 | tf_op jit(solution)/shard_map/all_to_all | solution.py:560
  21.5 2.6 %collective-permute-start.5 = (bf16[256,1536]{1,0:T(8,128)(2,1)}, bf16[256,1536]{1,0:T(8,128)(2,1)}, u32[]{:S(2)}, u32[]{:S(2)}) collective-permute-start(bf16[256,1536]{1,0:T(8,128)(2,1)} %collective-permute-done.a_ref), channel_id=1, source_target_pairs={{0,1},{1,0},{2,3},{3,2},{4,5},{5,4},{6,7},{7,6},{8,9},{9,8},{10,11... | collective-permute-start | bytes 2359304 | tf_op jit(solution)/shard_map/ppermute | solution.py:552
  30.0 12.2 %copy-start = (f32[768,256]{1,0:T(8,128)S(1)}, f32[768,256]{1,0:T(8,128)}, u32[]{:S(2)}) copy-start(f32[768,256]{1,0:T(8,128)} %shard_map.85.after_ref.start) | copy-start | bytes 2359300
  33.0 23.9 %all-to-all-start.1 = ((bf16[8,256,256]{2,1,0:T(8,128)(2,1)}), bf16[8,256,256]{2,1,0:T(8,128)(2,1)}, u32[]{:S(2)}, u32[]{:S(2)}) async-start(bf16[8,256,256]{2,1,0:T(8,128)(2,1)} %shard_map.87), calls=%async_computation.1 | async-start | bytes 2097152 | tf_op jit(solution)/shard_map/all_to_all | solution.py:560
  44.7 23.8 %collective-permute-start.2 = (bf16[1312,256]{1,0:T(8,128)(2,1)}, bf16[1312,256]{1,0:T(8,128)(2,1)}, u32[]{:S(2)}, u32[]{:S(2)}) collective-permute-start(bf16[1312,256]{1,0:T(8,128)(2,1)} %get-tuple-element.25), channel_id=1, source_target_pairs={{0,32},{32,64},{64,96},{1,33},{33,65},{65,97},{2,34},{34,66},{66,9... | collective-permute-start | bytes 2015240 | tf_op jit(solution)/shard_map/ppermute | solution.py:556
  48.5 19.0 %collective-permute-start.4 = (bf16[528,256]{1,0:T(8,128)(2,1)}, bf16[528,256]{1,0:T(8,128)(2,1)}, u32[]{:S(2)}, u32[]{:S(2)}) collective-permute-start(bf16[528,256]{1,0:T(8,128)(2,1)} %get-tuple-element.24.own_ref), channel_id=1, source_target_pairs={{0,96},{1,97},{2,98},{3,99},{4,100},{5,101},{6,102},{7,103},{8,104... | collective-permute-start | bytes 811016 | tf_op jit(solution)/shard_map/ppermute | solution.py:556
  49.9 17.6 %collective-permute-start.3 = (bf16[528,256]{1,0:T(8,128)(2,1)}, bf16[528,256]{1,0:T(8,128)(2,1)}, u32[]{:S(2)}, u32[]{:S(2)}) collective-permute-start(bf16[528,256]{1,0:T(8,128)(2,1)} %get-tuple-element.24.own_ref), channel_id=1, source_target_pairs={{0,64},{32,96},{1,65},{33,97},{2,66},{34,98},{3,67},{35,99},{4,68}... | collective-permute-start | bytes 811016 | tf_op jit(solution)/shard_map/ppermute | solution.py:556
  86.6 19.7 %all-to-all-start.2 = ((bf16[8,256,256]{2,1,0:T(8,128)(2,1)}), bf16[8,256,256]{2,1,0:T(8,128)(2,1)}, u32[]{:S(2)}, u32[]{:S(2)}) async-start(bf16[8,256,256]{2,1,0:T(8,128)(2,1)} %bitcast.7), calls=%async_computation.2 | async-start | bytes 2097152 | tf_op jit(solution)/shard_map/all_to_all | solution.py:560
  93.9 24.3 %collective-permute-start.7 = (bf16[1312,256]{1,0:T(8,128)(2,1)}, bf16[1312,256]{1,0:T(8,128)(2,1)}, u32[]{:S(2)}, u32[]{:S(2)}) collective-permute-start(bf16[1312,256]{1,0:T(8,128)(2,1)} %get-tuple-element.34), channel_id=1, source_target_pairs={{32,0},{64,32},{96,64},{33,1},{65,33},{97,65},{34,2},{66,34},{98,6... | collective-permute-start | bytes 2015240 | tf_op jit(solution)/shard_map/ppermute | solution.py:556
  95.9 22.3 %collective-permute-start.8 = (bf16[528,256]{1,0:T(8,128)(2,1)}, bf16[528,256]{1,0:T(8,128)(2,1)}, u32[]{:S(2)}, u32[]{:S(2)}) collective-permute-start(bf16[528,256]{1,0:T(8,128)(2,1)} %get-tuple-element.35), channel_id=1, source_target_pairs={{64,0},{96,32},{65,1},{97,33},{66,2},{98,34},{67,3},{99,35},{68,4}... | collective-permute-start | bytes 811016 | tf_op jit(solution)/shard_map/ppermute | solution.py:556
  97.2 21.0 %collective-permute-start.9 = (bf16[528,256]{1,0:T(8,128)(2,1)}, bf16[528,256]{1,0:T(8,128)(2,1)}, u32[]{:S(2)}, u32[]{:S(2)}) collective-permute-start(bf16[528,256]{1,0:T(8,128)(2,1)} %get-tuple-element.36), channel_id=1, source_target_pairs={{96,0},{97,1},{98,2},{99,3},{100,4},{101,5},{102,6},{103,7},{104,8... | collective-permute-start | bytes 811016 | tf_op jit(solution)/shard_map/ppermute | solution.py:556
  127.8 7.4 %copy-start.2 = (bf16[256,1536]{1,0:T(8,128)(2,1)S(1)}, bf16[256,1536]{1,0:T(8,128)(2,1)}, u32[]{:S(2)}) copy-start(bf16[256,1536]{1,0:T(8,128)(2,1)} %get-tuple-element.37) | copy-start | bytes 2359300
  127.8 7.4 %collective-permute-start.10 = (bf16[256,1536]{1,0:T(8,128)(2,1)}, bf16[256,1536]{1,0:T(8,128)(2,1)S(1)}, u32[]{:S(2)}, u32[]{:S(2)}) collective-permute-start(bf16[256,1536]{1,0:T(8,128)(2,1)} %get-tuple-element.38), channel_id=1, source_target_pairs={{0,1},{1,0},{2,3},{3,2},{4,5},{5,4},{6,7},{7,6},{8,9},{9,8},{10,11... | collective-permute-start | bytes 2359304 | tf_op jit(solution)/shard_map/ppermute | solution.py:552
  127.9 23.1 %all-to-all-start.3 = ((bf16[8,272,256]{2,1,0:T(8,128)(2,1)}), bf16[8,272,256]{2,1,0:T(8,128)(2,1)S(1)}, u32[]{:S(2)}, u32[]{:S(2)}) async-start(bf16[8,272,256]{2,1,0:T(8,128)(2,1)} %shard_map.91.refs_0_), calls=%async_computation.3 | async-start | bytes 2228224 | tf_op jit(solution)/shard_map/all_to_all | solution.py:560
  135.2 18.2 %collective-permute-start.6 = (bf16[256,1536]{1,0:T(8,128)(2,1)}, bf16[256,1536]{1,0:T(8,128)(2,1)S(1)}, u32[]{:S(2)}, u32[]{:S(2)}) collective-permute-start(bf16[256,1536]{1,0:T(8,128)(2,1)} %get-tuple-element.30), channel_id=1, source_target_pairs={{0,1},{1,0},{2,3},{3,2},{4,5},{5,4},{6,7},{7,6},{8,9},{9,8},{10,11... | collective-permute-start | bytes 2359304 | tf_op jit(solution)/shard_map/ppermute | solution.py:552
  136.3 29.9 %copy-start.1 = (bf16[256,1536]{1,0:T(8,128)(2,1)S(1)}, bf16[256,1536]{1,0:T(8,128)(2,1)}, u32[]{:S(2)}) copy-start(bf16[256,1536]{1,0:T(8,128)(2,1)} %get-tuple-element.29.after_ref) | copy-start | bytes 2359300
  136.3 29.9 %collective-permute-start.11 = (bf16[256,1536]{1,0:T(8,128)(2,1)}, bf16[256,1536]{1,0:T(8,128)(2,1)S(1)}, u32[]{:S(2)}, u32[]{:S(2)}) collective-permute-start(bf16[256,1536]{1,0:T(8,128)(2,1)} %add_convert_fusion.1), channel_id=1, source_target_pairs={{0,2},{2,0},{1,3},{3,1},{4,6},{6,4},{5,7},{7,5},{8,10},{10,8},{9,1... | collective-permute-start | bytes 2359304 | tf_op jit(solution)/shard_map/ppermute | solution.py:552
